TPU v7x, 32 devices: a whole 2x2x4 slice. The times are simulated.
32 devices in a mesh: seq: 8 (over z, y), tp: 4 (over x, core).
Axes of the slice: x: 2, y: 2, z: 4, core: 2. Of those that a mesh axis runs over, the one named last changes fastest.
Arguments:
- queries: bfloat16 [2048, 8192], P('seq', 'tp'), may hold values from -6 to 6
- key_matrix: bfloat16 [2048, 1024], P('seq', 'tp'), may hold values from -6 to 6
- value_matrix: bfloat16 [2048, 1024], P('seq', 'tp'), may hold values from -6 to 6
- output_gradient: bfloat16 [2048, 8192], P(('seq', 'tp')), may hold values from -6 to 6
- document: int32 [2048], P('seq'), may hold values from 0 to 7, never falling along the last dimension, each value on 1 to 1024 neighbouring positions
Outputs:
- query_grad: bfloat16 [2048, 8192], P('seq', 'tp')
- key_gradient: bfloat16 [2048, 1024], P('seq', 'tp')
- value_gradient: bfloat16 [2048, 1024], P('seq', 'tp')
Inputs may be any that keep to these rules, and one draw needn't show every extreme that they name: document never falls along the sequence; there are exactly 8 documents, each of at most 1024 tokens, and one holds exactly that many.
All inputs are finite; a program needn't handle non-finite values.
Results may differ from a plain program's by a relative error of at most 0.009.
Values may be sent and summed in bfloat16 or wider, within the bound.
No kernel may reach another device: no remote copies, remote signals or barrier semaphores. Data moves between devices by JAX's collectives and lax.ppermute only.
A program may use at most 64 MiB of HBM per device.

v0:
```python
import functools
import math

import jax
import jax.numpy as jnp
from jax import lax
from jax.experimental import pallas as pl
from jax.experimental.pallas import tpu as pltpu
from jax.sharding import PartitionSpec as P

HEAD_WIDTH = 128
DOCS = 8
PAD = 16
NEG = -1e30
ANY = pl.BlockSpec(memory_space=pl.ANY)
VMEM = pl.BlockSpec(memory_space=pltpu.VMEM)
SMALL = pltpu.CompilerParams(vmem_limit_bytes=2 * 1024 * 1024)


def prepare_kernel(n_tp, heads, key_ref, value_ref, doc_ref, grad_ref, query_ref, *rest):
    outs, (doc_scr, sems) = rest[:-2], rest[-2:]
    block_out, query_out, own_out, beside_out, across_outs = *outs[:4], outs[4:]
    tokens = key_ref.shape[0]
    rows = grad_ref.shape[0]
    me = lax.axis_index("tp")
    width = grad_ref.shape[1] // n_tp
    copies = []

    def add(src, dst):
        copies.append(pltpu.make_async_copy(src, dst, sems.at[len(copies)]))
        copies[-1].start()

    def columns(m):
        return grad_ref.at[:, pl.ds(pl.multiple_of((me ^ m) * width, width), width)]

    add(doc_ref, doc_scr)
    for h in range(heads):
        for part, src in enumerate((key_ref, value_ref)):
            cols = pl.ds((2 * h + part) * HEAD_WIDTH, HEAD_WIDTH)
            add(
                src.at[:, pl.ds(h * HEAD_WIDTH, HEAD_WIDTH)],
                block_out.at[pl.ds(0, tokens), cols],
            )
    for m in range(2, n_tp):
        add(columns(m), across_outs[m // 2 - 1].at[pl.ds(m % 2 * rows, rows), :])
    add(columns(1), beside_out)
    add(columns(0), own_out)
    add(query_ref, query_out)
    copies[0].wait()
    row = doc_scr[...].astype(jnp.float32).astype(jnp.bfloat16)
    row = jnp.concatenate([row] * heads, axis=1)
    block_out[tokens : tokens + PAD, :] = jnp.broadcast_to(row, (PAD, row.shape[1]))
    for copy in copies[1:]:
        copy.wait()


def prepare(key_matrix, value_matrix, document, output_gradient, queries, n_tp):
    tokens, kv_width = key_matrix.shape
    heads = kv_width // HEAD_WIDTH
    rows, width = output_gradient.shape
    chips = n_tp // 2 - 1
    one = pltpu.VMEM((rows, width // n_tp), jnp.bfloat16)
    two = pltpu.VMEM((2 * rows, width // n_tp), jnp.bfloat16)
    shapes = (
        pltpu.VMEM((tokens + PAD, 2 * kv_width), jnp.bfloat16),
        pltpu.VMEM(queries.shape, jnp.bfloat16),
        one,
        one,
    ) + (two,) * chips
    args = (key_matrix, value_matrix, document.reshape(1, tokens), output_gradient, queries)
    block, query, own, beside, *across = pl.pallas_call(
        functools.partial(prepare_kernel, n_tp, heads),
        out_shape=shapes,
        in_specs=[ANY] * len(args),
        out_specs=(VMEM,) * len(shapes),
        scratch_shapes=[
            pltpu.VMEM((1, tokens), jnp.int32),
            pltpu.SemaphoreType.DMA((2 * heads + n_tp + 2,)),
        ],
        compiler_params=SMALL,
    )(*[pltpu.with_memory_space_constraint(x, pltpu.HBM) for x in args])
    return block, query, own, beside, across


def choose_kernel(even_ref, odd_ref, out_ref):
    odd = lax.rem(lax.axis_index("seq"), 2) == 1

    @pl.when(odd)
    def _():
        out_ref[...] = odd_ref[...]

    @pl.when(jnp.logical_not(odd))
    def _():
        out_ref[...] = even_ref[...]


def choose(even, odd):
    return pl.pallas_call(
        choose_kernel,
        out_shape=pltpu.VMEM(even.shape, even.dtype),
        in_specs=[VMEM, VMEM],
        out_specs=VMEM,
        compiler_params=SMALL,
    )(*held(even, odd))


def lower_kernel(pair_ref, out_ref):
    out_ref[...] = pair_ref[out_ref.shape[0] :, :]


def lower(pair):
    rows, width = pair.shape
    return pl.pallas_call(
        lower_kernel,
        out_shape=pltpu.VMEM((rows // 2, width), pair.dtype),
        in_specs=[VMEM],
        out_specs=VMEM,
        compiler_params=SMALL,
    )(*held(pair))


def relay_kernel(near, *refs):
    total = refs[0][...].astype(jnp.float32)
    for ref in refs[1 : -2 if near else -1]:
        total = total + ref[...].astype(jnp.float32)
    if near:
        odd = lax.rem(lax.axis_index("seq"), 2) == 1
        total = total + jnp.where(odd, refs[-2][...].astype(jnp.float32), 0.0)
    refs[-1][...] = total.astype(refs[-1].dtype)


def relay(near, *parts):
    return pl.pallas_call(
        functools.partial(relay_kernel, near),
        out_shape=pltpu.VMEM(parts[0].shape, jnp.bfloat16),
        in_specs=[VMEM] * len(parts),
        out_specs=VMEM,
        compiler_params=SMALL,
    )(*held(*parts))


def finish_kernel(heads, *refs):
    key_out, value_out = refs[-2:]
    even = lax.rem(lax.axis_index("seq"), 2) == 0
    factor = 1.0 / math.sqrt(HEAD_WIDTH)
    for h in range(heads):
        own, moved, near = refs[3 * h : 3 * h + 3]
        total = own[...] + moved[...].astype(jnp.float32)
        total = total + jnp.where(even, near[...].astype(jnp.float32), 0.0)
        cols = slice(h * HEAD_WIDTH, (h + 1) * HEAD_WIDTH)
        key_out[:, cols] = (total[:, :HEAD_WIDTH] * factor).astype(jnp.bfloat16)
        value_out[:, cols] = total[:, HEAD_WIDTH:].astype(jnp.bfloat16)


def finish(*parts):
    heads = len(parts) // 3
    out = jax.ShapeDtypeStruct((parts[0].shape[0], heads * HEAD_WIDTH), jnp.bfloat16)
    return pl.pallas_call(
        functools.partial(finish_kernel, heads),
        out_shape=(out, out),
        in_specs=[VMEM] * len(parts),
        out_specs=(VMEM, VMEM),
        compiler_params=SMALL,
    )(*held(*parts))


def held(*arrays):
    return [pltpu.with_memory_space_constraint(x, pltpu.VMEM) for x in arrays]


def after(array, *others):
    return lax.optimization_barrier((array, *others))[0]


def nt_dot(a, b):
    return lax.dot_general(a, b, (((1,), (1,)), ((), ())), preferred_element_type=jnp.float32)


def nn_dot(a, b):
    return lax.dot_general(a, b, (((1,), (0,)), ((), ())), preferred_element_type=jnp.float32)


def main_kernel(h, reach, group, n_tp, first, *refs):
    half = reach // 2
    refs = list(refs)
    take = lambda count: [refs.pop(0) for _ in range(count)]
    (query_ref,) = take(1)
    grad_refs = take(n_tp)
    (own_ref,) = take(1)
    odd_refs = take(half)
    even_refs = take(half)
    if not first:
        take(1)
    (dq_ref,) = take(1)
    odd_outs = take(half)
    even_outs = take(half)
    (own_out_ref,) = take(1)
    (kx, vx, kt, qx, gs) = take(5)
    scores, peaks, grads, weights, stats = take(2), take(2), take(2), take(2), take(2)
    (dk_acc, dv_acc, dq_out, out_sems) = take(4)

    T = own_out_ref.shape[0]
    W = group * HEAD_WIDTH
    i = lax.axis_index("seq")
    t = lax.axis_index("tp")
    sub = T // n_tp
    window = (reach + 1) * T
    block_refs = [own_ref]
    for k in range(half):
        block_refs += [odd_refs[k], even_refs[k]]
    dk_acc[...] = jnp.zeros(dk_acc.shape, jnp.float32)
    dv_acc[...] = jnp.zeros(dv_acc.shape, jnp.float32)

    code = lax.broadcasted_iota(jnp.int32, (HEAD_WIDTH, T), 0).astype(jnp.float32)
    at = 2 * h * HEAD_WIDTH
    for d, block in enumerate(block_refs):
        row = block[T : T + 1, at : at + T].astype(jnp.float32)
        row = jnp.where(i >= d, row, float(DOCS))
        one_hot = jnp.where(code == row, 1.0, 0.0).astype(jnp.bfloat16)
        kx[reach - d, :, 0:HEAD_WIDTH] = block[0:T, at : at + HEAD_WIDTH]
        kx[reach - d, :, HEAD_WIDTH : 2 * HEAD_WIDTH] = one_hot.T
        vx[reach - d] = block[0:T, at + HEAD_WIDTH : at + 2 * HEAD_WIDTH]
    own_row = own_ref[T : T + 1, at : at + T].astype(jnp.float32)
    away = jnp.where((code == own_row) | (code > DOCS), 0.0, NEG).astype(jnp.bfloat16).T
    for g in range(group):
        at = (h * group + g) * HEAD_WIDTH
        qx[g, :, 0:HEAD_WIDTH] = query_ref[:, at : at + HEAD_WIDTH]
        qx[g, :, HEAD_WIDTH : 2 * HEAD_WIDTH] = away

    factor = 1.0 / math.sqrt(HEAD_WIDTH)
    scale = factor * math.log2(math.e)
    before = reach * T

    def by_eight(x):
        return x.reshape(x.shape[0] // 8, 8, T)

    def dq_copy(g):
        cols = pl.ds(pl.multiple_of((h * group + g) * HEAD_WIDTH, HEAD_WIDTH), HEAD_WIDTH)
        return pltpu.make_async_copy(dq_out.at[g], dq_ref.at[:, cols], out_sems.at[g])

    def step(score_of, weight_of, grad_of, b):
        c = 1 - b
        if score_of is not None:
            s = nt_dot(kx[...].reshape(window, 2 * HEAD_WIDTH), qx[score_of])
            causal = lax.broadcasted_iota(jnp.int32, (T, T), 0) <= lax.broadcasted_iota(
                jnp.int32, (T, T), 1
            )
            own = jnp.where(causal, s[before:], NEG)
            scores[b][0:before] = s[:before]
            scores[b][before:] = own
            peaks[b][...] = jnp.maximum(
                jnp.max(by_eight(s[:before]), axis=0), jnp.max(by_eight(own), axis=0)
            )
        if weight_of is not None:
            top = jnp.max(peaks[c][...], axis=0, keepdims=True) * scale
            dp = nt_dot(vx[...].reshape(window, HEAD_WIDTH), gs[weight_of])
            e = jnp.exp2(scores[c][...] * scale - top)
            weights[c][...] = e.astype(jnp.bfloat16)
            grads[c][...] = dp
            total = jnp.sum(jnp.sum(by_eight(e), axis=0), axis=0, keepdims=True)
            weighted = jnp.sum(jnp.sum(by_eight(e * dp), axis=0), axis=0, keepdims=True)
            stats[c][0:1] = 1.0 / total
            stats[c][1:2] = weighted / total
        if grad_of is not None:
            inverse = stats[b][0:1]
            e_old = weights[b][...]
            ds = (e_old.astype(jnp.float32) * (grads[b][...] - stats[b][1:2])).astype(jnp.bfloat16)
            column = jnp.broadcast_to(inverse, (HEAD_WIDTH, T)).T
            query = (qx[grad_of, :, 0:HEAD_WIDTH].astype(jnp.float32) * column).astype(jnp.bfloat16)
            grad = (gs[grad_of].astype(jnp.float32) * column).astype(jnp.bfloat16)
        if grad_of is not None:
            dq = nn_dot(kt[...], ds) * (inverse * factor)
            dq_out[grad_of] = dq.T.astype(jnp.bfloat16)
            dq_copy(grad_of).start()
            dv_acc[...] += nn_dot(e_old, grad)
            dk_acc[...] += nn_dot(ds, query)

    def two_steps(pair, _):
        g = 2 * pair
        step(g + 2, g + 1, g, 0)
        step(g + 3, g + 2, g + 1, 1)
        return 0

    step(0, None, None, 0)
    for d in range(reach + 1):
        kt[:, (reach - d) * T : (reach - d + 1) * T] = kx[reach - d, :, 0:HEAD_WIDTH].T
    for m in range(n_tp):
        rows = pl.ds(pl.multiple_of((t ^ m) * sub, sub), sub)
        src = grad_refs[m]
        for g in range(group):
            at = h * W + g * HEAD_WIDTH
            gs[g, rows, :] = src[0:sub, at : at + HEAD_WIDTH]
    step(1, 0, None, 1)
    lax.fori_loop(0, group // 2 - 1, two_steps, 0)
    step(None, group - 1, group - 2, 0)
    step(None, None, group - 1, 1)

    for d in range(reach + 1):
        dst = (odd_outs if d % 2 else even_outs)[(d - 1) // 2] if d else own_out_ref
        rows = slice((reach - d) * T, (reach - d + 1) * T)
        dst[:, 0:HEAD_WIDTH] = dk_acc[rows, :].astype(dst.dtype)
        dst[:, HEAD_WIDTH : 2 * HEAD_WIDTH] = dv_acc[rows, :].astype(dst.dtype)
    for g in range(group):
        dq_copy(g).wait()


def scratch_of(window, T, group):
    bf16, f32 = jnp.bfloat16, jnp.float32
    return [
        pltpu.VMEM((window, T, 2 * HEAD_WIDTH), bf16),
        pltpu.VMEM((window, T, HEAD_WIDTH), bf16),
        pltpu.VMEM((HEAD_WIDTH, window * T), bf16),
        pltpu.VMEM((group, T, 2 * HEAD_WIDTH), bf16),
        pltpu.VMEM((group, T, HEAD_WIDTH), bf16),
        *[pltpu.VMEM((window * T, T), f32)] * 2,
        *[pltpu.VMEM((8, T), f32)] * 2,
        *[pltpu.VMEM((window * T, T), f32)] * 2,
        *[pltpu.VMEM((window * T, T), bf16)] * 2,
        *[pltpu.VMEM((8, T), f32)] * 2,
        pltpu.VMEM((window * T, HEAD_WIDTH), f32),
        pltpu.VMEM((window * T, HEAD_WIDTH), f32),
        pltpu.VMEM((group, T, HEAD_WIDTH), bf16),
    ]


def head_call(h, reach, group, n_tp, queries, grads, block, odds, evens, dq):
    T, q_width = queries.shape
    window = reach + 1
    first = dq is None
    args = held(queries, *grads, block, *odds, *evens)
    specs = [VMEM] * len(args)
    if not first:
        args.append(dq)
        specs.append(ANY)
    flops = 5 * 2 * T * (window * T) * group * HEAD_WIDTH
    scratch = scratch_of(window, T, group)
    outs = pl.pallas_call(
        functools.partial(main_kernel, h, reach, group, n_tp, first),
        out_shape=(pltpu.HBM((T, q_width), jnp.bfloat16),)
        + (pltpu.VMEM((T, 2 * HEAD_WIDTH), jnp.bfloat16),) * reach
        + (pltpu.VMEM((T, 2 * HEAD_WIDTH), jnp.float32),),
        in_specs=specs,
        out_specs=(ANY,) + (VMEM,) * (reach + 1),
        input_output_aliases={} if first else {len(args) - 1: 0},
        scratch_shapes=[*scratch, pltpu.SemaphoreType.DMA((group,))],
        compiler_params=pltpu.CompilerParams(
            vmem_limit_bytes=2 * sum(math.prod(x.shape) * x.dtype.itemsize for x in scratch)
        ),
        cost_estimate=pl.CostEstimate(
            flops=4 * flops,
            bytes_accessed=4 * 1024 * 1024,
            transcendentals=T * window * T * group,
        ),
    )(*args)
    half = reach // 2
    return outs[0], outs[1 : half + 1], outs[half + 1 : -1], outs[-1]


def local(queries, key_matrix, value_matrix, output_gradient, document):
    n = lax.axis_size("seq")
    n_tp = lax.axis_size("tp")
    T, q_width = queries.shape
    heads = key_matrix.shape[1] // HEAD_WIDTH
    group = q_width // (heads * HEAD_WIDTH)
    reach = n // 2
    half = reach // 2

    block, queries, mine, beside, across = prepare(
        key_matrix, value_matrix, document, output_gradient, queries, n_tp
    )

    swap = [(a, a ^ 1) for a in range(n)]
    one_up = [(a, (a + 1) % n) for a in range(n)]
    two_up = [(a, (a + 2) % n) for a in range(n)]
    one_down = [(b, a) for a, b in one_up]
    two_down = [(b, a) for a, b in two_up]
    cores = [(a, a ^ 1) for a in range(n_tp)]

    evens = [lax.ppermute(block, "seq", two_up)]
    pairs = [
        lax.ppermute(pair, "tp", [(a, a ^ (2 * m + 2)) for a in range(n_tp)])
        for m, pair in enumerate(across)
    ]
    odds = [None]
    for k in range(1, half):
        odds.append(lax.ppermute(evens[-1], "seq", one_up))
        evens.append(lax.ppermute(evens[-1], "seq", two_up))
    odds[0] = lax.ppermute(choose(block, evens[0]), "seq", swap)
    grads = [mine, lax.ppermute(beside, "tp", cores)]
    for pair in pairs:
        grads += [pair, lax.ppermute(lower(pair), "tp", cores)]

    dq = None
    odds_in, evens_in = odds, evens
    leaving = []
    for h in range(heads):
        dq, odds, evens, own = head_call(
            h, reach, group, n_tp, queries, grads, block, odds_in, evens_in, dq
        )
        last = evens[-1]
        if leaving:
            moved = [*leaving[-1][0], leaving[-1][2]]
            odds = [after(x, *moved) for x in odds]
            last = after(last, *moved)
        moving = lax.ppermute(last, "seq", two_down)
        odds = [lax.ppermute(x, "seq", one_down if k else swap) for k, x in enumerate(odds)]
        leaving.append((odds, evens, moving, own))
    ends = []
    for h in range(heads):
        odds, evens, moving, own = leaving[h]
        for k in range(half - 1, 0, -1):
            if h < heads - 1:
                moving = after(moving, dq)
            parts = [moving, evens[k - 1], odds[k]] + ([odds[0]] if k == 1 else [])
            moving = lax.ppermute(relay(k == 1, *parts), "seq", two_down)
        ends += [own, moving, odds[0]]
    return (dq, *finish(*ends))


def solution(mesh):
    return jax.shard_map(
        local,
        mesh=mesh,
        in_specs=(P("seq", "tp"), P("seq", "tp"), P("seq", "tp"), P(("seq", "tp"), None), P("seq")),
        out_specs=(P("seq", "tp"), P("seq", "tp"), P("seq", "tp")),
        check_vma=False,
    )
```

profile of v0, /device:TPU:0, one launch (start us, length us, event | category | flops | bytes accessed | tf_op | source)
XLA Modules:
  0.0 65.8 jit_solution(7111568482274772402)
XLA Ops:
  0.6 1.8 %shard_map.76 = (bf16[272,512]{1,0:T(8,128)(2,1)S(1)}, bf16[256,2048]{1,0:T(8,128)(2,1)S(1)}, bf16[64,2048]{1,0:T(8,128)(2,1)S(1)}, bf16[64,2048]{1,0:T(8,128)(2,1)S(1)}, bf16[128,2048]{1,0:T(8,128)(2,1)S(1)}) custom-call(bf16[256,256]{1,0:T(8,128)(2,1)} %key_ref.1, bf16[256,256]{1,0:T(8,128)(2,1)} %value_ref.1, s32[1,256]{1,0:T(1,128)} %bitcast.1, ...), custom_call_target="tpu_custom_call" | custom-call | tf_op jit(solution)/shard_map/pallas_call | solution.py:71
  2.4 3.0 %collective-permute-start.1 = (bf16[128,2048]{1,0:T(8,128)(2,1)S(1)}, bf16[128,2048]{1,0:T(8,128)(2,1)S(1)}, u32[]{:S(2)}, u32[]{:S(2)}) collective-permute-start(bf16[128,2048]{1,0:T(8,128)(2,1)S(1)} %get-tuple-element.29), channel_id=1, source_target_pairs={{0,2},{1,3},{2,0},{3,1},{4,6},{5,7},{6,4},{7,5},{8,10},{9,11},{10,... | collective-permute-start | bytes 1572872 | tf_op jit(solution)/shard_map/ppermute | solution.py:381
  5.4 1.6 %collective-permute-start.3 = (bf16[272,512]{1,0:T(8,128)(2,1)S(1)}, bf16[272,512]{1,0:T(8,128)(2,1)S(1)}, u32[]{:S(2)}, u32[]{:S(2)}) collective-permute-start(bf16[272,512]{1,0:T(8,128)(2,1)S(1)} %get-tuple-element.30.even_ref.refs_5_), channel_id=1, source_target_pairs={{0,8},{4,12},{8,16},{12,20},{16,24},{20,28},{24,0},{28,4},{1,9},{5... | collective-permute-start | bytes 835592 | tf_op jit(solution)/shard_map/ppermute | solution.py:379
  7.0 8.4 %collective-permute-done.3.odd_ref.refs_8_ = bf16[272,512]{1,0:T(8,128)(2,1)S(1)} collective-permute-done((bf16[272,512]{1,0:T(8,128)(2,1)S(1)}, bf16[272,512]{1,0:T(8,128)(2,1)S(1)}, u32[]{:S(2)}, u32[]{:S(2)}) %collective-permute-start.3) | collective-permute-done | bytes 278560 | tf_op jit(solution)/shard_map/ppermute | solution.py:379
  15.4 1.6 %collective-permute-start.4 = (bf16[272,512]{1,0:T(8,128)(2,1)S(1)}, bf16[272,512]{1,0:T(8,128)(2,1)S(1)}, u32[]{:S(2)}, u32[]{:S(2)}) collective-permute-start(bf16[272,512]{1,0:T(8,128)(2,1)S(1)} %shard_map.78), channel_id=1, source_target_pairs={{0,4},{4,0},{8,12},{12,8},{16,20},{20,16},{24,28},{28,24},{1,5},{5... | collective-permute-start | bytes 835592 | tf_op jit(solution)/shard_map/ppermute | solution.py:388
  17.0 0.5 collective-permute-start.5
  17.6 0.6 collective-permute-start.2
  18.1 0.9 %collective-permute-done.refs_2_ = bf16[64,2048]{1,0:T(8,128)(2,1)S(1)} collective-permute-done((bf16[64,2048]{1,0:T(8,128)(2,1)S(1)}, bf16[64,2048]{1,0:T(8,128)(2,1)S(1)}, u32[]{:S(2)}, u32[]{:S(2)}) %collective-permute-start) | collective-permute-done | bytes 262176 | tf_op jit(solution)/shard_map/ppermute | solution.py:389
  19.1 5.1 %collective-permute-done.4.refs_6_ = bf16[272,512]{1,0:T(8,128)(2,1)S(1)} collective-permute-done((bf16[272,512]{1,0:T(8,128)(2,1)S(1)}, bf16[272,512]{1,0:T(8,128)(2,1)S(1)}, u32[]{:S(2)}, u32[]{:S(2)}) %collective-permute-start.4) | collective-permute-done | bytes 278560 | tf_op jit(solution)/shard_map/ppermute | solution.py:388
  24.1 1.7 %collective-permute-done.6.refs_9_ = bf16[272,512]{1,0:T(8,128)(2,1)S(1)} collective-permute-done((bf16[272,512]{1,0:T(8,128)(2,1)S(1)}, bf16[272,512]{1,0:T(8,128)(2,1)S(1)}, u32[]{:S(2)}, u32[]{:S(2)}) %collective-permute-start.6) | collective-permute-done | bytes 278560 | tf_op jit(solution)/shard_map/ppermute | solution.py:387
  25.8 5.9 %collective-permute-done.5.refs_7_ = bf16[272,512]{1,0:T(8,128)(2,1)S(1)} collective-permute-done((bf16[272,512]{1,0:T(8,128)(2,1)S(1)}, bf16[272,512]{1,0:T(8,128)(2,1)S(1)}, u32[]{:S(2)}, u32[]{:S(2)}) %collective-permute-start.5) | collective-permute-done | bytes 278560 | tf_op jit(solution)/shard_map/ppermute | solution.py:386
  31.7 9.4 %shard_map.79 = (bf16[256,2048]{1,0:T(8,128)(2,1)}, bf16[256,256]{1,0:T(8,128)(2,1)S(1)}, bf16[256,256]{1,0:T(8,128)(2,1)S(1)}, bf16[256,256]{1,0:T(8,128)(2,1)S...) custom-call(bf16[256,2048]{1,0:T(8,128)(2,1)S(1)} %get-tuple-element.26.refs_0_, ...), custom_call_target="tpu_custom_call" | custom-call | flops 13421772800 | bytes 4194304 | tf_op jit(solution)/shard_map/pallas_call | solution.py:337
  41.2 0.1 collective-permute-start.8
  41.3 2.0 %collective-permute-start.9 = (bf16[256,256]{1,0:T(8,128)(2,1)S(1)}, bf16[256,256]{1,0:T(8,128)(2,1)S(1)}, u32[]{:S(2)}, u32[]{:S(2)}) collective-permute-start(bf16[256,256]{1,0:T(8,128)(2,1)S(1)} %get-tuple-element.38), channel_id=1, source_target_pairs={{0,4},{4,0},{8,12},{12,8},{16,20},{20,16},{24,28},{28,24},{1,5},{5... | collective-permute-start | bytes 393224 | tf_op jit(solution)/shard_map/ppermute | solution.py:406
  43.2 9.3 %shard_map.80 = (bf16[256,2048]{1,0:T(8,128)(2,1)}, bf16[256,256]{1,0:T(8,128)(2,1)S(1)}, bf16[256,256]{1,0:T(8,128)(2,1)S(1)}, bf16[256,256]{1,0:T(8,128)(2,1)S...) custom-call(bf16[256,2048]{1,0:T(8,128)(2,1)S(1)} %get-tuple-element.26.refs_0_, ...), custom_call_target="tpu_custom_call", output_to_operand_aliasing={{0}: (10, {})} | custom-call | flops 13421772800 | bytes 4194304 | tf_op jit(solution)/shard_map/pallas_call | solution.py:337
  52.6 0.3 collective-permute-start.11
  52.9 2.0 %collective-permute-start.12 = (bf16[256,256]{1,0:T(8,128)(2,1)S(1)}, bf16[256,256]{1,0:T(8,128)(2,1)S(1)}, u32[]{:S(2)}, u32[]{:S(2)}) collective-permute-start(bf16[256,256]{1,0:T(8,128)(2,1)S(1)} %get-tuple-element.44), channel_id=1, source_target_pairs={{4,0},{8,4},{12,8},{16,12},{20,16},{24,20},{28,24},{0,28},{5,1},{9... | collective-permute-start | bytes 393224 | tf_op jit(solution)/shard_map/ppermute | solution.py:406
  55.0 2.1 %collective-permute-start.10 = (bf16[256,256]{1,0:T(8,128)(2,1)S(1)}, bf16[256,256]{1,0:T(8,128)(2,1)S(1)}, u32[]{:S(2)}, u32[]{:S(2)}) collective-permute-start(bf16[256,256]{1,0:T(8,128)(2,1)S(1)} %shard_map.81), channel_id=1, source_target_pairs={{8,0},{12,4},{16,8},{20,12},{24,16},{28,20},{0,24},{4,28},{9,1},{1... | collective-permute-start | bytes 393224 | tf_op jit(solution)/shard_map/ppermute | solution.py:415
  57.2 0.7 %collective-permute-done.11.refs_0_ = bf16[256,256]{1,0:T(8,128)(2,1)S(1)} collective-permute-done((bf16[256,256]{1,0:T(8,128)(2,1)S(1)}, bf16[256,256]{1,0:T(8,128)(2,1)S(1)}, u32[]{:S(2)}, u32[]{:S(2)}) %collective-permute-start.11) | collective-permute-done | bytes 131104 | tf_op jit(solution)/shard_map/ppermute | solution.py:405
  57.9 0.3 collective-permute-done.12.refs_2_
  58.2 1.7 %collective-permute-done.13.refs_3_.refs_5_ = bf16[256,256]{1,0:T(8,128)(2,1)S(1)} collective-permute-done((bf16[256,256]{1,0:T(8,128)(2,1)S(1)}, bf16[256,256]{1,0:T(8,128)(2,1)S(1)}, u32[]{:S(2)}, u32[]{:S(2)}) %collective-permute-start.13) | collective-permute-done | bytes 131104 | tf_op jit(solution)/shard_map/ppermute | solution.py:406
  60.0 2.1 %collective-permute-start.14 = (bf16[256,256]{1,0:T(8,128)(2,1)S(1)}, bf16[256,256]{1,0:T(8,128)(2,1)S(1)}, u32[]{:S(2)}, u32[]{:S(2)}) collective-permute-start(bf16[256,256]{1,0:T(8,128)(2,1)S(1)} %shard_map.82), channel_id=1, source_target_pairs={{8,0},{12,4},{16,8},{20,12},{24,16},{28,20},{0,24},{4,28},{9,1},{1... | collective-permute-start | bytes 393224 | tf_op jit(solution)/shard_map/ppermute | solution.py:415
  62.1 2.9 %collective-permute-done.14.refs_4_ = bf16[256,256]{1,0:T(8,128)(2,1)S(1)} collective-permute-done((bf16[256,256]{1,0:T(8,128)(2,1)S(1)}, bf16[256,256]{1,0:T(8,128)(2,1)S(1)}, u32[]{:S(2)}, u32[]{:S(2)}) %collective-permute-start.14) | collective-permute-done | bytes 131104 | tf_op jit(solution)/shard_map/ppermute | solution.py:415
  65.0 0.8 %shard_map.83 = (bf16[256,256]{1,0:T(8,128)(2,1)}, bf16[256,256]{1,0:T(8,128)(2,1)}) custom-call(f32[256,256]{1,0:T(8,128)S(1)} %get-tuple-element.33.refs_0_, bf16[256,256]{1,0:T(8,128)(2,1)S(1)} %collective-permute-done.10.refs_1_, bf16[256,256]{1,0:T(8,128)(2,1)S(1)} %collective-permute-done.9.refs_3_.refs_2_, f32[256,256]{1,0:T(8,128)S(1)} %get-tuple-element.39.refs_3_, ...), custom_call_target="tpu_custom_call" | custom-call | tf_op jit(solution)/shard_map/pallas_call | solution.py:158
  (14 shorter events, 0.3 us)
Async XLA Ops:
  2.4 15.1 %collective-permute-start.1 = (bf16[128,2048]{1,0:T(8,128)(2,1)S(1)}, bf16[128,2048]{1,0:T(8,128)(2,1)S(1)}, u32[]{:S(2)}, u32[]{:S(2)}) collective-permute-start(bf16[128,2048]{1,0:T(8,128)(2,1)S(1)} %get-tuple-element.29), channel_id=1, source_target_pairs={{0,2},{1,3},{2,0},{3,1},{4,6},{5,7},{6,4},{7,5},{8,10},{9,11},{10,... | collective-permute-start | bytes 1572872 | tf_op jit(solution)/shard_map/ppermute | solution.py:381
  5.4 10.0 %collective-permute-start.3 = (bf16[272,512]{1,0:T(8,128)(2,1)S(1)}, bf16[272,512]{1,0:T(8,128)(2,1)S(1)}, u32[]{:S(2)}, u32[]{:S(2)}) collective-permute-start(bf16[272,512]{1,0:T(8,128)(2,1)S(1)} %get-tuple-element.30.even_ref.refs_5_), channel_id=1, source_target_pairs={{0,8},{4,12},{8,16},{12,20},{16,24},{20,28},{24,0},{28,4},{1,9},{5... | collective-permute-start | bytes 835592 | tf_op jit(solution)/shard_map/ppermute | solution.py:379
  15.4 8.7 %collective-permute-start.4 = (bf16[272,512]{1,0:T(8,128)(2,1)S(1)}, bf16[272,512]{1,0:T(8,128)(2,1)S(1)}, u32[]{:S(2)}, u32[]{:S(2)}) collective-permute-start(bf16[272,512]{1,0:T(8,128)(2,1)S(1)} %shard_map.78), channel_id=1, source_target_pairs={{0,4},{4,0},{8,12},{12,8},{16,20},{20,16},{24,28},{28,24},{1,5},{5... | collective-permute-start | bytes 835592 | tf_op jit(solution)/shard_map/ppermute | solution.py:388
  17.0 8.8 %collective-permute-start.6 = (bf16[272,512]{1,0:T(8,128)(2,1)S(1)}, bf16[272,512]{1,0:T(8,128)(2,1)S(1)}, u32[]{:S(2)}, u32[]{:S(2)}) collective-permute-start(bf16[272,512]{1,0:T(8,128)(2,1)S(1)} %collective-permute-done.3.odd_ref.refs_8_), channel_id=1, source_target_pairs={{0,8},{4,12},{8,16},{12,20},{16,24},{20,28},{24,0},{28,4},{1,9},{5... | collective-permute-start | bytes 835592 | tf_op jit(solution)/shard_map/ppermute | solution.py:387
  17.0 14.7 %collective-permute-start.5 = (bf16[272,512]{1,0:T(8,128)(2,1)S(1)}, bf16[272,512]{1,0:T(8,128)(2,1)S(1)}, u32[]{:S(2)}, u32[]{:S(2)}) collective-permute-start(bf16[272,512]{1,0:T(8,128)(2,1)S(1)} %collective-permute-done.3.odd_ref.refs_8_), channel_id=1, source_target_pairs={{0,4},{4,8},{8,12},{12,16},{16,20},{20,24},{24,28},{28,0},{1,5},{5... | collective-permute-start | bytes 835592 | tf_op jit(solution)/shard_map/ppermute | solution.py:386
  17.5 1.5 %collective-permute-start = (bf16[64,2048]{1,0:T(8,128)(2,1)S(1)}, bf16[64,2048]{1,0:T(8,128)(2,1)S(1)}, u32[]{:S(2)}, u32[]{:S(2)}) collective-permute-start(bf16[64,2048]{1,0:T(8,128)(2,1)S(1)} %get-tuple-element.28), channel_id=1, source_target_pairs={{0,1},{1,0},{2,3},{3,2},{4,5},{5,4},{6,7},{7,6},{8,9},{9,8},{10,11... | collective-permute-start | bytes 786440 | tf_op jit(solution)/shard_map/ppermute | solution.py:389
  17.6 14.2 %collective-permute-start.2 = (bf16[64,2048]{1,0:T(8,128)(2,1)S(1)}, bf16[64,2048]{1,0:T(8,128)(2,1)S(1)}, u32[]{:S(2)}, u32[]{:S(2)}) collective-permute-start(bf16[64,2048]{1,0:T(8,128)(2,1)S(1)} %shard_map.77), channel_id=1, source_target_pairs={{0,1},{1,0},{2,3},{3,2},{4,5},{5,4},{6,7},{7,6},{8,9},{9,8},{10,11... | collective-permute-start | bytes 786440 | tf_op jit(solution)/shard_map/ppermute | solution.py:391
  41.1 11.5 %collective-permute-start.7 = (bf16[256,256]{1,0:T(8,128)(2,1)S(1)}, bf16[256,256]{1,0:T(8,128)(2,1)S(1)}, u32[]{:S(2)}, u32[]{:S(2)}) collective-permute-start(bf16[256,256]{1,0:T(8,128)(2,1)S(1)} %get-tuple-element.34), channel_id=1, source_target_pairs={{8,0},{12,4},{16,8},{20,12},{24,16},{28,20},{0,24},{4,28},{9,1},{1... | collective-permute-start | bytes 393224 | tf_op jit(solution)/shard_map/ppermute | solution.py:405
  41.2 11.4 %collective-permute-start.8 = (bf16[256,256]{1,0:T(8,128)(2,1)S(1)}, bf16[256,256]{1,0:T(8,128)(2,1)S(1)}, u32[]{:S(2)}, u32[]{:S(2)}) collective-permute-start(bf16[256,256]{1,0:T(8,128)(2,1)S(1)} %get-tuple-element.37), channel_id=1, source_target_pairs={{4,0},{8,4},{12,8},{16,12},{20,16},{24,20},{28,24},{0,28},{5,1},{9... | collective-permute-start | bytes 393224 | tf_op jit(solution)/shard_map/ppermute | solution.py:406
  41.3 11.4 %collective-permute-start.9 = (bf16[256,256]{1,0:T(8,128)(2,1)S(1)}, bf16[256,256]{1,0:T(8,128)(2,1)S(1)}, u32[]{:S(2)}, u32[]{:S(2)}) collective-permute-start(bf16[256,256]{1,0:T(8,128)(2,1)S(1)} %get-tuple-element.38), channel_id=1, source_target_pairs={{0,4},{4,0},{8,12},{12,8},{16,20},{20,16},{24,28},{28,24},{1,5},{5... | collective-permute-start | bytes 393224 | tf_op jit(solution)/shard_map/ppermute | solution.py:406
  52.6 5.2 %collective-permute-start.11 = (bf16[256,256]{1,0:T(8,128)(2,1)S(1)}, bf16[256,256]{1,0:T(8,128)(2,1)S(1)}, u32[]{:S(2)}, u32[]{:S(2)}) collective-permute-start(bf16[256,256]{1,0:T(8,128)(2,1)S(1)} %get-tuple-element.41), channel_id=1, source_target_pairs={{8,0},{12,4},{16,8},{20,12},{24,16},{28,20},{0,24},{4,28},{9,1},{1... | collective-permute-start | bytes 393224 | tf_op jit(solution)/shard_map/ppermute | solution.py:405
  52.9 5.3 %collective-permute-start.12 = (bf16[256,256]{1,0:T(8,128)(2,1)S(1)}, bf16[256,256]{1,0:T(8,128)(2,1)S(1)}, u32[]{:S(2)}, u32[]{:S(2)}) collective-permute-start(bf16[256,256]{1,0:T(8,128)(2,1)S(1)} %get-tuple-element.44), channel_id=1, source_target_pairs={{4,0},{8,4},{12,8},{16,12},{20,16},{24,20},{28,24},{0,28},{5,1},{9... | collective-permute-start | bytes 393224 | tf_op jit(solution)/shard_map/ppermute | solution.py:406
  55.0 5.0 %collective-permute-start.13 = (bf16[256,256]{1,0:T(8,128)(2,1)S(1)}, bf16[256,256]{1,0:T(8,128)(2,1)S(1)}, u32[]{:S(2)}, u32[]{:S(2)}) collective-permute-start(bf16[256,256]{1,0:T(8,128)(2,1)S(1)} %get-tuple-element.46), channel_id=1, source_target_pairs={{0,4},{4,0},{8,12},{12,8},{16,20},{20,16},{24,28},{28,24},{1,5},{5... | collective-permute-start | bytes 393224 | tf_op jit(solution)/shard_map/ppermute | solution.py:406
  55.0 7.1 %collective-permute-start.10 = (bf16[256,256]{1,0:T(8,128)(2,1)S(1)}, bf16[256,256]{1,0:T(8,128)(2,1)S(1)}, u32[]{:S(2)}, u32[]{:S(2)}) collective-permute-start(bf16[256,256]{1,0:T(8,128)(2,1)S(1)} %shard_map.81), channel_id=1, source_target_pairs={{8,0},{12,4},{16,8},{20,12},{24,16},{28,20},{0,24},{4,28},{9,1},{1... | collective-permute-start | bytes 393224 | tf_op jit(solution)/shard_map/ppermute | solution.py:415
  60.0 5.0 %collective-permute-start.14 = (bf16[256,256]{1,0:T(8,128)(2,1)S(1)}, bf16[256,256]{1,0:T(8,128)(2,1)S(1)}, u32[]{:S(2)}, u32[]{:S(2)}) collective-permute-start(bf16[256,256]{1,0:T(8,128)(2,1)S(1)} %shard_map.82), channel_id=1, source_target_pairs={{8,0},{12,4},{16,8},{20,12},{24,16},{28,20},{0,24},{4,28},{9,1},{1... | collective-permute-start | bytes 393224 | tf_op jit(solution)/shard_map/ppermute | solution.py:415
where the time goes:
time: 66 us; the launch traced here: 65.8 us
  waiting for transfers between devices  27.7 us (42%)
  Pallas kernels  21.5 us (33%)
  starting transfers between devices  16 us (24%)
  between operations  0.71 us (1%)
    pallas_call x2, Pallas kernels, head_call(): pl.pallas_call(functools.partial(main_kernel, h, reach, group, n_tp, firs...  18.7 us
    ppermute x1, waiting for transfers between devices, local(): evens = [lax.ppermute(block, 'seq', two_up)]  8.4 us
    ppermute x1, waiting for transfers between devices, local(): odds.append(lax.ppermute(evens[-1], 'seq', one_up))  5.91 us
    ppermute x1, waiting for transfers between devices, local(): odds[0] = lax.ppermute(choose(block, evens[0]), 'seq', swap)  5.07 us
    ppermute x2, starting transfers between devices, local(): moving = lax.ppermute(relay(k == 1, *parts), 'seq', two_down)  4.24 us
    ppermute x4, starting transfers between devices, local(): lax.ppermute(x, 'seq', one_down if k else swap)  4.12 us
    ppermute x1, starting transfers between devices, local(): lax.ppermute(pair, 'tp', [(a, a ^ 2 * m + 2) for a in range(n_tp)])  3 us
    ppermute x2, waiting for transfers between devices, local(): moving = lax.ppermute(relay(k == 1, *parts), 'seq', two_down)  2.9 us
  transfers between devices with their start and end apart: 15, of which 9 were waited for; matrix products, arithmetic and copies ran while one was open for 0% of the time, Pallas kernels for 14%

commit v1 on v0

--- a/solution.py
+++ b/solution.py
@@ -217,34 +217,50 @@
         row = block[T : T + 1, at : at + T].astype(jnp.float32)
         row = jnp.where(i >= d, row, float(DOCS))
         one_hot = jnp.where(code == row, 1.0, 0.0).astype(jnp.bfloat16)
-        kx[reach - d, :, 0:HEAD_WIDTH] = block[0:T, at : at + HEAD_WIDTH]
-        kx[reach - d, :, HEAD_WIDTH : 2 * HEAD_WIDTH] = one_hot.T
-        vx[reach - d] = block[0:T, at + HEAD_WIDTH : at + 2 * HEAD_WIDTH]
+        rows = slice((reach - d) * T, (reach - d + 1) * T)
+        kx[rows, 0:HEAD_WIDTH] = block[0:T, at : at + HEAD_WIDTH]
+        kx[rows, HEAD_WIDTH : 2 * HEAD_WIDTH] = one_hot.T
+        vx[rows, :] = block[0:T, at + HEAD_WIDTH : at + 2 * HEAD_WIDTH]
     own_row = own_ref[T : T + 1, at : at + T].astype(jnp.float32)
     away = jnp.where((code == own_row) | (code > DOCS), 0.0, NEG).astype(jnp.bfloat16).T
-    for g in range(group):
-        at = (h * group + g) * HEAD_WIDTH
-        qx[g, :, 0:HEAD_WIDTH] = query_ref[:, at : at + HEAD_WIDTH]
-        qx[g, :, HEAD_WIDTH : 2 * HEAD_WIDTH] = away
+    half_rows = T // 2
+    for unit in range(group):
+        queries_at = slice(unit % 2 * half_rows, (unit % 2 + 1) * half_rows)
+        for two in range(2):
+            at = (h * group + unit - unit % 2 + two) * HEAD_WIDTH
+            rows = slice(two * half_rows, (two + 1) * half_rows)
+            qx[unit, rows, 0:HEAD_WIDTH] = query_ref[queries_at, at : at + HEAD_WIDTH]
+            qx[unit, rows, HEAD_WIDTH : 2 * HEAD_WIDTH] = away[queries_at, :]
 
     factor = 1.0 / math.sqrt(HEAD_WIDTH)
     scale = factor * math.log2(math.e)
-    before = reach * T
+    seen_rows = window - half_rows
+    before = seen_rows - half_rows
 
     def by_eight(x):
         return x.reshape(x.shape[0] // 8, 8, T)
 
-    def dq_copy(g):
-        cols = pl.ds(pl.multiple_of((h * group + g) * HEAD_WIDTH, HEAD_WIDTH), HEAD_WIDTH)
-        return pltpu.make_async_copy(dq_out.at[g], dq_ref.at[:, cols], out_sems.at[g])
+    def dq_copies(unit, part):
+        copies = []
+        for two in range(2):
+            at = pl.multiple_of((h * group + unit - part + two) * HEAD_WIDTH, HEAD_WIDTH)
+            copies.append(
+                pltpu.make_async_copy(
+                    dq_out.at[unit, pl.ds(two * half_rows, half_rows), :],
+                    dq_ref.at[pl.ds(part * half_rows, half_rows), pl.ds(at, HEAD_WIDTH)],
+                    out_sems.at[unit, two],
+                )
+            )
+        return copies
 
     def step(score_of, weight_of, grad_of, b):
         c = 1 - b
+        rows = [slice(half_rows * part, half_rows * part + seen_rows) for part in range(2)]
         if score_of is not None:
-            s = nt_dot(kx[...].reshape(window, 2 * HEAD_WIDTH), qx[score_of])
-            causal = lax.broadcasted_iota(jnp.int32, (T, T), 0) <= lax.broadcasted_iota(
-                jnp.int32, (T, T), 1
-            )
+            s = nt_dot(kx[rows[b], :], qx[score_of])
+            query = lax.broadcasted_iota(jnp.int32, (half_rows, T), 1)
+            query = jnp.where(query >= half_rows, query - half_rows, query)
+            causal = lax.broadcasted_iota(jnp.int32, (half_rows, T), 0) <= query
             own = jnp.where(causal, s[before:], NEG)
             scores[b][0:before] = s[:before]
             scores[b][before:] = own
@@ -253,7 +269,7 @@
             )
         if weight_of is not None:
             top = jnp.max(peaks[c][...], axis=0, keepdims=True) * scale
-            dp = nt_dot(vx[...].reshape(window, HEAD_WIDTH), gs[weight_of])
+            dp = nt_dot(vx[rows[c], :], gs[weight_of])
             e = jnp.exp2(scores[c][...] * scale - top)
             weights[c][...] = e.astype(jnp.bfloat16)
             grads[c][...] = dp
@@ -268,12 +284,12 @@
             column = jnp.broadcast_to(inverse, (HEAD_WIDTH, T)).T
             query = (qx[grad_of, :, 0:HEAD_WIDTH].astype(jnp.float32) * column).astype(jnp.bfloat16)
             grad = (gs[grad_of].astype(jnp.float32) * column).astype(jnp.bfloat16)
-        if grad_of is not None:
-            dq = nn_dot(kt[...], ds) * (inverse * factor)
+            dq = nn_dot(kt[:, rows[b]], ds) * (inverse * factor)
             dq_out[grad_of] = dq.T.astype(jnp.bfloat16)
-            dq_copy(grad_of).start()
-            dv_acc[...] += nn_dot(e_old, grad)
-            dk_acc[...] += nn_dot(ds, query)
+            for copy in dq_copies(grad_of, b):
+                copy.start()
+            dv_acc[rows[b], :] += nn_dot(e_old, grad)
+            dk_acc[rows[b], :] += nn_dot(ds, query)
 
     def two_steps(pair, _):
         g = 2 * pair
@@ -282,14 +298,16 @@
         return 0
 
     step(0, None, None, 0)
-    for d in range(reach + 1):
-        kt[:, (reach - d) * T : (reach - d + 1) * T] = kx[reach - d, :, 0:HEAD_WIDTH].T
+    for j in range(reach + 1):
+        kt[:, j * T : (j + 1) * T] = kx[j * T : (j + 1) * T, 0:HEAD_WIDTH].T
     for m in range(n_tp):
-        rows = pl.ds(pl.multiple_of((t ^ m) * sub, sub), sub)
-        src = grad_refs[m]
+        first_row = (t ^ m) * sub
+        part = first_row // half_rows
+        at_row = pl.multiple_of(first_row - part * half_rows, sub)
         for g in range(group):
             at = h * W + g * HEAD_WIDTH
-            gs[g, rows, :] = src[0:sub, at : at + HEAD_WIDTH]
+            rows = pl.ds(pl.multiple_of(g % 2 * half_rows + at_row, sub), sub)
+            gs[g - g % 2 + part, rows, :] = grad_refs[m][0:sub, at : at + HEAD_WIDTH]
     step(1, 0, None, 1)
     lax.fori_loop(0, group // 2 - 1, two_steps, 0)
     step(None, group - 1, group - 2, 0)
@@ -300,22 +318,23 @@
         rows = slice((reach - d) * T, (reach - d + 1) * T)
         dst[:, 0:HEAD_WIDTH] = dk_acc[rows, :].astype(dst.dtype)
         dst[:, HEAD_WIDTH : 2 * HEAD_WIDTH] = dv_acc[rows, :].astype(dst.dtype)
-    for g in range(group):
-        dq_copy(g).wait()
+    for unit in range(group):
+        for copy in dq_copies(unit, unit % 2):
+            copy.wait()
 
 
 def scratch_of(window, T, group):
     bf16, f32 = jnp.bfloat16, jnp.float32
     return [
-        pltpu.VMEM((window, T, 2 * HEAD_WIDTH), bf16),
-        pltpu.VMEM((window, T, HEAD_WIDTH), bf16),
+        pltpu.VMEM((window * T, 2 * HEAD_WIDTH), bf16),
+        pltpu.VMEM((window * T, HEAD_WIDTH), bf16),
         pltpu.VMEM((HEAD_WIDTH, window * T), bf16),
         pltpu.VMEM((group, T, 2 * HEAD_WIDTH), bf16),
         pltpu.VMEM((group, T, HEAD_WIDTH), bf16),
-        *[pltpu.VMEM((window * T, T), f32)] * 2,
+        *[pltpu.VMEM((window * T - T // 2, T), f32)] * 2,
         *[pltpu.VMEM((8, T), f32)] * 2,
-        *[pltpu.VMEM((window * T, T), f32)] * 2,
-        *[pltpu.VMEM((window * T, T), bf16)] * 2,
+        *[pltpu.VMEM((window * T - T // 2, T), f32)] * 2,
+        *[pltpu.VMEM((window * T - T // 2, T), bf16)] * 2,
         *[pltpu.VMEM((8, T), f32)] * 2,
         pltpu.VMEM((window * T, HEAD_WIDTH), f32),
         pltpu.VMEM((window * T, HEAD_WIDTH), f32),
@@ -342,7 +361,7 @@
         in_specs=specs,
         out_specs=(ANY,) + (VMEM,) * (reach + 1),
         input_output_aliases={} if first else {len(args) - 1: 0},
-        scratch_shapes=[*scratch, pltpu.SemaphoreType.DMA((group,))],
+        scratch_shapes=[*scratch, pltpu.SemaphoreType.DMA((group, 2))],
         compiler_params=pltpu.CompilerParams(
             vmem_limit_bytes=2 * sum(math.prod(x.shape) * x.dtype.itemsize for x in scratch)
         ),

time: 66 us -> 64.1 us (0.971)
  Pallas kernels: 21.5 us -> 19.6 us
    pallas_call x2, Pallas kernels: 18.7 us -> 16.8 us  [head_call(): pl.pallas_call(functools.partial(main_kernel, h, reach, group, n_tp, firs...]
  transfers between devices with their start and end apart: 15 -> 15, of which waited for: 9 -> 9; matrix products, arithmetic and copies ran while one was open for 0% -> 0% of each run, Pallas kernels for 14% -> 13%
where the time goes in v1:
time: 64.1 us; the launch traced here: 63.9 us
  waiting for transfers between devices  27.7 us (43%)
  Pallas kernels  19.6 us (31%)
  starting transfers between devices  16 us (25%)
  between operations  0.71 us (1%)
    pallas_call x2, Pallas kernels, head_call(): pl.pallas_call(functools.partial(main_kernel, h, reach, group, n_tp, firs...  16.8 us
    ppermute x1, waiting for transfers between devices, local(): evens = [lax.ppermute(block, 'seq', two_up)]  8.4 us
    ppermute x1, waiting for transfers between devices, local(): odds.append(lax.ppermute(evens[-1], 'seq', one_up))  5.91 us
    ppermute x1, waiting for transfers between devices, local(): odds[0] = lax.ppermute(choose(block, evens[0]), 'seq', swap)  5.07 us
    ppermute x2, starting transfers between devices, local(): moving = lax.ppermute(relay(k == 1, *parts), 'seq', two_down)  4.24 us
    ppermute x4, starting transfers between devices, local(): lax.ppermute(x, 'seq', one_down if k else swap)  4.12 us
    ppermute x1, starting transfers between devices, local(): lax.ppermute(pair, 'tp', [(a, a ^ 2 * m + 2) for a in range(n_tp)])  3 us
    ppermute x2, waiting for transfers between devices, local(): moving = lax.ppermute(relay(k == 1, *parts), 'seq', two_down)  2.9 us
  transfers between devices with their start and end apart: 15, of which 9 were waited for; matrix products, arithmetic and copies ran while one was open for 0% of the time, Pallas kernels for 13%

profile of v1, /device:TPU:0, one launch (start us, length us, event | category | flops | bytes accessed | tf_op | source)
XLA Modules:
  0.0 63.9 jit_solution(11885781396411855798)
XLA Ops:
  0.6 1.8 %shard_map.76 = (bf16[272,512]{1,0:T(8,128)(2,1)S(1)}, bf16[256,2048]{1,0:T(8,128)(2,1)S(1)}, bf16[64,2048]{1,0:T(8,128)(2,1)S(1)}, bf16[64,2048]{1,0:T(8,128)(2,1)S(1)}, bf16[128,2048]{1,0:T(8,128)(2,1)S(1)}) custom-call(bf16[256,256]{1,0:T(8,128)(2,1)} %key_ref.1, bf16[256,256]{1,0:T(8,128)(2,1)} %value_ref.1, s32[1,256]{1,0:T(1,128)} %bitcast.1, ...), custom_call_target="tpu_custom_call" | custom-call | tf_op jit(solution)/shard_map/pallas_call | solution.py:71
  2.4 3.0 %collective-permute-start.1 = (bf16[128,2048]{1,0:T(8,128)(2,1)S(1)}, bf16[128,2048]{1,0:T(8,128)(2,1)S(1)}, u32[]{:S(2)}, u32[]{:S(2)}) collective-permute-start(bf16[128,2048]{1,0:T(8,128)(2,1)S(1)} %get-tuple-element.29), channel_id=1, source_target_pairs={{0,2},{1,3},{2,0},{3,1},{4,6},{5,7},{6,4},{7,5},{8,10},{9,11},{10,... | collective-permute-start | bytes 1572872 | tf_op jit(solution)/shard_map/ppermute | solution.py:400
  5.4 1.6 %collective-permute-start.3 = (bf16[272,512]{1,0:T(8,128)(2,1)S(1)}, bf16[272,512]{1,0:T(8,128)(2,1)S(1)}, u32[]{:S(2)}, u32[]{:S(2)}) collective-permute-start(bf16[272,512]{1,0:T(8,128)(2,1)S(1)} %get-tuple-element.30.even_ref.refs_5_), channel_id=1, source_target_pairs={{0,8},{4,12},{8,16},{12,20},{16,24},{20,28},{24,0},{28,4},{1,9},{5... | collective-permute-start | bytes 835592 | tf_op jit(solution)/shard_map/ppermute | solution.py:398
  7.0 8.4 %collective-permute-done.3.odd_ref.refs_8_ = bf16[272,512]{1,0:T(8,128)(2,1)S(1)} collective-permute-done((bf16[272,512]{1,0:T(8,128)(2,1)S(1)}, bf16[272,512]{1,0:T(8,128)(2,1)S(1)}, u32[]{:S(2)}, u32[]{:S(2)}) %collective-permute-start.3) | collective-permute-done | bytes 278560 | tf_op jit(solution)/shard_map/ppermute | solution.py:398
  15.4 1.6 %collective-permute-start.4 = (bf16[272,512]{1,0:T(8,128)(2,1)S(1)}, bf16[272,512]{1,0:T(8,128)(2,1)S(1)}, u32[]{:S(2)}, u32[]{:S(2)}) collective-permute-start(bf16[272,512]{1,0:T(8,128)(2,1)S(1)} %shard_map.78), channel_id=1, source_target_pairs={{0,4},{4,0},{8,12},{12,8},{16,20},{20,16},{24,28},{28,24},{1,5},{5... | collective-permute-start | bytes 835592 | tf_op jit(solution)/shard_map/ppermute | solution.py:407
  17.0 0.5 collective-permute-start.5
  17.6 0.6 collective-permute-start.2
  18.1 0.9 %collective-permute-done.refs_2_ = bf16[64,2048]{1,0:T(8,128)(2,1)S(1)} collective-permute-done((bf16[64,2048]{1,0:T(8,128)(2,1)S(1)}, bf16[64,2048]{1,0:T(8,128)(2,1)S(1)}, u32[]{:S(2)}, u32[]{:S(2)}) %collective-permute-start) | collective-permute-done | bytes 262176 | tf_op jit(solution)/shard_map/ppermute | solution.py:408
  19.1 5.1 %collective-permute-done.4.refs_6_ = bf16[272,512]{1,0:T(8,128)(2,1)S(1)} collective-permute-done((bf16[272,512]{1,0:T(8,128)(2,1)S(1)}, bf16[272,512]{1,0:T(8,128)(2,1)S(1)}, u32[]{:S(2)}, u32[]{:S(2)}) %collective-permute-start.4) | collective-permute-done | bytes 278560 | tf_op jit(solution)/shard_map/ppermute | solution.py:407
  24.1 1.7 %collective-permute-done.6.refs_9_ = bf16[272,512]{1,0:T(8,128)(2,1)S(1)} collective-permute-done((bf16[272,512]{1,0:T(8,128)(2,1)S(1)}, bf16[272,512]{1,0:T(8,128)(2,1)S(1)}, u32[]{:S(2)}, u32[]{:S(2)}) %collective-permute-start.6) | collective-permute-done | bytes 278560 | tf_op jit(solution)/shard_map/ppermute | solution.py:406
  25.8 5.9 %collective-permute-done.5.refs_7_ = bf16[272,512]{1,0:T(8,128)(2,1)S(1)} collective-permute-done((bf16[272,512]{1,0:T(8,128)(2,1)S(1)}, bf16[272,512]{1,0:T(8,128)(2,1)S(1)}, u32[]{:S(2)}, u32[]{:S(2)}) %collective-permute-start.5) | collective-permute-done | bytes 278560 | tf_op jit(solution)/shard_map/ppermute | solution.py:405
  31.7 8.4 %shard_map.79 = (bf16[256,2048]{1,0:T(8,128)(2,1)}, bf16[256,256]{1,0:T(8,128)(2,1)S(1)}, bf16[256,256]{1,0:T(8,128)(2,1)S(1)}, bf16[256,256]{1,0:T(8,128)(2,1)S...) custom-call(bf16[256,2048]{1,0:T(8,128)(2,1)S(1)} %get-tuple-element.26.refs_0_, ...), custom_call_target="tpu_custom_call" | custom-call | flops 13421772800 | bytes 4194304 | tf_op jit(solution)/shard_map/pallas_call | solution.py:356
  40.2 0.1 collective-permute-start.8
  40.3 2.0 %collective-permute-start.9 = (bf16[256,256]{1,0:T(8,128)(2,1)S(1)}, bf16[256,256]{1,0:T(8,128)(2,1)S(1)}, u32[]{:S(2)}, u32[]{:S(2)}) collective-permute-start(bf16[256,256]{1,0:T(8,128)(2,1)S(1)} %get-tuple-element.38), channel_id=1, source_target_pairs={{0,4},{4,0},{8,12},{12,8},{16,20},{20,16},{24,28},{28,24},{1,5},{5... | collective-permute-start | bytes 393224 | tf_op jit(solution)/shard_map/ppermute | solution.py:425
  42.3 8.4 %shard_map.80 = (bf16[256,2048]{1,0:T(8,128)(2,1)}, bf16[256,256]{1,0:T(8,128)(2,1)S(1)}, bf16[256,256]{1,0:T(8,128)(2,1)S(1)}, bf16[256,256]{1,0:T(8,128)(2,1)S...) custom-call(bf16[256,2048]{1,0:T(8,128)(2,1)S(1)} %get-tuple-element.26.refs_0_, ...), custom_call_target="tpu_custom_call", output_to_operand_aliasing={{0}: (10, {})} | custom-call | flops 13421772800 | bytes 4194304 | tf_op jit(solution)/shard_map/pallas_call | solution.py:356
  50.7 0.3 collective-permute-start.11
  51.0 2.0 %collective-permute-start.12 = (bf16[256,256]{1,0:T(8,128)(2,1)S(1)}, bf16[256,256]{1,0:T(8,128)(2,1)S(1)}, u32[]{:S(2)}, u32[]{:S(2)}) collective-permute-start(bf16[256,256]{1,0:T(8,128)(2,1)S(1)} %get-tuple-element.44), channel_id=1, source_target_pairs={{4,0},{8,4},{12,8},{16,12},{20,16},{24,20},{28,24},{0,28},{5,1},{9... | collective-permute-start | bytes 393224 | tf_op jit(solution)/shard_map/ppermute | solution.py:425
  53.1 2.1 %collective-permute-start.10 = (bf16[256,256]{1,0:T(8,128)(2,1)S(1)}, bf16[256,256]{1,0:T(8,128)(2,1)S(1)}, u32[]{:S(2)}, u32[]{:S(2)}) collective-permute-start(bf16[256,256]{1,0:T(8,128)(2,1)S(1)} %shard_map.81), channel_id=1, source_target_pairs={{8,0},{12,4},{16,8},{20,12},{24,16},{28,20},{0,24},{4,28},{9,1},{1... | collective-permute-start | bytes 393224 | tf_op jit(solution)/shard_map/ppermute | solution.py:434
  55.3 0.7 %collective-permute-done.11.refs_0_ = bf16[256,256]{1,0:T(8,128)(2,1)S(1)} collective-permute-done((bf16[256,256]{1,0:T(8,128)(2,1)S(1)}, bf16[256,256]{1,0:T(8,128)(2,1)S(1)}, u32[]{:S(2)}, u32[]{:S(2)}) %collective-permute-start.11) | collective-permute-done | bytes 131104 | tf_op jit(solution)/shard_map/ppermute | solution.py:424
  56.0 0.3 collective-permute-done.12.refs_2_
  56.3 1.7 %collective-permute-done.13.refs_3_.refs_5_ = bf16[256,256]{1,0:T(8,128)(2,1)S(1)} collective-permute-done((bf16[256,256]{1,0:T(8,128)(2,1)S(1)}, bf16[256,256]{1,0:T(8,128)(2,1)S(1)}, u32[]{:S(2)}, u32[]{:S(2)}) %collective-permute-start.13) | collective-permute-done | bytes 131104 | tf_op jit(solution)/shard_map/ppermute | solution.py:425
  58.1 2.1 %collective-permute-start.14 = (bf16[256,256]{1,0:T(8,128)(2,1)S(1)}, bf16[256,256]{1,0:T(8,128)(2,1)S(1)}, u32[]{:S(2)}, u32[]{:S(2)}) collective-permute-start(bf16[256,256]{1,0:T(8,128)(2,1)S(1)} %shard_map.82), channel_id=1, source_target_pairs={{8,0},{12,4},{16,8},{20,12},{24,16},{28,20},{0,24},{4,28},{9,1},{1... | collective-permute-start | bytes 393224 | tf_op jit(solution)/shard_map/ppermute | solution.py:434
  60.2 2.9 %collective-permute-done.14.refs_4_ = bf16[256,256]{1,0:T(8,128)(2,1)S(1)} collective-permute-done((bf16[256,256]{1,0:T(8,128)(2,1)S(1)}, bf16[256,256]{1,0:T(8,128)(2,1)S(1)}, u32[]{:S(2)}, u32[]{:S(2)}) %collective-permute-start.14) | collective-permute-done | bytes 131104 | tf_op jit(solution)/shard_map/ppermute | solution.py:434
  63.1 0.8 %shard_map.83 = (bf16[256,256]{1,0:T(8,128)(2,1)}, bf16[256,256]{1,0:T(8,128)(2,1)}) custom-call(f32[256,256]{1,0:T(8,128)S(1)} %get-tuple-element.33.refs_0_, bf16[256,256]{1,0:T(8,128)(2,1)S(1)} %collective-permute-done.10.refs_1_, bf16[256,256]{1,0:T(8,128)(2,1)S(1)} %collective-permute-done.9.refs_3_.refs_2_, f32[256,256]{1,0:T(8,128)S(1)} %get-tuple-element.39.refs_3_, ...), custom_call_target="tpu_custom_call" | custom-call | tf_op jit(solution)/shard_map/pallas_call | solution.py:158
  (14 shorter events, 0.3 us)
Async XLA Ops:
  2.4 15.1 %collective-permute-start.1 = (bf16[128,2048]{1,0:T(8,128)(2,1)S(1)}, bf16[128,2048]{1,0:T(8,128)(2,1)S(1)}, u32[]{:S(2)}, u32[]{:S(2)}) collective-permute-start(bf16[128,2048]{1,0:T(8,128)(2,1)S(1)} %get-tuple-element.29), channel_id=1, source_target_pairs={{0,2},{1,3},{2,0},{3,1},{4,6},{5,7},{6,4},{7,5},{8,10},{9,11},{10,... | collective-permute-start | bytes 1572872 | tf_op jit(solution)/shard_map/ppermute | solution.py:400
  5.4 10.0 %collective-permute-start.3 = (bf16[272,512]{1,0:T(8,128)(2,1)S(1)}, bf16[272,512]{1,0:T(8,128)(2,1)S(1)}, u32[]{:S(2)}, u32[]{:S(2)}) collective-permute-start(bf16[272,512]{1,0:T(8,128)(2,1)S(1)} %get-tuple-element.30.even_ref.refs_5_), channel_id=1, source_target_pairs={{0,8},{4,12},{8,16},{12,20},{16,24},{20,28},{24,0},{28,4},{1,9},{5... | collective-permute-start | bytes 835592 | tf_op jit(solution)/shard_map/ppermute | solution.py:398
  15.4 8.7 %collective-permute-start.4 = (bf16[272,512]{1,0:T(8,128)(2,1)S(1)}, bf16[272,512]{1,0:T(8,128)(2,1)S(1)}, u32[]{:S(2)}, u32[]{:S(2)}) collective-permute-start(bf16[272,512]{1,0:T(8,128)(2,1)S(1)} %shard_map.78), channel_id=1, source_target_pairs={{0,4},{4,0},{8,12},{12,8},{16,20},{20,16},{24,28},{28,24},{1,5},{5... | collective-permute-start | bytes 835592 | tf_op jit(solution)/shard_map/ppermute | solution.py:407
  17.0 8.8 %collective-permute-start.6 = (bf16[272,512]{1,0:T(8,128)(2,1)S(1)}, bf16[272,512]{1,0:T(8,128)(2,1)S(1)}, u32[]{:S(2)}, u32[]{:S(2)}) collective-permute-start(bf16[272,512]{1,0:T(8,128)(2,1)S(1)} %collective-permute-done.3.odd_ref.refs_8_), channel_id=1, source_target_pairs={{0,8},{4,12},{8,16},{12,20},{16,24},{20,28},{24,0},{28,4},{1,9},{5... | collective-permute-start | bytes 835592 | tf_op jit(solution)/shard_map/ppermute | solution.py:406
  17.0 14.7 %collective-permute-start.5 = (bf16[272,512]{1,0:T(8,128)(2,1)S(1)}, bf16[272,512]{1,0:T(8,128)(2,1)S(1)}, u32[]{:S(2)}, u32[]{:S(2)}) collective-permute-start(bf16[272,512]{1,0:T(8,128)(2,1)S(1)} %collective-permute-done.3.odd_ref.refs_8_), channel_id=1, source_target_pairs={{0,4},{4,8},{8,12},{12,16},{16,20},{20,24},{24,28},{28,0},{1,5},{5... | collective-permute-start | bytes 835592 | tf_op jit(solution)/shard_map/ppermute | solution.py:405
  17.5 1.5 %collective-permute-start = (bf16[64,2048]{1,0:T(8,128)(2,1)S(1)}, bf16[64,2048]{1,0:T(8,128)(2,1)S(1)}, u32[]{:S(2)}, u32[]{:S(2)}) collective-permute-start(bf16[64,2048]{1,0:T(8,128)(2,1)S(1)} %get-tuple-element.28), channel_id=1, source_target_pairs={{0,1},{1,0},{2,3},{3,2},{4,5},{5,4},{6,7},{7,6},{8,9},{9,8},{10,11... | collective-permute-start | bytes 786440 | tf_op jit(solution)/shard_map/ppermute | solution.py:408
  17.6 14.2 %collective-permute-start.2 = (bf16[64,2048]{1,0:T(8,128)(2,1)S(1)}, bf16[64,2048]{1,0:T(8,128)(2,1)S(1)}, u32[]{:S(2)}, u32[]{:S(2)}) collective-permute-start(bf16[64,2048]{1,0:T(8,128)(2,1)S(1)} %shard_map.77), channel_id=1, source_target_pairs={{0,1},{1,0},{2,3},{3,2},{4,5},{5,4},{6,7},{7,6},{8,9},{9,8},{10,11... | collective-permute-start | bytes 786440 | tf_op jit(solution)/shard_map/ppermute | solution.py:410
  40.1 10.6 %collective-permute-start.7 = (bf16[256,256]{1,0:T(8,128)(2,1)S(1)}, bf16[256,256]{1,0:T(8,128)(2,1)S(1)}, u32[]{:S(2)}, u32[]{:S(2)}) collective-permute-start(bf16[256,256]{1,0:T(8,128)(2,1)S(1)} %get-tuple-element.34), channel_id=1, source_target_pairs={{8,0},{12,4},{16,8},{20,12},{24,16},{28,20},{0,24},{4,28},{9,1},{1... | collective-permute-start | bytes 393224 | tf_op jit(solution)/shard_map/ppermute | solution.py:424
  40.2 10.5 %collective-permute-start.8 = (bf16[256,256]{1,0:T(8,128)(2,1)S(1)}, bf16[256,256]{1,0:T(8,128)(2,1)S(1)}, u32[]{:S(2)}, u32[]{:S(2)}) collective-permute-start(bf16[256,256]{1,0:T(8,128)(2,1)S(1)} %get-tuple-element.37), channel_id=1, source_target_pairs={{4,0},{8,4},{12,8},{16,12},{20,16},{24,20},{28,24},{0,28},{5,1},{9... | collective-permute-start | bytes 393224 | tf_op jit(solution)/shard_map/ppermute | solution.py:425
  40.3 10.4 %collective-permute-start.9 = (bf16[256,256]{1,0:T(8,128)(2,1)S(1)}, bf16[256,256]{1,0:T(8,128)(2,1)S(1)}, u32[]{:S(2)}, u32[]{:S(2)}) collective-permute-start(bf16[256,256]{1,0:T(8,128)(2,1)S(1)} %get-tuple-element.38), channel_id=1, source_target_pairs={{0,4},{4,0},{8,12},{12,8},{16,20},{20,16},{24,28},{28,24},{1,5},{5... | collective-permute-start | bytes 393224 | tf_op jit(solution)/shard_map/ppermute | solution.py:425
  50.7 5.3 %collective-permute-start.11 = (bf16[256,256]{1,0:T(8,128)(2,1)S(1)}, bf16[256,256]{1,0:T(8,128)(2,1)S(1)}, u32[]{:S(2)}, u32[]{:S(2)}) collective-permute-start(bf16[256,256]{1,0:T(8,128)(2,1)S(1)} %get-tuple-element.41), channel_id=1, source_target_pairs={{8,0},{12,4},{16,8},{20,12},{24,16},{28,20},{0,24},{4,28},{9,1},{1... | collective-permute-start | bytes 393224 | tf_op jit(solution)/shard_map/ppermute | solution.py:424
  51.0 5.3 %collective-permute-start.12 = (bf16[256,256]{1,0:T(8,128)(2,1)S(1)}, bf16[256,256]{1,0:T(8,128)(2,1)S(1)}, u32[]{:S(2)}, u32[]{:S(2)}) collective-permute-start(bf16[256,256]{1,0:T(8,128)(2,1)S(1)} %get-tuple-element.44), channel_id=1, source_target_pairs={{4,0},{8,4},{12,8},{16,12},{20,16},{24,20},{28,24},{0,28},{5,1},{9... | collective-permute-start | bytes 393224 | tf_op jit(solution)/shard_map/ppermute | solution.py:425
  53.1 5.0 %collective-permute-start.13 = (bf16[256,256]{1,0:T(8,128)(2,1)S(1)}, bf16[256,256]{1,0:T(8,128)(2,1)S(1)}, u32[]{:S(2)}, u32[]{:S(2)}) collective-permute-start(bf16[256,256]{1,0:T(8,128)(2,1)S(1)} %get-tuple-element.46), channel_id=1, source_target_pairs={{0,4},{4,0},{8,12},{12,8},{16,20},{20,16},{24,28},{28,24},{1,5},{5... | collective-permute-start | bytes 393224 | tf_op jit(solution)/shard_map/ppermute | solution.py:425
  53.1 7.1 %collective-permute-start.10 = (bf16[256,256]{1,0:T(8,128)(2,1)S(1)}, bf16[256,256]{1,0:T(8,128)(2,1)S(1)}, u32[]{:S(2)}, u32[]{:S(2)}) collective-permute-start(bf16[256,256]{1,0:T(8,128)(2,1)S(1)} %shard_map.81), channel_id=1, source_target_pairs={{8,0},{12,4},{16,8},{20,12},{24,16},{28,20},{0,24},{4,28},{9,1},{1... | collective-permute-start | bytes 393224 | tf_op jit(solution)/shard_map/ppermute | solution.py:434
  58.1 5.0 %collective-permute-start.14 = (bf16[256,256]{1,0:T(8,128)(2,1)S(1)}, bf16[256,256]{1,0:T(8,128)(2,1)S(1)}, u32[]{:S(2)}, u32[]{:S(2)}) collective-permute-start(bf16[256,256]{1,0:T(8,128)(2,1)S(1)} %shard_map.82), channel_id=1, source_target_pairs={{8,0},{12,4},{16,8},{20,12},{24,16},{28,20},{0,24},{4,28},{9,1},{1... | collective-permute-start | bytes 393224 | tf_op jit(solution)/shard_map/ppermute | solution.py:434

commit v2 on v1

--- a/solution.py
+++ b/solution.py
@@ -30,8 +30,9 @@
         copies.append(pltpu.make_async_copy(src, dst, sems.at[len(copies)]))
         copies[-1].start()
 
-    def columns(m):
-        return grad_ref.at[:, pl.ds(pl.multiple_of((me ^ m) * width, width), width)]
+    def columns(m, at, size):
+        start = pl.multiple_of((me ^ m) * width + at, size)
+        return grad_ref.at[:, pl.ds(start, size)]
 
     add(doc_ref, doc_scr)
     for h in range(heads):
@@ -41,10 +42,14 @@
                 src.at[:, pl.ds(h * HEAD_WIDTH, HEAD_WIDTH)],
                 block_out.at[pl.ds(0, tokens), cols],
             )
+    part = width // heads
     for m in range(2, n_tp):
-        add(columns(m), across_outs[m // 2 - 1].at[pl.ds(m % 2 * rows, rows), :])
-    add(columns(1), beside_out)
-    add(columns(0), own_out)
+        for h in range(heads):
+            out = across_outs[(m // 2 - 1) * heads + h]
+            src = columns(m, h * part, part)
+            add(src, out.at[pl.ds(m % 2 * rows, rows), :])
+    add(columns(1, 0, width), beside_out)
+    add(columns(0, 0, width), own_out)
     add(query_ref, query_out)
     copies[0].wait()
     row = doc_scr[...].astype(jnp.float32).astype(jnp.bfloat16)
@@ -60,13 +65,13 @@
     rows, width = output_gradient.shape
     chips = n_tp // 2 - 1
     one = pltpu.VMEM((rows, width // n_tp), jnp.bfloat16)
-    two = pltpu.VMEM((2 * rows, width // n_tp), jnp.bfloat16)
+    two = pltpu.VMEM((2 * rows, width // n_tp // heads), jnp.bfloat16)
     shapes = (
         pltpu.VMEM((tokens + PAD, 2 * kv_width), jnp.bfloat16),
         pltpu.VMEM(queries.shape, jnp.bfloat16),
         one,
         one,
-    ) + (two,) * chips
+    ) + (two,) * (chips * heads)
     args = (key_matrix, value_matrix, document.reshape(1, tokens), output_gradient, queries)
     block, query, own, beside, *across = pl.pallas_call(
         functools.partial(prepare_kernel, n_tp, heads),
@@ -75,48 +80,54 @@
         out_specs=(VMEM,) * len(shapes),
         scratch_shapes=[
             pltpu.VMEM((1, tokens), jnp.int32),
-            pltpu.SemaphoreType.DMA((2 * heads + n_tp + 2,)),
+            pltpu.SemaphoreType.DMA((2 * heads + 4 + 2 * chips * heads,)),
         ],
         compiler_params=SMALL,
     )(*[pltpu.with_memory_space_constraint(x, pltpu.HBM) for x in args])
     return block, query, own, beside, across
 
 
-def choose_kernel(even_ref, odd_ref, out_ref):
+def choose_kernel(at, even_ref, odd_ref, out_ref):
     odd = lax.rem(lax.axis_index("seq"), 2) == 1
+    cols = slice(at, at + out_ref.shape[1])
 
     @pl.when(odd)
     def _():
-        out_ref[...] = odd_ref[...]
+        out_ref[...] = odd_ref[:, cols]
 
     @pl.when(jnp.logical_not(odd))
     def _():
-        out_ref[...] = even_ref[...]
-
-
-def choose(even, odd):
+        out_ref[...] = even_ref[:, cols]
+
+
+def choose(even, odd, at=0, width=None):
+    shape = (even.shape[0], width or even.shape[1])
     return pl.pallas_call(
-        choose_kernel,
-        out_shape=pltpu.VMEM(even.shape, even.dtype),
+        functools.partial(choose_kernel, at),
+        out_shape=pltpu.VMEM(shape, even.dtype),
         in_specs=[VMEM, VMEM],
         out_specs=VMEM,
         compiler_params=SMALL,
     )(*held(even, odd))
 
 
-def lower_kernel(pair_ref, out_ref):
-    out_ref[...] = pair_ref[out_ref.shape[0] :, :]
-
-
-def lower(pair):
-    rows, width = pair.shape
+def lower_kernel(*refs):
+    out_ref = refs[-1]
+    rows = out_ref.shape[0]
+    width = out_ref.shape[1] // (len(refs) - 1)
+    for h, ref in enumerate(refs[:-1]):
+        out_ref[:, h * width : (h + 1) * width] = ref[rows:, :]
+
+
+def lower(*pairs):
+    rows, width = pairs[0].shape
     return pl.pallas_call(
         lower_kernel,
-        out_shape=pltpu.VMEM((rows // 2, width), pair.dtype),
-        in_specs=[VMEM],
+        out_shape=pltpu.VMEM((rows // 2, width * len(pairs)), pairs[0].dtype),
+        in_specs=[VMEM] * len(pairs),
         out_specs=VMEM,
         compiler_params=SMALL,
-    )(*held(pair))
+    )(*held(*pairs))
 
 
 def relay_kernel(near, *refs):
@@ -212,8 +223,8 @@
     dv_acc[...] = jnp.zeros(dv_acc.shape, jnp.float32)
 
     code = lax.broadcasted_iota(jnp.int32, (HEAD_WIDTH, T), 0).astype(jnp.float32)
-    at = 2 * h * HEAD_WIDTH
     for d, block in enumerate(block_refs):
+        at = 2 * h * HEAD_WIDTH if block.shape[1] > 2 * HEAD_WIDTH else 0
         row = block[T : T + 1, at : at + T].astype(jnp.float32)
         row = jnp.where(i >= d, row, float(DOCS))
         one_hot = jnp.where(code == row, 1.0, 0.0).astype(jnp.bfloat16)
@@ -221,7 +232,7 @@
         kx[rows, 0:HEAD_WIDTH] = block[0:T, at : at + HEAD_WIDTH]
         kx[rows, HEAD_WIDTH : 2 * HEAD_WIDTH] = one_hot.T
         vx[rows, :] = block[0:T, at + HEAD_WIDTH : at + 2 * HEAD_WIDTH]
-    own_row = own_ref[T : T + 1, at : at + T].astype(jnp.float32)
+    own_row = own_ref[T : T + 1, 0:T].astype(jnp.float32)
     away = jnp.where((code == own_row) | (code > DOCS), 0.0, NEG).astype(jnp.bfloat16).T
     half_rows = T // 2
     for unit in range(group):
@@ -305,7 +316,7 @@
         part = first_row // half_rows
         at_row = pl.multiple_of(first_row - part * half_rows, sub)
         for g in range(group):
-            at = h * W + g * HEAD_WIDTH
+            at = g * HEAD_WIDTH + (h * W if m < 2 or m % 2 else 0)
             rows = pl.ds(pl.multiple_of(g % 2 * half_rows + at_row, sub), sub)
             gs[g - g % 2 + part, rows, :] = grad_refs[m][0:sub, at : at + HEAD_WIDTH]
     step(1, 0, None, 1)
@@ -397,24 +408,32 @@
 
     evens = [lax.ppermute(block, "seq", two_up)]
     pairs = [
-        lax.ppermute(pair, "tp", [(a, a ^ (2 * m + 2)) for a in range(n_tp)])
+        lax.ppermute(pair, "tp", [(a, a ^ (2 * (m // heads) + 2)) for a in range(n_tp)])
         for m, pair in enumerate(across)
     ]
-    odds = [None]
+    width = 2 * HEAD_WIDTH
+    odds = [[None] for _ in range(heads)]
     for k in range(1, half):
-        odds.append(lax.ppermute(evens[-1], "seq", one_up))
+        step = choose(evens[-1], evens[-1], 0, width)
+        odds[0].append(lax.ppermute(step, "seq", one_up))
         evens.append(lax.ppermute(evens[-1], "seq", two_up))
-    odds[0] = lax.ppermute(choose(block, evens[0]), "seq", swap)
-    grads = [mine, lax.ppermute(beside, "tp", cores)]
-    for pair in pairs:
-        grads += [pair, lax.ppermute(lower(pair), "tp", cores)]
+        for h in range(1, heads):
+            step = choose(evens[-2], evens[-2], h * width, width)
+            odds[h].append(lax.ppermute(step, "seq", one_up))
+    near = lax.ppermute(choose(block, evens[0]), "seq", swap)
+    beside = lax.ppermute(beside, "tp", cores)
+    grads = [[mine, beside] for _ in range(heads)]
+    for m in range(0, len(pairs), heads):
+        rest = lax.ppermute(lower(*pairs[m : m + heads]), "tp", cores)
+        for h in range(heads):
+            grads[h] += [pairs[m + h], rest]
 
     dq = None
-    odds_in, evens_in = odds, evens
+    odds_in, evens_in = [[near, *x[1:]] for x in odds], evens
     leaving = []
     for h in range(heads):
         dq, odds, evens, own = head_call(
-            h, reach, group, n_tp, queries, grads, block, odds_in, evens_in, dq
+            h, reach, group, n_tp, queries, grads[h], block, odds_in[h], evens_in, dq
         )
         last = evens[-1]
         if leaving:

time: 64.1 us -> 62.2 us (0.970)
  waiting for transfers between devices: 27.7 us -> 22.4 us
  starting transfers between devices: 16 us -> 19 us
    ppermute x5 -> x7, waiting for transfers between devices: 11.9 us -> 9.21 us  [the longest x1 6.12 us: local(): odds[0].append(lax.ppermute(step, 'seq', one_up))]
    ppermute x2, starting transfers between devices: 0.36 us -> 2.28 us  [local(): moving = lax.ppermute(last, 'seq', two_down)]
    ppermute x1, waiting for transfers between devices: 8.4 us -> 6.65 us  [local(): evens = [lax.ppermute(block, 'seq', two_up)]]
    ppermute x1, waiting for transfers between devices: 1.68 us -> 0.01 us  [local(): evens.append(lax.ppermute(evens[-1], 'seq', two_up))]
    ppermute x2, starting transfers between devices: 4.24 us -> 2.72 us  [local(): moving = lax.ppermute(relay(k == 1, *parts), 'seq', two_down)]
    ppermute x1, starting transfers between devices: 1.58 us -> 3.08 us  [local(): evens = [lax.ppermute(block, 'seq', two_up)]]
    ppermute x5 -> x7, starting transfers between devices: 5.67 us -> 6.84 us  [the longest x2 2.03 us: local(): lax.ppermute(pair, 'tp', [(a, a ^ 2 * (m // heads) + 2) for a in range(n_...]
    ppermute x2, waiting for transfers between devices: 0.71 us -> 1.86 us  [local(): moving = lax.ppermute(last, 'seq', two_down)]
  transfers between devices with their start and end apart: 15 -> 17, of which waited for: 9 -> 8; matrix products, arithmetic and copies ran while one was open for 0% -> 0% of each run, Pallas kernels for 13% -> 28%
where the time goes in v2:
time: 62.2 us; the launch traced here: 61.9 us
  waiting for transfers between devices  22.4 us (36%)
  Pallas kernels  19.7 us (32%)
  starting transfers between devices  19 us (31%)
  between operations  0.74 us (1%)
    pallas_call x2, Pallas kernels, head_call(): pl.pallas_call(functools.partial(main_kernel, h, reach, group, n_tp, firs...  16.8 us
    ppermute x1, waiting for transfers between devices, local(): evens = [lax.ppermute(block, 'seq', two_up)]  6.65 us
    ppermute x1, waiting for transfers between devices, local(): odds[0].append(lax.ppermute(step, 'seq', one_up))  6.12 us
    ppermute x4, starting transfers between devices, local(): lax.ppermute(x, 'seq', one_down if k else swap)  4.05 us
    ppermute x2, waiting for transfers between devices, local(): moving = lax.ppermute(relay(k == 1, *parts), 'seq', two_down)  3.1 us
    ppermute x2, waiting for transfers between devices, local(): lax.ppermute(pair, 'tp', [(a, a ^ 2 * (m // heads) + 2) for a in range(n_...  3.08 us
    ppermute x1, starting transfers between devices, local(): evens = [lax.ppermute(block, 'seq', two_up)]  3.08 us
    ppermute x2, starting transfers between devices, local(): moving = lax.ppermute(relay(k == 1, *parts), 'seq', two_down)  2.72 us
  transfers between devices with their start and end apart: 17, of which 8 were waited for; matrix products, arithmetic and copies ran while one was open for 0% of the time, Pallas kernels for 28%

profile of v2, /device:TPU:0, one launch (start us, length us, event | category | flops | bytes accessed | tf_op | source)
XLA Modules:
  0.0 61.9 jit_solution(9090803686678483762)
XLA Ops:
  0.6 1.9 %shard_map.76 = (bf16[272,512]{1,0:T(8,128)(2,1)S(1)}, bf16[256,2048]{1,0:T(8,128)(2,1)S(1)}, bf16[64,2048]{1,0:T(8,128)(2,1)S(1)}, bf16[64,2048]{1,0:T(8,128)(2...) custom-call(bf16[256,256]{1,0:T(8,128)(2,1)} %key_ref.1, bf16[256,256]{1,0:T(8,128)(2,1)} %value_ref.1, ...), custom_call_target="tpu_custom_call" | custom-call | tf_op jit(solution)/shard_map/pallas_call | solution.py:76
  2.5 3.1 %collective-permute-start.4 = (bf16[272,512]{1,0:T(8,128)(2,1)S(1)}, bf16[272,512]{1,0:T(8,128)(2,1)S(1)}, u32[]{:S(2)}, u32[]{:S(2)}) collective-permute-start(bf16[272,512]{1,0:T(8,128)(2,1)S(1)} %get-tuple-element.32.even_ref.refs_5_), channel_id=1, source_target_pairs={{0,8},{4,12},{8,16},{12,20},{16,24},{20,28},{24,0},{28,4},{1,9},{5... | collective-permute-start | bytes 835592 | tf_op jit(solution)/shard_map/ppermute | solution.py:409
  5.6 1.5 %collective-permute-start.1 = (bf16[128,1024]{1,0:T(8,128)(2,1)S(1)}, bf16[128,1024]{1,0:T(8,128)(2,1)S(1)}, u32[]{:S(2)}, u32[]{:S(2)}) collective-permute-start(bf16[128,1024]{1,0:T(8,128)(2,1)S(1)} %get-tuple-element.30), channel_id=1, source_target_pairs={{0,2},{1,3},{2,0},{3,1},{4,6},{5,7},{6,4},{7,5},{8,10},{9,11},{10,... | collective-permute-start | bytes 786440 | tf_op jit(solution)/shard_map/ppermute | solution.py:411
  7.1 0.5 collective-permute-start.2
  7.6 6.7 %collective-permute-done.4.odd_ref.even_ref.refs_8_ = bf16[272,512]{1,0:T(8,128)(2,1)S(1)} collective-permute-done((bf16[272,512]{1,0:T(8,128)(2,1)S(1)}, bf16[272,512]{1,0:T(8,128)(2,1)S(1)}, u32[]{:S(2)}, u32[]{:S(2)}) %collective-permute-start.4) | collective-permute-done | bytes 278560 | tf_op jit(solution)/shard_map/ppermute | solution.py:409
  14.3 1.6 %collective-permute-start.5 = (bf16[272,512]{1,0:T(8,128)(2,1)S(1)}, bf16[272,512]{1,0:T(8,128)(2,1)S(1)}, u32[]{:S(2)}, u32[]{:S(2)}) collective-permute-start(bf16[272,512]{1,0:T(8,128)(2,1)S(1)} %shard_map.78), channel_id=1, source_target_pairs={{0,4},{4,0},{8,12},{12,8},{16,20},{20,16},{24,28},{28,24},{1,5},{5... | collective-permute-start | bytes 835592 | tf_op jit(solution)/shard_map/ppermute | solution.py:423
  15.9 3.1 %collective-permute-done.2.refs_0_.refs_3_ = bf16[128,1024]{1,0:T(8,128)(2,1)S(1)} collective-permute-done((bf16[128,1024]{1,0:T(8,128)(2,1)S(1)}, bf16[128,1024]{1,0:T(8,128)(2,1)S(1)}, u32[]{:S(2)}, u32[]{:S(2)}) %collective-permute-start.2) | collective-permute-done | bytes 262176 | tf_op jit(solution)/shard_map/ppermute | solution.py:411
  19.1 1.6 %collective-permute-start.8 = (bf16[272,256]{1,0:T(8,128)(2,1)S(1)}, bf16[272,256]{1,0:T(8,128)(2,1)S(1)}, u32[]{:S(2)}, u32[]{:S(2)}) collective-permute-start(bf16[272,256]{1,0:T(8,128)(2,1)S(1)} %shard_map.80), channel_id=1, source_target_pairs={{0,4},{4,8},{8,12},{12,16},{16,20},{20,24},{24,28},{28,0},{1,5},{5... | collective-permute-start | bytes 417800 | tf_op jit(solution)/shard_map/ppermute | solution.py:418
  20.7 1.6 %collective-permute-start.6 = (bf16[272,256]{1,0:T(8,128)(2,1)S(1)}, bf16[272,256]{1,0:T(8,128)(2,1)S(1)}, u32[]{:S(2)}, u32[]{:S(2)}) collective-permute-start(bf16[272,256]{1,0:T(8,128)(2,1)S(1)} %shard_map.79), channel_id=1, source_target_pairs={{0,4},{4,8},{8,12},{12,16},{16,20},{20,24},{24,28},{28,0},{1,5},{5... | collective-permute-start | bytes 417800 | tf_op jit(solution)/shard_map/ppermute | solution.py:422
  22.3 6.1 %collective-permute-done.8.refs_7_ = bf16[272,256]{1,0:T(8,128)(2,1)S(1)} collective-permute-done((bf16[272,256]{1,0:T(8,128)(2,1)S(1)}, bf16[272,256]{1,0:T(8,128)(2,1)S(1)}, u32[]{:S(2)}, u32[]{:S(2)}) %collective-permute-start.8) | collective-permute-done | bytes 139296 | tf_op jit(solution)/shard_map/ppermute | solution.py:418
  28.4 8.4 %shard_map.81 = (bf16[256,2048]{1,0:T(8,128)(2,1)}, bf16[256,256]{1,0:T(8,128)(2,1)S(1)}, bf16[256,256]{1,0:T(8,128)(2,1)S(1)}, bf16[256,256]{1,0:T(8,128)(2,1)S...) custom-call(bf16[256,2048]{1,0:T(8,128)(2,1)S(1)} %get-tuple-element.27.refs_0_, ...), custom_call_target="tpu_custom_call" | custom-call | flops 13421772800 | bytes 4194304 | tf_op jit(solution)/shard_map/pallas_call | solution.py:367
  36.8 0.6 collective-permute-start.9
  37.4 1.7 %collective-permute-start.10 = (bf16[256,256]{1,0:T(8,128)(2,1)S(1)}, bf16[256,256]{1,0:T(8,128)(2,1)S(1)}, u32[]{:S(2)}, u32[]{:S(2)}) collective-permute-start(bf16[256,256]{1,0:T(8,128)(2,1)S(1)} %get-tuple-element.39), channel_id=1, source_target_pairs={{4,0},{8,4},{12,8},{16,12},{20,16},{24,20},{28,24},{0,28},{5,1},{9... | collective-permute-start | bytes 393224 | tf_op jit(solution)/shard_map/ppermute | solution.py:444
  39.4 8.4 %shard_map.82 = (bf16[256,2048]{1,0:T(8,128)(2,1)}, bf16[256,256]{1,0:T(8,128)(2,1)S(1)}, bf16[256,256]{1,0:T(8,128)(2,1)S(1)}, bf16[256,256]{1,0:T(8,128)(2,1)S...) custom-call(bf16[256,2048]{1,0:T(8,128)(2,1)S(1)} %get-tuple-element.27.refs_0_, ...), custom_call_target="tpu_custom_call", output_to_operand_aliasing={{0}: (10, {})} | custom-call | flops 13421772800 | bytes 4194304 | tf_op jit(solution)/shard_map/pallas_call | solution.py:367
  47.9 1.7 %collective-permute-start.13 = (bf16[256,256]{1,0:T(8,128)(2,1)S(1)}, bf16[256,256]{1,0:T(8,128)(2,1)S(1)}, u32[]{:S(2)}, u32[]{:S(2)}) collective-permute-start(bf16[256,256]{1,0:T(8,128)(2,1)S(1)} %get-tuple-element.43), channel_id=1, source_target_pairs={{8,0},{12,4},{16,8},{20,12},{24,16},{28,20},{0,24},{4,28},{9,1},{1... | collective-permute-start | bytes 393224 | tf_op jit(solution)/shard_map/ppermute | solution.py:443
  50.0 1.6 %collective-permute-start.15 = (bf16[256,256]{1,0:T(8,128)(2,1)S(1)}, bf16[256,256]{1,0:T(8,128)(2,1)S(1)}, u32[]{:S(2)}, u32[]{:S(2)}) collective-permute-start(bf16[256,256]{1,0:T(8,128)(2,1)S(1)} %get-tuple-element.48), channel_id=1, source_target_pairs={{0,4},{4,0},{8,12},{12,8},{16,20},{20,16},{24,28},{28,24},{1,5},{5... | collective-permute-start | bytes 393224 | tf_op jit(solution)/shard_map/ppermute | solution.py:444
  51.7 0.8 %collective-permute-start.12 = (bf16[256,256]{1,0:T(8,128)(2,1)S(1)}, bf16[256,256]{1,0:T(8,128)(2,1)S(1)}, u32[]{:S(2)}, u32[]{:S(2)}) collective-permute-start(bf16[256,256]{1,0:T(8,128)(2,1)S(1)} %shard_map.83), channel_id=1, source_target_pairs={{8,0},{12,4},{16,8},{20,12},{24,16},{28,20},{0,24},{4,28},{9,1},{1... | collective-permute-start | bytes 393224 | tf_op jit(solution)/shard_map/ppermute | solution.py:453
  52.5 1.9 %collective-permute-done.13.refs_0_ = bf16[256,256]{1,0:T(8,128)(2,1)S(1)} collective-permute-done((bf16[256,256]{1,0:T(8,128)(2,1)S(1)}, bf16[256,256]{1,0:T(8,128)(2,1)S(1)}, u32[]{:S(2)}, u32[]{:S(2)}) %collective-permute-start.13) | collective-permute-done | bytes 131104 | tf_op jit(solution)/shard_map/ppermute | solution.py:443
  54.4 0.8 %collective-permute-done.14.refs_2_ = bf16[256,256]{1,0:T(8,128)(2,1)S(1)} collective-permute-done((bf16[256,256]{1,0:T(8,128)(2,1)S(1)}, bf16[256,256]{1,0:T(8,128)(2,1)S(1)}, u32[]{:S(2)}, u32[]{:S(2)}) %collective-permute-start.14) | collective-permute-done | bytes 131104 | tf_op jit(solution)/shard_map/ppermute | solution.py:444
  55.2 0.8 %collective-permute-done.15.refs_3_.refs_5_ = bf16[256,256]{1,0:T(8,128)(2,1)S(1)} collective-permute-done((bf16[256,256]{1,0:T(8,128)(2,1)S(1)}, bf16[256,256]{1,0:T(8,128)(2,1)S(1)}, u32[]{:S(2)}, u32[]{:S(2)}) %collective-permute-start.15) | collective-permute-done | bytes 131104 | tf_op jit(solution)/shard_map/ppermute | solution.py:444
  56.0 1.9 %collective-permute-start.16 = (bf16[256,256]{1,0:T(8,128)(2,1)S(1)}, bf16[256,256]{1,0:T(8,128)(2,1)S(1)}, u32[]{:S(2)}, u32[]{:S(2)}) collective-permute-start(bf16[256,256]{1,0:T(8,128)(2,1)S(1)} %shard_map.84), channel_id=1, source_target_pairs={{8,0},{12,4},{16,8},{20,12},{24,16},{28,20},{0,24},{4,28},{9,1},{1... | collective-permute-start | bytes 393224 | tf_op jit(solution)/shard_map/ppermute | solution.py:453
  58.0 1.0 %collective-permute-done.12.refs_1_ = bf16[256,256]{1,0:T(8,128)(2,1)S(1)} collective-permute-done((bf16[256,256]{1,0:T(8,128)(2,1)S(1)}, bf16[256,256]{1,0:T(8,128)(2,1)S(1)}, u32[]{:S(2)}, u32[]{:S(2)}) %collective-permute-start.12) | collective-permute-done | bytes 131104 | tf_op jit(solution)/shard_map/ppermute | solution.py:453
  59.0 2.1 %collective-permute-done.16.refs_4_ = bf16[256,256]{1,0:T(8,128)(2,1)S(1)} collective-permute-done((bf16[256,256]{1,0:T(8,128)(2,1)S(1)}, bf16[256,256]{1,0:T(8,128)(2,1)S(1)}, u32[]{:S(2)}, u32[]{:S(2)}) %collective-permute-start.16) | collective-permute-done | bytes 131104 | tf_op jit(solution)/shard_map/ppermute | solution.py:453
  61.1 0.8 %shard_map.85 = (bf16[256,256]{1,0:T(8,128)(2,1)}, bf16[256,256]{1,0:T(8,128)(2,1)}) custom-call(f32[256,256]{1,0:T(8,128)S(1)} %get-tuple-element.35.refs_0_, bf16[256,256]{1,0:T(8,128)(2,1)S(1)} %collective-permute-done.12.refs_1_, bf16[256,256]{1,0:T(8,128)(2,1)S(1)} %collective-permute-done.11.refs_3_.refs_2_, f32[256,256]{1,0:T(8,128)S(1)} %get-tuple-element.41.refs_3_, ...), custom_call_target="tpu_custom_call" | custom-call | tf_op jit(solution)/shard_map/pallas_call | solution.py:169
  (20 shorter events, 1.0 us)
Async XLA Ops:
  2.5 11.8 %collective-permute-start.4 = (bf16[272,512]{1,0:T(8,128)(2,1)S(1)}, bf16[272,512]{1,0:T(8,128)(2,1)S(1)}, u32[]{:S(2)}, u32[]{:S(2)}) collective-permute-start(bf16[272,512]{1,0:T(8,128)(2,1)S(1)} %get-tuple-element.32.even_ref.refs_5_), channel_id=1, source_target_pairs={{0,8},{4,12},{8,16},{12,20},{16,24},{20,28},{24,0},{28,4},{1,9},{5... | collective-permute-start | bytes 835592 | tf_op jit(solution)/shard_map/ppermute | solution.py:409
  5.6 10.3 %collective-permute-start.1 = (bf16[128,1024]{1,0:T(8,128)(2,1)S(1)}, bf16[128,1024]{1,0:T(8,128)(2,1)S(1)}, u32[]{:S(2)}, u32[]{:S(2)}) collective-permute-start(bf16[128,1024]{1,0:T(8,128)(2,1)S(1)} %get-tuple-element.30), channel_id=1, source_target_pairs={{0,2},{1,3},{2,0},{3,1},{4,6},{5,7},{6,4},{7,5},{8,10},{9,11},{10,... | collective-permute-start | bytes 786440 | tf_op jit(solution)/shard_map/ppermute | solution.py:411
  7.1 11.9 %collective-permute-start.2 = (bf16[128,1024]{1,0:T(8,128)(2,1)S(1)}, bf16[128,1024]{1,0:T(8,128)(2,1)S(1)}, u32[]{:S(2)}, u32[]{:S(2)}) collective-permute-start(bf16[128,1024]{1,0:T(8,128)(2,1)S(1)} %get-tuple-element.31), channel_id=1, source_target_pairs={{0,2},{1,3},{2,0},{3,1},{4,6},{5,7},{6,4},{7,5},{8,10},{9,11},{10,... | collective-permute-start | bytes 786440 | tf_op jit(solution)/shard_map/ppermute | solution.py:411
  14.3 14.1 %collective-permute-start.5 = (bf16[272,512]{1,0:T(8,128)(2,1)S(1)}, bf16[272,512]{1,0:T(8,128)(2,1)S(1)}, u32[]{:S(2)}, u32[]{:S(2)}) collective-permute-start(bf16[272,512]{1,0:T(8,128)(2,1)S(1)} %shard_map.78), channel_id=1, source_target_pairs={{0,4},{4,0},{8,12},{12,8},{16,20},{20,16},{24,28},{28,24},{1,5},{5... | collective-permute-start | bytes 835592 | tf_op jit(solution)/shard_map/ppermute | solution.py:423
  15.9 12.5 %collective-permute-start.7 = (bf16[272,512]{1,0:T(8,128)(2,1)S(1)}, bf16[272,512]{1,0:T(8,128)(2,1)S(1)}, u32[]{:S(2)}, u32[]{:S(2)}) collective-permute-start(bf16[272,512]{1,0:T(8,128)(2,1)S(1)} %collective-permute-done.4.odd_ref.even_ref.refs_8_), channel_id=1, source_target_pairs={{0,8},{4,12},{8,16},{12,20},{16,24},{20,28},{24,0},{28,4},{1,9},{5... | collective-permute-start | bytes 835592 | tf_op jit(solution)/shard_map/ppermute | solution.py:419
  15.9 4.8 %collective-permute-start = (bf16[64,2048]{1,0:T(8,128)(2,1)S(1)}, bf16[64,2048]{1,0:T(8,128)(2,1)S(1)}, u32[]{:S(2)}, u32[]{:S(2)}) collective-permute-start(bf16[64,2048]{1,0:T(8,128)(2,1)S(1)} %get-tuple-element.29), channel_id=1, source_target_pairs={{0,1},{1,0},{2,3},{3,2},{4,5},{5,4},{6,7},{7,6},{8,9},{9,8},{10,11... | collective-permute-start | bytes 786440 | tf_op jit(solution)/shard_map/ppermute | solution.py:424
  19.0 9.4 %collective-permute-start.3 = (bf16[64,2048]{1,0:T(8,128)(2,1)S(1)}, bf16[64,2048]{1,0:T(8,128)(2,1)S(1)}, u32[]{:S(2)}, u32[]{:S(2)}) collective-permute-start(bf16[64,2048]{1,0:T(8,128)(2,1)S(1)} %shard_map.77), channel_id=1, source_target_pairs={{0,1},{1,0},{2,3},{3,2},{4,5},{5,4},{6,7},{7,6},{8,9},{9,8},{10,11... | collective-permute-start | bytes 786440 | tf_op jit(solution)/shard_map/ppermute | solution.py:427
  19.1 9.3 %collective-permute-start.8 = (bf16[272,256]{1,0:T(8,128)(2,1)S(1)}, bf16[272,256]{1,0:T(8,128)(2,1)S(1)}, u32[]{:S(2)}, u32[]{:S(2)}) collective-permute-start(bf16[272,256]{1,0:T(8,128)(2,1)S(1)} %shard_map.80), channel_id=1, source_target_pairs={{0,4},{4,8},{8,12},{12,16},{16,20},{20,24},{24,28},{28,0},{1,5},{5... | collective-permute-start | bytes 417800 | tf_op jit(solution)/shard_map/ppermute | solution.py:418
  20.7 18.7 %collective-permute-start.6 = (bf16[272,256]{1,0:T(8,128)(2,1)S(1)}, bf16[272,256]{1,0:T(8,128)(2,1)S(1)}, u32[]{:S(2)}, u32[]{:S(2)}) collective-permute-start(bf16[272,256]{1,0:T(8,128)(2,1)S(1)} %shard_map.79), channel_id=1, source_target_pairs={{0,4},{4,8},{8,12},{12,16},{16,20},{20,24},{24,28},{28,0},{1,5},{5... | collective-permute-start | bytes 417800 | tf_op jit(solution)/shard_map/ppermute | solution.py:422
  36.8 11.0 %collective-permute-start.9 = (bf16[256,256]{1,0:T(8,128)(2,1)S(1)}, bf16[256,256]{1,0:T(8,128)(2,1)S(1)}, u32[]{:S(2)}, u32[]{:S(2)}) collective-permute-start(bf16[256,256]{1,0:T(8,128)(2,1)S(1)} %get-tuple-element.36), channel_id=1, source_target_pairs={{8,0},{12,4},{16,8},{20,12},{24,16},{28,20},{0,24},{4,28},{9,1},{1... | collective-permute-start | bytes 393224 | tf_op jit(solution)/shard_map/ppermute | solution.py:443
  37.4 10.5 %collective-permute-start.10 = (bf16[256,256]{1,0:T(8,128)(2,1)S(1)}, bf16[256,256]{1,0:T(8,128)(2,1)S(1)}, u32[]{:S(2)}, u32[]{:S(2)}) collective-permute-start(bf16[256,256]{1,0:T(8,128)(2,1)S(1)} %get-tuple-element.39), channel_id=1, source_target_pairs={{4,0},{8,4},{12,8},{16,12},{20,16},{24,20},{28,24},{0,28},{5,1},{9... | collective-permute-start | bytes 393224 | tf_op jit(solution)/shard_map/ppermute | solution.py:444
  39.1 8.8 %collective-permute-start.11 = (bf16[256,256]{1,0:T(8,128)(2,1)S(1)}, bf16[256,256]{1,0:T(8,128)(2,1)S(1)}, u32[]{:S(2)}, u32[]{:S(2)}) collective-permute-start(bf16[256,256]{1,0:T(8,128)(2,1)S(1)} %get-tuple-element.40), channel_id=1, source_target_pairs={{0,4},{4,0},{8,12},{12,8},{16,20},{20,16},{24,28},{28,24},{1,5},{5... | collective-permute-start | bytes 393224 | tf_op jit(solution)/shard_map/ppermute | solution.py:444
  47.9 6.5 %collective-permute-start.13 = (bf16[256,256]{1,0:T(8,128)(2,1)S(1)}, bf16[256,256]{1,0:T(8,128)(2,1)S(1)}, u32[]{:S(2)}, u32[]{:S(2)}) collective-permute-start(bf16[256,256]{1,0:T(8,128)(2,1)S(1)} %get-tuple-element.43), channel_id=1, source_target_pairs={{8,0},{12,4},{16,8},{20,12},{24,16},{28,20},{0,24},{4,28},{9,1},{1... | collective-permute-start | bytes 393224 | tf_op jit(solution)/shard_map/ppermute | solution.py:443
  49.6 5.6 %collective-permute-start.14 = (bf16[256,256]{1,0:T(8,128)(2,1)S(1)}, bf16[256,256]{1,0:T(8,128)(2,1)S(1)}, u32[]{:S(2)}, u32[]{:S(2)}) collective-permute-start(bf16[256,256]{1,0:T(8,128)(2,1)S(1)} %get-tuple-element.46), channel_id=1, source_target_pairs={{4,0},{8,4},{12,8},{16,12},{20,16},{24,20},{28,24},{0,28},{5,1},{9... | collective-permute-start | bytes 393224 | tf_op jit(solution)/shard_map/ppermute | solution.py:444
  50.0 6.0 %collective-permute-start.15 = (bf16[256,256]{1,0:T(8,128)(2,1)S(1)}, bf16[256,256]{1,0:T(8,128)(2,1)S(1)}, u32[]{:S(2)}, u32[]{:S(2)}) collective-permute-start(bf16[256,256]{1,0:T(8,128)(2,1)S(1)} %get-tuple-element.48), channel_id=1, source_target_pairs={{0,4},{4,0},{8,12},{12,8},{16,20},{20,16},{24,28},{28,24},{1,5},{5... | collective-permute-start | bytes 393224 | tf_op jit(solution)/shard_map/ppermute | solution.py:444
  51.7 7.3 %collective-permute-start.12 = (bf16[256,256]{1,0:T(8,128)(2,1)S(1)}, bf16[256,256]{1,0:T(8,128)(2,1)S(1)}, u32[]{:S(2)}, u32[]{:S(2)}) collective-permute-start(bf16[256,256]{1,0:T(8,128)(2,1)S(1)} %shard_map.83), channel_id=1, source_target_pairs={{8,0},{12,4},{16,8},{20,12},{24,16},{28,20},{0,24},{4,28},{9,1},{1... | collective-permute-start | bytes 393224 | tf_op jit(solution)/shard_map/ppermute | solution.py:453
  56.0 5.0 %collective-permute-start.16 = (bf16[256,256]{1,0:T(8,128)(2,1)S(1)}, bf16[256,256]{1,0:T(8,128)(2,1)S(1)}, u32[]{:S(2)}, u32[]{:S(2)}) collective-permute-start(bf16[256,256]{1,0:T(8,128)(2,1)S(1)} %shard_map.84), channel_id=1, source_target_pairs={{8,0},{12,4},{16,8},{20,12},{24,16},{28,20},{0,24},{4,28},{9,1},{1... | collective-permute-start | bytes 393224 | tf_op jit(solution)/shard_map/ppermute | solution.py:453

commit v3 on v2

--- a/solution.py
+++ b/solution.py
@@ -400,13 +400,20 @@
     )
 
     swap = [(a, a ^ 1) for a in range(n)]
-    one_up = [(a, (a + 1) % n) for a in range(n)]
-    two_up = [(a, (a + 2) % n) for a in range(n)]
-    one_down = [(b, a) for a, b in one_up]
-    two_down = [(b, a) for a, b in two_up]
+
+    def up(step, low):
+        if step == 2:
+            return [(a, (a + step) % n) for a in range(n)]
+        moved = [(a, a + step) for a in range(low, n - step)]
+        unused = [(a, a ^ 1) for a in range(low)]
+        return moved + unused + [(n - step + a, low + a) for a in range(step)]
+
+    def down(step, low):
+        return [((a + step) % n, a) for a in range(n)]
+
     cores = [(a, a ^ 1) for a in range(n_tp)]
 
-    evens = [lax.ppermute(block, "seq", two_up)]
+    evens = [lax.ppermute(block, "seq", up(2, 0))]
     pairs = [
         lax.ppermute(pair, "tp", [(a, a ^ (2 * (m // heads) + 2)) for a in range(n_tp)])
         for m, pair in enumerate(across)
@@ -415,16 +422,17 @@
     odds = [[None] for _ in range(heads)]
     for k in range(1, half):
         step = choose(evens[-1], evens[-1], 0, width)
-        odds[0].append(lax.ppermute(step, "seq", one_up))
-        evens.append(lax.ppermute(evens[-1], "seq", two_up))
+        odds[0].append(lax.ppermute(step, "seq", up(1, 2 * k)))
+        evens.append(lax.ppermute(evens[-1], "seq", up(2, 2 * k)))
         for h in range(1, heads):
             step = choose(evens[-2], evens[-2], h * width, width)
-            odds[h].append(lax.ppermute(step, "seq", one_up))
+            odds[h].append(lax.ppermute(step, "seq", up(1, 2 * k)))
     near = lax.ppermute(choose(block, evens[0]), "seq", swap)
-    beside = lax.ppermute(beside, "tp", cores)
+    beside = lax.ppermute(after(beside, *odds[0][1:]), "tp", cores)
     grads = [[mine, beside] for _ in range(heads)]
     for m in range(0, len(pairs), heads):
-        rest = lax.ppermute(lower(*pairs[m : m + heads]), "tp", cores)
+        rest = after(lower(*pairs[m : m + heads]), *odds[0][1:])
+        rest = lax.ppermute(rest, "tp", cores)
         for h in range(heads):
             grads[h] += [pairs[m + h], rest]
 
@@ -440,8 +448,10 @@
             moved = [*leaving[-1][0], leaving[-1][2]]
             odds = [after(x, *moved) for x in odds]
             last = after(last, *moved)
-        moving = lax.ppermute(last, "seq", two_down)
-        odds = [lax.ppermute(x, "seq", one_down if k else swap) for k, x in enumerate(odds)]
+        moving = lax.ppermute(last, "seq", down(2, 2 * half - 2))
+        odds = [
+            lax.ppermute(x, "seq", down(1, 2 * k) if k else swap) for k, x in enumerate(odds)
+        ]
         leaving.append((odds, evens, moving, own))
     ends = []
     for h in range(heads):
@@ -450,7 +460,7 @@
             if h < heads - 1:
                 moving = after(moving, dq)
             parts = [moving, evens[k - 1], odds[k]] + ([odds[0]] if k == 1 else [])
-            moving = lax.ppermute(relay(k == 1, *parts), "seq", two_down)
+            moving = lax.ppermute(relay(k == 1, *parts), "seq", down(2, 2 * k - 2))
         ends += [own, moving, odds[0]]
     return (dq, *finish(*ends))
 

time: 62.2 us -> 61.6 us (level)
  waiting for transfers between devices: 22.4 us -> 21.2 us
  starting transfers between devices: 19 us -> 19.8 us
    ppermute x1, waiting for transfers between devices: 0.01 us -> 3.08 us  [local(): near = lax.ppermute(choose(block, evens[0]), 'seq', swap)]
    ppermute x14, waiting for transfers between devices: 19.4 us -> 16.4 us  [the longest x1 6.65 us: local(): evens = [lax.ppermute(block, 'seq', up(2, 0))]]
    ppermute x14, starting transfers between devices: 15.4 us -> 17.2 us  [the longest x4 5.65 us: local(): lax.ppermute(x, 'seq', down(1, 2 * k) if k else swap)]
    ppermute x2, waiting for transfers between devices: 3.08 us -> 1.79 us  [local(): lax.ppermute(pair, 'tp', [(a, a ^ 2 * (m // heads) + 2) for a in range(n_...]
    ppermute x1, starting transfers between devices: 1.59 us -> 0.59 us  [local(): near = lax.ppermute(choose(block, evens[0]), 'seq', swap)]
  transfers between devices with their start and end apart: 17 -> 17, of which waited for: 8 -> 9; matrix products, arithmetic and copies ran while one was open for 0% -> 0% of each run, Pallas kernels for 28% -> 28%
where the time goes in v3:
time: 61.6 us; the launch traced here: 61.4 us
  waiting for transfers between devices  21.2 us (34%)
  starting transfers between devices  19.8 us (32%)
  Pallas kernels  19.7 us (32%)
  between operations  0.72 us (1%)
    pallas_call x2, Pallas kernels, head_call(): pl.pallas_call(functools.partial(main_kernel, h, reach, group, n_tp, firs...  16.8 us
    ppermute x1, waiting for transfers between devices, local(): evens = [lax.ppermute(block, 'seq', up(2, 0))]  6.65 us
    ppermute x4, starting transfers between devices, local(): lax.ppermute(x, 'seq', down(1, 2 * k) if k else swap)  5.65 us
    ppermute x2, waiting for transfers between devices, local(): moving = lax.ppermute(relay(k == 1, *parts), 'seq', down(2, 2 * k - 2))  3.93 us
    ppermute x1, waiting for transfers between devices, local(): near = lax.ppermute(choose(block, evens[0]), 'seq', swap)  3.08 us
    ppermute x1, starting transfers between devices, local(): evens = [lax.ppermute(block, 'seq', up(2, 0))]  3.08 us
    ppermute x4, waiting for transfers between devices, local(): lax.ppermute(x, 'seq', down(1, 2 * k) if k else swap)  2.6 us
    ppermute x2, starting transfers between devices, local(): moving = lax.ppermute(relay(k == 1, *parts), 'seq', down(2, 2 * k - 2))  2.17 us
  transfers between devices with their start and end apart: 17, of which 9 were waited for; matrix products, arithmetic and copies ran while one was open for 0% of the time, Pallas kernels for 28%

profile of v3, /device:TPU:0, one launch (start us, length us, event | category | flops | bytes accessed | tf_op | source)
XLA Modules:
  0.0 61.4 jit_solution(7384843892667281707)
XLA Ops:
  0.6 1.9 %shard_map.76 = (bf16[272,512]{1,0:T(8,128)(2,1)S(1)}, bf16[256,2048]{1,0:T(8,128)(2,1)S(1)}, bf16[64,2048]{1,0:T(8,128)(2,1)S(1)}, bf16[64,2048]{1,0:T(8,128)(2...) custom-call(bf16[256,256]{1,0:T(8,128)(2,1)} %key_ref.1, bf16[256,256]{1,0:T(8,128)(2,1)} %value_ref.1, ...), custom_call_target="tpu_custom_call" | custom-call | tf_op jit(solution)/shard_map/pallas_call | solution.py:76
  2.5 3.1 %collective-permute-start = (bf16[272,512]{1,0:T(8,128)(2,1)S(1)}, bf16[272,512]{1,0:T(8,128)(2,1)S(1)}, u32[]{:S(2)}, u32[]{:S(2)}) collective-permute-start(bf16[272,512]{1,0:T(8,128)(2,1)S(1)} %get-tuple-element.32.even_ref.refs_5_), channel_id=1, source_target_pairs={{0,8},{4,12},{8,16},{12,20},{16,24},{20,28},{24,0},{28,4},{1,9},{5... | collective-permute-start | bytes 835592 | tf_op jit(solution)/shard_map/ppermute | solution.py:416
  5.6 1.5 %collective-permute-start.3 = (bf16[128,1024]{1,0:T(8,128)(2,1)S(1)}, bf16[128,1024]{1,0:T(8,128)(2,1)S(1)}, u32[]{:S(2)}, u32[]{:S(2)}) collective-permute-start(bf16[128,1024]{1,0:T(8,128)(2,1)S(1)} %get-tuple-element.34), channel_id=1, source_target_pairs={{0,2},{1,3},{2,0},{3,1},{4,6},{5,7},{6,4},{7,5},{8,10},{9,11},{10,... | collective-permute-start | bytes 786440 | tf_op jit(solution)/shard_map/ppermute | solution.py:418
  7.6 6.7 %collective-permute-done.even_ref.odd_ref.refs_8_ = bf16[272,512]{1,0:T(8,128)(2,1)S(1)} collective-permute-done((bf16[272,512]{1,0:T(8,128)(2,1)S(1)}, bf16[272,512]{1,0:T(8,128)(2,1)S(1)}, u32[]{:S(2)}, u32[]{:S(2)}) %collective-permute-start) | collective-permute-done | bytes 278560 | tf_op jit(solution)/shard_map/ppermute | solution.py:416
  14.3 1.6 %collective-permute-start.1 = (bf16[272,256]{1,0:T(8,128)(2,1)S(1)}, bf16[272,256]{1,0:T(8,128)(2,1)S(1)}, u32[]{:S(2)}, u32[]{:S(2)}) collective-permute-start(bf16[272,256]{1,0:T(8,128)(2,1)S(1)} %shard_map.77), channel_id=1, source_target_pairs={{8,12},{12,16},{16,20},{20,24},{24,28},{0,4},{4,0},{28,8},{9,13},{... | collective-permute-start | bytes 417800 | tf_op jit(solution)/shard_map/ppermute | solution.py:425
  16.5 0.7 %collective-permute-start.8 = (bf16[272,512]{1,0:T(8,128)(2,1)S(1)}, bf16[272,512]{1,0:T(8,128)(2,1)S(1)}, u32[]{:S(2)}, u32[]{:S(2)}) collective-permute-start(bf16[272,512]{1,0:T(8,128)(2,1)S(1)} %collective-permute-done.even_ref.odd_ref.refs_8_), channel_id=1, source_target_pairs={{0,8},{4,12},{8,16},{12,20},{16,24},{20,28},{24,0},{28,4},{1,9},{5... | collective-permute-start | bytes 835592 | tf_op jit(solution)/shard_map/ppermute | solution.py:426
  17.2 1.8 %collective-permute-done.4.refs_0_.refs_3_ = bf16[128,1024]{1,0:T(8,128)(2,1)S(1)} collective-permute-done((bf16[128,1024]{1,0:T(8,128)(2,1)S(1)}, bf16[128,1024]{1,0:T(8,128)(2,1)S(1)}, u32[]{:S(2)}, u32[]{:S(2)}) %collective-permute-start.4) | collective-permute-done | bytes 262176 | tf_op jit(solution)/shard_map/ppermute | solution.py:418
  19.0 2.0 %collective-permute-done.1.refs_7_ = bf16[272,256]{1,0:T(8,128)(2,1)S(1)} collective-permute-done((bf16[272,256]{1,0:T(8,128)(2,1)S(1)}, bf16[272,256]{1,0:T(8,128)(2,1)S(1)}, u32[]{:S(2)}, u32[]{:S(2)}) %collective-permute-start.1) | collective-permute-done | bytes 139296 | tf_op jit(solution)/shard_map/ppermute | solution.py:425
  21.5 1.6 %collective-permute-start.7 = (bf16[272,256]{1,0:T(8,128)(2,1)S(1)}, bf16[272,256]{1,0:T(8,128)(2,1)S(1)}, u32[]{:S(2)}, u32[]{:S(2)}) collective-permute-start(bf16[272,256]{1,0:T(8,128)(2,1)S(1)} %shard_map.80), channel_id=1, source_target_pairs={{8,12},{12,16},{16,20},{20,24},{24,28},{0,4},{4,0},{28,8},{9,13},{... | collective-permute-start | bytes 417800 | tf_op jit(solution)/shard_map/ppermute | solution.py:429
  23.0 3.1 %collective-permute-done.6.refs_6_ = bf16[272,512]{1,0:T(8,128)(2,1)S(1)} collective-permute-done((bf16[272,512]{1,0:T(8,128)(2,1)S(1)}, bf16[272,512]{1,0:T(8,128)(2,1)S(1)}, u32[]{:S(2)}, u32[]{:S(2)}) %collective-permute-start.6) | collective-permute-done | bytes 278560 | tf_op jit(solution)/shard_map/ppermute | solution.py:430
  26.1 8.4 %shard_map.81 = (bf16[256,2048]{1,0:T(8,128)(2,1)}, bf16[256,256]{1,0:T(8,128)(2,1)S(1)}, bf16[256,256]{1,0:T(8,128)(2,1)S(1)}, bf16[256,256]{1,0:T(8,128)(2,1)S...) custom-call(bf16[256,2048]{1,0:T(8,128)(2,1)S(1)} %get-tuple-element.29.refs_0_, ...), custom_call_target="tpu_custom_call" | custom-call | flops 13421772800 | bytes 4194304 | tf_op jit(solution)/shard_map/pallas_call | solution.py:367
  34.5 1.4 %collective-permute-start.9 = (bf16[256,256]{1,0:T(8,128)(2,1)S(1)}, bf16[256,256]{1,0:T(8,128)(2,1)S(1)}, u32[]{:S(2)}, u32[]{:S(2)}) collective-permute-start(bf16[256,256]{1,0:T(8,128)(2,1)S(1)} %get-tuple-element.40), channel_id=1, source_target_pairs={{8,0},{12,4},{16,8},{20,12},{24,16},{28,20},{0,24},{4,28},{9,1},{1... | collective-permute-start | bytes 393224 | tf_op jit(solution)/shard_map/ppermute | solution.py:451
  36.0 1.1 %collective-permute-start.10 = (bf16[256,256]{1,0:T(8,128)(2,1)S(1)}, bf16[256,256]{1,0:T(8,128)(2,1)S(1)}, u32[]{:S(2)}, u32[]{:S(2)}) collective-permute-start(bf16[256,256]{1,0:T(8,128)(2,1)S(1)} %get-tuple-element.43), channel_id=1, source_target_pairs={{4,0},{8,4},{12,8},{16,12},{20,16},{24,20},{28,24},{0,28},{5,1},{9... | collective-permute-start | bytes 393224 | tf_op jit(solution)/shard_map/ppermute | solution.py:453
  37.1 0.9 %collective-permute-start.11 = (bf16[256,256]{1,0:T(8,128)(2,1)S(1)}, bf16[256,256]{1,0:T(8,128)(2,1)S(1)}, u32[]{:S(2)}, u32[]{:S(2)}) collective-permute-start(bf16[256,256]{1,0:T(8,128)(2,1)S(1)} %get-tuple-element.44), channel_id=1, source_target_pairs={{0,4},{4,0},{8,12},{12,8},{16,20},{20,16},{24,28},{28,24},{1,5},{5... | collective-permute-start | bytes 393224 | tf_op jit(solution)/shard_map/ppermute | solution.py:453
  38.0 8.4 %shard_map.82 = (bf16[256,2048]{1,0:T(8,128)(2,1)}, bf16[256,256]{1,0:T(8,128)(2,1)S(1)}, bf16[256,256]{1,0:T(8,128)(2,1)S(1)}, bf16[256,256]{1,0:T(8,128)(2,1)S...) custom-call(bf16[256,2048]{1,0:T(8,128)(2,1)S(1)} %get-tuple-element.29.refs_0_, ...), custom_call_target="tpu_custom_call", output_to_operand_aliasing={{0}: (10, {})} | custom-call | flops 13421772800 | bytes 4194304 | tf_op jit(solution)/shard_map/pallas_call | solution.py:367
  46.9 3.6 %collective-permute-start.14 = (bf16[256,256]{1,0:T(8,128)(2,1)S(1)}, bf16[256,256]{1,0:T(8,128)(2,1)S(1)}, u32[]{:S(2)}, u32[]{:S(2)}) collective-permute-start(bf16[256,256]{1,0:T(8,128)(2,1)S(1)} %get-tuple-element.50), channel_id=1, source_target_pairs={{4,0},{8,4},{12,8},{16,12},{20,16},{24,20},{28,24},{0,28},{5,1},{9... | collective-permute-start | bytes 393224 | tf_op jit(solution)/shard_map/ppermute | solution.py:453
  50.6 1.1 %collective-permute-start.12 = (bf16[256,256]{1,0:T(8,128)(2,1)S(1)}, bf16[256,256]{1,0:T(8,128)(2,1)S(1)}, u32[]{:S(2)}, u32[]{:S(2)}) collective-permute-start(bf16[256,256]{1,0:T(8,128)(2,1)S(1)} %shard_map.83), channel_id=1, source_target_pairs={{8,0},{12,4},{16,8},{20,12},{24,16},{28,20},{0,24},{4,28},{9,1},{1... | collective-permute-start | bytes 393224 | tf_op jit(solution)/shard_map/ppermute | solution.py:463
  51.7 1.2 %collective-permute-done.13.refs_0_ = bf16[256,256]{1,0:T(8,128)(2,1)S(1)} collective-permute-done((bf16[256,256]{1,0:T(8,128)(2,1)S(1)}, bf16[256,256]{1,0:T(8,128)(2,1)S(1)}, u32[]{:S(2)}, u32[]{:S(2)}) %collective-permute-start.13) | collective-permute-done | bytes 131104 | tf_op jit(solution)/shard_map/ppermute | solution.py:451
  52.9 1.2 %collective-permute-done.14.refs_2_ = bf16[256,256]{1,0:T(8,128)(2,1)S(1)} collective-permute-done((bf16[256,256]{1,0:T(8,128)(2,1)S(1)}, bf16[256,256]{1,0:T(8,128)(2,1)S(1)}, u32[]{:S(2)}, u32[]{:S(2)}) %collective-permute-start.14) | collective-permute-done | bytes 131104 | tf_op jit(solution)/shard_map/ppermute | solution.py:453
  54.1 1.4 %collective-permute-done.15.refs_3_.refs_5_ = bf16[256,256]{1,0:T(8,128)(2,1)S(1)} collective-permute-done((bf16[256,256]{1,0:T(8,128)(2,1)S(1)}, bf16[256,256]{1,0:T(8,128)(2,1)S(1)}, u32[]{:S(2)}, u32[]{:S(2)}) %collective-permute-start.15) | collective-permute-done | bytes 131104 | tf_op jit(solution)/shard_map/ppermute | solution.py:453
  55.6 1.1 %collective-permute-start.16 = (bf16[256,256]{1,0:T(8,128)(2,1)S(1)}, bf16[256,256]{1,0:T(8,128)(2,1)S(1)}, u32[]{:S(2)}, u32[]{:S(2)}) collective-permute-start(bf16[256,256]{1,0:T(8,128)(2,1)S(1)} %shard_map.84), channel_id=1, source_target_pairs={{8,0},{12,4},{16,8},{20,12},{24,16},{28,20},{0,24},{4,28},{9,1},{1... | collective-permute-start | bytes 393224 | tf_op jit(solution)/shard_map/ppermute | solution.py:463
  56.7 0.6 %collective-permute-done.12.refs_1_ = bf16[256,256]{1,0:T(8,128)(2,1)S(1)} collective-permute-done((bf16[256,256]{1,0:T(8,128)(2,1)S(1)}, bf16[256,256]{1,0:T(8,128)(2,1)S(1)}, u32[]{:S(2)}, u32[]{:S(2)}) %collective-permute-start.12) | collective-permute-done | bytes 131104 | tf_op jit(solution)/shard_map/ppermute | solution.py:463
  57.3 3.3 %collective-permute-done.16.refs_4_ = bf16[256,256]{1,0:T(8,128)(2,1)S(1)} collective-permute-done((bf16[256,256]{1,0:T(8,128)(2,1)S(1)}, bf16[256,256]{1,0:T(8,128)(2,1)S(1)}, u32[]{:S(2)}, u32[]{:S(2)}) %collective-permute-start.16) | collective-permute-done | bytes 131104 | tf_op jit(solution)/shard_map/ppermute | solution.py:463
  60.6 0.8 %shard_map.85 = (bf16[256,256]{1,0:T(8,128)(2,1)}, bf16[256,256]{1,0:T(8,128)(2,1)}) custom-call(f32[256,256]{1,0:T(8,128)S(1)} %get-tuple-element.39.refs_0_, bf16[256,256]{1,0:T(8,128)(2,1)S(1)} %collective-permute-done.12.refs_1_, bf16[256,256]{1,0:T(8,128)(2,1)S(1)} %collective-permute-done.11.refs_3_.refs_2_, f32[256,256]{1,0:T(8,128)S(1)} %get-tuple-element.45.refs_3_, ...), custom_call_target="tpu_custom_call" | custom-call | tf_op jit(solution)/shard_map/pallas_call | solution.py:169
  (20 shorter events, 2.4 us)
Async XLA Ops:
  2.5 11.8 %collective-permute-start = (bf16[272,512]{1,0:T(8,128)(2,1)S(1)}, bf16[272,512]{1,0:T(8,128)(2,1)S(1)}, u32[]{:S(2)}, u32[]{:S(2)}) collective-permute-start(bf16[272,512]{1,0:T(8,128)(2,1)S(1)} %get-tuple-element.32.even_ref.refs_5_), channel_id=1, source_target_pairs={{0,8},{4,12},{8,16},{12,20},{16,24},{20,28},{24,0},{28,4},{1,9},{5... | collective-permute-start | bytes 835592 | tf_op jit(solution)/shard_map/ppermute | solution.py:416
  5.6 11.6 %collective-permute-start.3 = (bf16[128,1024]{1,0:T(8,128)(2,1)S(1)}, bf16[128,1024]{1,0:T(8,128)(2,1)S(1)}, u32[]{:S(2)}, u32[]{:S(2)}) collective-permute-start(bf16[128,1024]{1,0:T(8,128)(2,1)S(1)} %get-tuple-element.34), channel_id=1, source_target_pairs={{0,2},{1,3},{2,0},{3,1},{4,6},{5,7},{6,4},{7,5},{8,10},{9,11},{10,... | collective-permute-start | bytes 786440 | tf_op jit(solution)/shard_map/ppermute | solution.py:418
  7.1 11.9 %collective-permute-start.4 = (bf16[128,1024]{1,0:T(8,128)(2,1)S(1)}, bf16[128,1024]{1,0:T(8,128)(2,1)S(1)}, u32[]{:S(2)}, u32[]{:S(2)}) collective-permute-start(bf16[128,1024]{1,0:T(8,128)(2,1)S(1)} %get-tuple-element.35), channel_id=1, source_target_pairs={{0,2},{1,3},{2,0},{3,1},{4,6},{5,7},{6,4},{7,5},{8,10},{9,11},{10,... | collective-permute-start | bytes 786440 | tf_op jit(solution)/shard_map/ppermute | solution.py:418
  14.3 6.7 %collective-permute-start.1 = (bf16[272,256]{1,0:T(8,128)(2,1)S(1)}, bf16[272,256]{1,0:T(8,128)(2,1)S(1)}, u32[]{:S(2)}, u32[]{:S(2)}) collective-permute-start(bf16[272,256]{1,0:T(8,128)(2,1)S(1)} %shard_map.77), channel_id=1, source_target_pairs={{8,12},{12,16},{16,20},{20,24},{24,28},{0,4},{4,0},{28,8},{9,13},{... | collective-permute-start | bytes 417800 | tf_op jit(solution)/shard_map/ppermute | solution.py:425
  15.9 10.2 %collective-permute-start.6 = (bf16[272,512]{1,0:T(8,128)(2,1)S(1)}, bf16[272,512]{1,0:T(8,128)(2,1)S(1)}, u32[]{:S(2)}, u32[]{:S(2)}) collective-permute-start(bf16[272,512]{1,0:T(8,128)(2,1)S(1)} %shard_map.79), channel_id=1, source_target_pairs={{0,4},{4,0},{8,12},{12,8},{16,20},{20,16},{24,28},{28,24},{1,5},{5... | collective-permute-start | bytes 835592 | tf_op jit(solution)/shard_map/ppermute | solution.py:430
  16.5 9.7 %collective-permute-start.8 = (bf16[272,512]{1,0:T(8,128)(2,1)S(1)}, bf16[272,512]{1,0:T(8,128)(2,1)S(1)}, u32[]{:S(2)}, u32[]{:S(2)}) collective-permute-start(bf16[272,512]{1,0:T(8,128)(2,1)S(1)} %collective-permute-done.even_ref.odd_ref.refs_8_), channel_id=1, source_target_pairs={{0,8},{4,12},{8,16},{12,20},{16,24},{20,28},{24,0},{28,4},{1,9},{5... | collective-permute-start | bytes 835592 | tf_op jit(solution)/shard_map/ppermute | solution.py:426
  20.9 5.2 %collective-permute-start.2 = (bf16[64,2048]{1,0:T(8,128)(2,1)S(1)}, bf16[64,2048]{1,0:T(8,128)(2,1)S(1)}, u32[]{:S(2)}, u32[]{:S(2)}) collective-permute-start(bf16[64,2048]{1,0:T(8,128)(2,1)S(1)} %get-tuple-element.33), channel_id=1, source_target_pairs={{0,1},{1,0},{2,3},{3,2},{4,5},{5,4},{6,7},{7,6},{8,9},{9,8},{10,11... | collective-permute-start | bytes 786440 | tf_op jit(solution)/shard_map/ppermute | solution.py:431
  21.0 5.2 %collective-permute-start.5 = (bf16[64,2048]{1,0:T(8,128)(2,1)S(1)}, bf16[64,2048]{1,0:T(8,128)(2,1)S(1)}, u32[]{:S(2)}, u32[]{:S(2)}) collective-permute-start(bf16[64,2048]{1,0:T(8,128)(2,1)S(1)} %shard_map.78), channel_id=1, source_target_pairs={{0,1},{1,0},{2,3},{3,2},{4,5},{5,4},{6,7},{7,6},{8,9},{9,8},{10,11... | collective-permute-start | bytes 786440 | tf_op jit(solution)/shard_map/ppermute | solution.py:435
  21.5 16.5 %collective-permute-start.7 = (bf16[272,256]{1,0:T(8,128)(2,1)S(1)}, bf16[272,256]{1,0:T(8,128)(2,1)S(1)}, u32[]{:S(2)}, u32[]{:S(2)}) collective-permute-start(bf16[272,256]{1,0:T(8,128)(2,1)S(1)} %shard_map.80), channel_id=1, source_target_pairs={{8,12},{12,16},{16,20},{20,24},{24,28},{0,4},{4,0},{28,8},{9,13},{... | collective-permute-start | bytes 417800 | tf_op jit(solution)/shard_map/ppermute | solution.py:429
  34.5 11.9 %collective-permute-start.9 = (bf16[256,256]{1,0:T(8,128)(2,1)S(1)}, bf16[256,256]{1,0:T(8,128)(2,1)S(1)}, u32[]{:S(2)}, u32[]{:S(2)}) collective-permute-start(bf16[256,256]{1,0:T(8,128)(2,1)S(1)} %get-tuple-element.40), channel_id=1, source_target_pairs={{8,0},{12,4},{16,8},{20,12},{24,16},{28,20},{0,24},{4,28},{9,1},{1... | collective-permute-start | bytes 393224 | tf_op jit(solution)/shard_map/ppermute | solution.py:451
  36.0 10.5 %collective-permute-start.10 = (bf16[256,256]{1,0:T(8,128)(2,1)S(1)}, bf16[256,256]{1,0:T(8,128)(2,1)S(1)}, u32[]{:S(2)}, u32[]{:S(2)}) collective-permute-start(bf16[256,256]{1,0:T(8,128)(2,1)S(1)} %get-tuple-element.43), channel_id=1, source_target_pairs={{4,0},{8,4},{12,8},{16,12},{20,16},{24,20},{28,24},{0,28},{5,1},{9... | collective-permute-start | bytes 393224 | tf_op jit(solution)/shard_map/ppermute | solution.py:453
  37.1 9.4 %collective-permute-start.11 = (bf16[256,256]{1,0:T(8,128)(2,1)S(1)}, bf16[256,256]{1,0:T(8,128)(2,1)S(1)}, u32[]{:S(2)}, u32[]{:S(2)}) collective-permute-start(bf16[256,256]{1,0:T(8,128)(2,1)S(1)} %get-tuple-element.44), channel_id=1, source_target_pairs={{0,4},{4,0},{8,12},{12,8},{16,20},{20,16},{24,28},{28,24},{1,5},{5... | collective-permute-start | bytes 393224 | tf_op jit(solution)/shard_map/ppermute | solution.py:453
  46.4 6.5 %collective-permute-start.13 = (bf16[256,256]{1,0:T(8,128)(2,1)S(1)}, bf16[256,256]{1,0:T(8,128)(2,1)S(1)}, u32[]{:S(2)}, u32[]{:S(2)}) collective-permute-start(bf16[256,256]{1,0:T(8,128)(2,1)S(1)} %get-tuple-element.47), channel_id=1, source_target_pairs={{8,0},{12,4},{16,8},{20,12},{24,16},{28,20},{0,24},{4,28},{9,1},{1... | collective-permute-start | bytes 393224 | tf_op jit(solution)/shard_map/ppermute | solution.py:451
  46.9 7.2 %collective-permute-start.14 = (bf16[256,256]{1,0:T(8,128)(2,1)S(1)}, bf16[256,256]{1,0:T(8,128)(2,1)S(1)}, u32[]{:S(2)}, u32[]{:S(2)}) collective-permute-start(bf16[256,256]{1,0:T(8,128)(2,1)S(1)} %get-tuple-element.50), channel_id=1, source_target_pairs={{4,0},{8,4},{12,8},{16,12},{20,16},{24,20},{28,24},{0,28},{5,1},{9... | collective-permute-start | bytes 393224 | tf_op jit(solution)/shard_map/ppermute | solution.py:453
  50.6 5.0 %collective-permute-start.15 = (bf16[256,256]{1,0:T(8,128)(2,1)S(1)}, bf16[256,256]{1,0:T(8,128)(2,1)S(1)}, u32[]{:S(2)}, u32[]{:S(2)}) collective-permute-start(bf16[256,256]{1,0:T(8,128)(2,1)S(1)} %get-tuple-element.52), channel_id=1, source_target_pairs={{0,4},{4,0},{8,12},{12,8},{16,20},{20,16},{24,28},{28,24},{1,5},{5... | collective-permute-start | bytes 393224 | tf_op jit(solution)/shard_map/ppermute | solution.py:453
  50.6 6.7 %collective-permute-start.12 = (bf16[256,256]{1,0:T(8,128)(2,1)S(1)}, bf16[256,256]{1,0:T(8,128)(2,1)S(1)}, u32[]{:S(2)}, u32[]{:S(2)}) collective-permute-start(bf16[256,256]{1,0:T(8,128)(2,1)S(1)} %shard_map.83), channel_id=1, source_target_pairs={{8,0},{12,4},{16,8},{20,12},{24,16},{28,20},{0,24},{4,28},{9,1},{1... | collective-permute-start | bytes 393224 | tf_op jit(solution)/shard_map/ppermute | solution.py:463
  55.6 5.0 %collective-permute-start.16 = (bf16[256,256]{1,0:T(8,128)(2,1)S(1)}, bf16[256,256]{1,0:T(8,128)(2,1)S(1)}, u32[]{:S(2)}, u32[]{:S(2)}) collective-permute-start(bf16[256,256]{1,0:T(8,128)(2,1)S(1)} %shard_map.84), channel_id=1, source_target_pairs={{8,0},{12,4},{16,8},{20,12},{24,16},{28,20},{0,24},{4,28},{9,1},{1... | collective-permute-start | bytes 393224 | tf_op jit(solution)/shard_map/ppermute | solution.py:463

commit v4 on v3

--- a/solution.py
+++ b/solution.py
@@ -17,9 +17,9 @@
 SMALL = pltpu.CompilerParams(vmem_limit_bytes=2 * 1024 * 1024)
 
 
-def prepare_kernel(n_tp, heads, key_ref, value_ref, doc_ref, grad_ref, query_ref, *rest):
+def prepare_kernel(n_tp, heads, key_ref, value_ref, doc_ref, grad_ref, *rest):
     outs, (doc_scr, sems) = rest[:-2], rest[-2:]
-    block_out, query_out, own_out, beside_out, across_outs = *outs[:4], outs[4:]
+    block_out, own_out, beside_out, across_outs = *outs[:3], outs[3:]
     tokens = key_ref.shape[0]
     rows = grad_ref.shape[0]
     me = lax.axis_index("tp")
@@ -50,7 +50,6 @@
             add(src, out.at[pl.ds(m % 2 * rows, rows), :])
     add(columns(1, 0, width), beside_out)
     add(columns(0, 0, width), own_out)
-    add(query_ref, query_out)
     copies[0].wait()
     row = doc_scr[...].astype(jnp.float32).astype(jnp.bfloat16)
     row = jnp.concatenate([row] * heads, axis=1)
@@ -59,7 +58,7 @@
         copy.wait()
 
 
-def prepare(key_matrix, value_matrix, document, output_gradient, queries, n_tp):
+def prepare(key_matrix, value_matrix, document, output_gradient, n_tp):
     tokens, kv_width = key_matrix.shape
     heads = kv_width // HEAD_WIDTH
     rows, width = output_gradient.shape
@@ -68,12 +67,11 @@
     two = pltpu.VMEM((2 * rows, width // n_tp // heads), jnp.bfloat16)
     shapes = (
         pltpu.VMEM((tokens + PAD, 2 * kv_width), jnp.bfloat16),
-        pltpu.VMEM(queries.shape, jnp.bfloat16),
         one,
         one,
     ) + (two,) * (chips * heads)
-    args = (key_matrix, value_matrix, document.reshape(1, tokens), output_gradient, queries)
-    block, query, own, beside, *across = pl.pallas_call(
+    args = (key_matrix, value_matrix, document.reshape(1, tokens), output_gradient)
+    block, own, beside, *across = pl.pallas_call(
         functools.partial(prepare_kernel, n_tp, heads),
         out_shape=shapes,
         in_specs=[ANY] * len(args),
@@ -84,7 +82,24 @@
         ],
         compiler_params=SMALL,
     )(*[pltpu.with_memory_space_constraint(x, pltpu.HBM) for x in args])
-    return block, query, own, beside, across
+    return block, own, beside, across
+
+
+def fetch_kernel(from_ref, out_ref, sem):
+    copy = pltpu.make_async_copy(from_ref, out_ref, sem)
+    copy.start()
+    copy.wait()
+
+
+def fetch(array):
+    return pl.pallas_call(
+        fetch_kernel,
+        out_shape=pltpu.VMEM(array.shape, array.dtype),
+        in_specs=[ANY],
+        out_specs=VMEM,
+        scratch_shapes=[pltpu.SemaphoreType.DMA],
+        compiler_params=SMALL,
+    )(pltpu.with_memory_space_constraint(array, pltpu.HBM))
 
 
 def choose_kernel(at, even_ref, odd_ref, out_ref):
@@ -395,9 +410,10 @@
     reach = n // 2
     half = reach // 2
 
-    block, queries, mine, beside, across = prepare(
-        key_matrix, value_matrix, document, output_gradient, queries, n_tp
+    block, mine, beside, across = prepare(
+        key_matrix, value_matrix, document, output_gradient, n_tp
     )
+    queries = fetch(after(queries, block))
 
     swap = [(a, a ^ 1) for a in range(n)]
 
@@ -428,7 +444,7 @@
             step = choose(evens[-2], evens[-2], h * width, width)
             odds[h].append(lax.ppermute(step, "seq", up(1, 2 * k)))
     near = lax.ppermute(choose(block, evens[0]), "seq", swap)
-    beside = lax.ppermute(after(beside, *odds[0][1:]), "tp", cores)
+    beside = lax.ppermute(after(beside, queries, *odds[0][1:]), "tp", cores)
     grads = [[mine, beside] for _ in range(heads)]
     for m in range(0, len(pairs), heads):
         rest = after(lower(*pairs[m : m + heads]), *odds[0][1:])

time: 61.6 us -> 61.3 us (level)
  waiting for transfers between devices: 21.2 us -> 20 us
  Pallas kernels: 19.7 us -> 20.6 us
    ppermute x2, waiting for transfers between devices: 1.79 us -> 0.54 us  [local(): lax.ppermute(pair, 'tp', [(a, a ^ 2 * (m // heads) + 2) for a in range(n_...]
    pallas_call x0 -> x1, Pallas kernels: none -> 1.23 us  [fetch(): pl.pallas_call(fetch_kernel, out_shape=pltpu.VMEM(array.shape, array.dtyp...]
  transfers between devices with their start and end apart: 17 -> 17, of which waited for: 9 -> 9; matrix products, arithmetic and copies ran while one was open for 0% -> 0% of each run, Pallas kernels for 28% -> 30%
where the time goes in v4:
time: 61.3 us; the launch traced here: 61.1 us
  Pallas kernels  20.6 us (34%)
  waiting for transfers between devices  20 us (33%)
  starting transfers between devices  19.8 us (32%)
  between operations  0.73 us (1%)
    pallas_call x2, Pallas kernels, head_call(): pl.pallas_call(functools.partial(main_kernel, h, reach, group, n_tp, firs...  16.8 us
    ppermute x1, waiting for transfers between devices, local(): evens = [lax.ppermute(block, 'seq', up(2, 0))]  6.65 us
    ppermute x4, starting transfers between devices, local(): lax.ppermute(x, 'seq', down(1, 2 * k) if k else swap)  5.67 us
    ppermute x2, waiting for transfers between devices, local(): moving = lax.ppermute(relay(k == 1, *parts), 'seq', down(2, 2 * k - 2))  3.94 us
    ppermute x1, waiting for transfers between devices, local(): near = lax.ppermute(choose(block, evens[0]), 'seq', swap)  3.08 us
    ppermute x1, starting transfers between devices, local(): evens = [lax.ppermute(block, 'seq', up(2, 0))]  3.08 us
    ppermute x4, waiting for transfers between devices, local(): lax.ppermute(x, 'seq', down(1, 2 * k) if k else swap)  2.61 us
    ppermute x2, starting transfers between devices, local(): moving = lax.ppermute(relay(k == 1, *parts), 'seq', down(2, 2 * k - 2))  2.16 us
  transfers between devices with their start and end apart: 17, of which 9 were waited for; matrix products, arithmetic and copies ran while one was open for 0% of the time, Pallas kernels for 30%

profile of v4, /device:TPU:0, one launch (start us, length us, event | category | flops | bytes accessed | tf_op | source)
XLA Modules:
  0.0 61.1 jit_solution(5036217807618310290)
XLA Ops:
  0.6 1.5 %shard_map.76 = (bf16[272,512]{1,0:T(8,128)(2,1)S(1)}, bf16[64,2048]{1,0:T(8,128)(2,1)S(1)}, bf16[64,2048]{1,0:T(8,128)(2,1)S(1)}, bf16[128,1024]{1,0:T(8,128)(2,1)S(1)}, bf16[128,1024]{1,0:T(8,128)(2,1)S(1)}) custom-call(bf16[256,256]{1,0:T(8,128)(2,1)} %key_ref.1, bf16[256,256]{1,0:T(8,128)(2,1)} %value_ref.1, s32[1,256]{1,0:T(1,128)} %bitcast.1, ...), custom_call_target="tpu_custom_call" | custom-call | tf_op jit(solution)/shard_map/pallas_call | solution.py:74
  2.1 3.1 %collective-permute-start = (bf16[272,512]{1,0:T(8,128)(2,1)S(1)}, bf16[272,512]{1,0:T(8,128)(2,1)S(1)}, u32[]{:S(2)}, u32[]{:S(2)}) collective-permute-start(bf16[272,512]{1,0:T(8,128)(2,1)S(1)} %get-tuple-element.29.even_ref.refs_5_), channel_id=1, source_target_pairs={{0,8},{4,12},{8,16},{12,20},{16,24},{20,28},{24,0},{28,4},{1,9},{5... | collective-permute-start | bytes 835592 | tf_op jit(solution)/shard_map/ppermute | solution.py:432
  5.2 1.5 %collective-permute-start.3 = (bf16[128,1024]{1,0:T(8,128)(2,1)S(1)}, bf16[128,1024]{1,0:T(8,128)(2,1)S(1)}, u32[]{:S(2)}, u32[]{:S(2)}) collective-permute-start(bf16[128,1024]{1,0:T(8,128)(2,1)S(1)} %get-tuple-element.34), channel_id=1, source_target_pairs={{0,2},{1,3},{2,0},{3,1},{4,6},{5,7},{6,4},{7,5},{8,10},{9,11},{10,... | collective-permute-start | bytes 786440 | tf_op jit(solution)/shard_map/ppermute | solution.py:434
  7.2 6.7 %collective-permute-done.even_ref.odd_ref.refs_8_ = bf16[272,512]{1,0:T(8,128)(2,1)S(1)} collective-permute-done((bf16[272,512]{1,0:T(8,128)(2,1)S(1)}, bf16[272,512]{1,0:T(8,128)(2,1)S(1)}, u32[]{:S(2)}, u32[]{:S(2)}) %collective-permute-start) | collective-permute-done | bytes 278560 | tf_op jit(solution)/shard_map/ppermute | solution.py:432
  13.9 1.6 %collective-permute-start.1 = (bf16[272,256]{1,0:T(8,128)(2,1)S(1)}, bf16[272,256]{1,0:T(8,128)(2,1)S(1)}, u32[]{:S(2)}, u32[]{:S(2)}) collective-permute-start(bf16[272,256]{1,0:T(8,128)(2,1)S(1)} %shard_map.78), channel_id=1, source_target_pairs={{8,12},{12,16},{16,20},{20,24},{24,28},{0,4},{4,0},{28,8},{9,13},{... | collective-permute-start | bytes 417800 | tf_op jit(solution)/shard_map/ppermute | solution.py:441
  16.1 0.7 %collective-permute-start.8 = (bf16[272,512]{1,0:T(8,128)(2,1)S(1)}, bf16[272,512]{1,0:T(8,128)(2,1)S(1)}, u32[]{:S(2)}, u32[]{:S(2)}) collective-permute-start(bf16[272,512]{1,0:T(8,128)(2,1)S(1)} %collective-permute-done.even_ref.odd_ref.refs_8_), channel_id=1, source_target_pairs={{0,8},{4,12},{8,16},{12,20},{16,24},{20,28},{24,0},{28,4},{1,9},{5... | collective-permute-start | bytes 835592 | tf_op jit(solution)/shard_map/ppermute | solution.py:442
  16.8 1.2 %shard_map.77.refs_0_ = bf16[256,2048]{1,0:T(8,128)(2,1)S(1)} custom-call(bf16[256,2048]{1,0:T(8,128)(2,1)} %from_ref), custom_call_target="tpu_custom_call" | custom-call | tf_op jit(solution)/shard_map/pallas_call | solution.py:95
  18.6 2.0 %collective-permute-done.1.refs_7_ = bf16[272,256]{1,0:T(8,128)(2,1)S(1)} collective-permute-done((bf16[272,256]{1,0:T(8,128)(2,1)S(1)}, bf16[272,256]{1,0:T(8,128)(2,1)S(1)}, u32[]{:S(2)}, u32[]{:S(2)}) %collective-permute-start.1) | collective-permute-done | bytes 139296 | tf_op jit(solution)/shard_map/ppermute | solution.py:441
  21.1 1.6 %collective-permute-start.7 = (bf16[272,256]{1,0:T(8,128)(2,1)S(1)}, bf16[272,256]{1,0:T(8,128)(2,1)S(1)}, u32[]{:S(2)}, u32[]{:S(2)}) collective-permute-start(bf16[272,256]{1,0:T(8,128)(2,1)S(1)} %shard_map.81), channel_id=1, source_target_pairs={{8,12},{12,16},{16,20},{20,24},{24,28},{0,4},{4,0},{28,8},{9,13},{... | collective-permute-start | bytes 417800 | tf_op jit(solution)/shard_map/ppermute | solution.py:445
  22.7 3.1 %collective-permute-done.6.refs_6_ = bf16[272,512]{1,0:T(8,128)(2,1)S(1)} collective-permute-done((bf16[272,512]{1,0:T(8,128)(2,1)S(1)}, bf16[272,512]{1,0:T(8,128)(2,1)S(1)}, u32[]{:S(2)}, u32[]{:S(2)}) %collective-permute-start.6) | collective-permute-done | bytes 278560 | tf_op jit(solution)/shard_map/ppermute | solution.py:446
  25.8 8.4 %shard_map.82 = (bf16[256,2048]{1,0:T(8,128)(2,1)}, bf16[256,256]{1,0:T(8,128)(2,1)S(1)}, bf16[256,256]{1,0:T(8,128)(2,1)S(1)}, bf16[256,256]{1,0:T(8,128)(2,1)S...) custom-call(bf16[256,2048]{1,0:T(8,128)(2,1)S(1)} %shard_map.77.refs_0_, ...), custom_call_target="tpu_custom_call" | custom-call | flops 13421772800 | bytes 4194304 | tf_op jit(solution)/shard_map/pallas_call | solution.py:382
  34.2 1.4 %collective-permute-start.9 = (bf16[256,256]{1,0:T(8,128)(2,1)S(1)}, bf16[256,256]{1,0:T(8,128)(2,1)S(1)}, u32[]{:S(2)}, u32[]{:S(2)}) collective-permute-start(bf16[256,256]{1,0:T(8,128)(2,1)S(1)} %get-tuple-element.40), channel_id=1, source_target_pairs={{8,0},{12,4},{16,8},{20,12},{24,16},{28,20},{0,24},{4,28},{9,1},{1... | collective-permute-start | bytes 393224 | tf_op jit(solution)/shard_map/ppermute | solution.py:467
  35.6 1.1 %collective-permute-start.10 = (bf16[256,256]{1,0:T(8,128)(2,1)S(1)}, bf16[256,256]{1,0:T(8,128)(2,1)S(1)}, u32[]{:S(2)}, u32[]{:S(2)}) collective-permute-start(bf16[256,256]{1,0:T(8,128)(2,1)S(1)} %get-tuple-element.43), channel_id=1, source_target_pairs={{4,0},{8,4},{12,8},{16,12},{20,16},{24,20},{28,24},{0,28},{5,1},{9... | collective-permute-start | bytes 393224 | tf_op jit(solution)/shard_map/ppermute | solution.py:469
  36.7 0.9 %collective-permute-start.11 = (bf16[256,256]{1,0:T(8,128)(2,1)S(1)}, bf16[256,256]{1,0:T(8,128)(2,1)S(1)}, u32[]{:S(2)}, u32[]{:S(2)}) collective-permute-start(bf16[256,256]{1,0:T(8,128)(2,1)S(1)} %get-tuple-element.44), channel_id=1, source_target_pairs={{0,4},{4,0},{8,12},{12,8},{16,20},{20,16},{24,28},{28,24},{1,5},{5... | collective-permute-start | bytes 393224 | tf_op jit(solution)/shard_map/ppermute | solution.py:469
  37.6 8.4 %shard_map.83 = (bf16[256,2048]{1,0:T(8,128)(2,1)}, bf16[256,256]{1,0:T(8,128)(2,1)S(1)}, bf16[256,256]{1,0:T(8,128)(2,1)S(1)}, bf16[256,256]{1,0:T(8,128)(2,1)S...) custom-call(bf16[256,2048]{1,0:T(8,128)(2,1)S(1)} %shard_map.77.refs_0_, ...), custom_call_target="tpu_custom_call", output_to_operand_aliasing={{0}: (10, {})} | custom-call | flops 13421772800 | bytes 4194304 | tf_op jit(solution)/shard_map/pallas_call | solution.py:382
  46.6 3.6 %collective-permute-start.14 = (bf16[256,256]{1,0:T(8,128)(2,1)S(1)}, bf16[256,256]{1,0:T(8,128)(2,1)S(1)}, u32[]{:S(2)}, u32[]{:S(2)}) collective-permute-start(bf16[256,256]{1,0:T(8,128)(2,1)S(1)} %get-tuple-element.50), channel_id=1, source_target_pairs={{4,0},{8,4},{12,8},{16,12},{20,16},{24,20},{28,24},{0,28},{5,1},{9... | collective-permute-start | bytes 393224 | tf_op jit(solution)/shard_map/ppermute | solution.py:469
  50.3 1.1 %collective-permute-start.12 = (bf16[256,256]{1,0:T(8,128)(2,1)S(1)}, bf16[256,256]{1,0:T(8,128)(2,1)S(1)}, u32[]{:S(2)}, u32[]{:S(2)}) collective-permute-start(bf16[256,256]{1,0:T(8,128)(2,1)S(1)} %shard_map.84), channel_id=1, source_target_pairs={{8,0},{12,4},{16,8},{20,12},{24,16},{28,20},{0,24},{4,28},{9,1},{1... | collective-permute-start | bytes 393224 | tf_op jit(solution)/shard_map/ppermute | solution.py:479
  51.4 1.2 %collective-permute-done.13.refs_0_ = bf16[256,256]{1,0:T(8,128)(2,1)S(1)} collective-permute-done((bf16[256,256]{1,0:T(8,128)(2,1)S(1)}, bf16[256,256]{1,0:T(8,128)(2,1)S(1)}, u32[]{:S(2)}, u32[]{:S(2)}) %collective-permute-start.13) | collective-permute-done | bytes 131104 | tf_op jit(solution)/shard_map/ppermute | solution.py:467
  52.6 1.2 %collective-permute-done.14.refs_2_ = bf16[256,256]{1,0:T(8,128)(2,1)S(1)} collective-permute-done((bf16[256,256]{1,0:T(8,128)(2,1)S(1)}, bf16[256,256]{1,0:T(8,128)(2,1)S(1)}, u32[]{:S(2)}, u32[]{:S(2)}) %collective-permute-start.14) | collective-permute-done | bytes 131104 | tf_op jit(solution)/shard_map/ppermute | solution.py:469
  53.8 1.4 %collective-permute-done.15.refs_3_.refs_5_ = bf16[256,256]{1,0:T(8,128)(2,1)S(1)} collective-permute-done((bf16[256,256]{1,0:T(8,128)(2,1)S(1)}, bf16[256,256]{1,0:T(8,128)(2,1)S(1)}, u32[]{:S(2)}, u32[]{:S(2)}) %collective-permute-start.15) | collective-permute-done | bytes 131104 | tf_op jit(solution)/shard_map/ppermute | solution.py:469
  55.3 1.1 %collective-permute-start.16 = (bf16[256,256]{1,0:T(8,128)(2,1)S(1)}, bf16[256,256]{1,0:T(8,128)(2,1)S(1)}, u32[]{:S(2)}, u32[]{:S(2)}) collective-permute-start(bf16[256,256]{1,0:T(8,128)(2,1)S(1)} %shard_map.85), channel_id=1, source_target_pairs={{8,0},{12,4},{16,8},{20,12},{24,16},{28,20},{0,24},{4,28},{9,1},{1... | collective-permute-start | bytes 393224 | tf_op jit(solution)/shard_map/ppermute | solution.py:479
  56.3 0.6 %collective-permute-done.12.refs_1_ = bf16[256,256]{1,0:T(8,128)(2,1)S(1)} collective-permute-done((bf16[256,256]{1,0:T(8,128)(2,1)S(1)}, bf16[256,256]{1,0:T(8,128)(2,1)S(1)}, u32[]{:S(2)}, u32[]{:S(2)}) %collective-permute-start.12) | collective-permute-done | bytes 131104 | tf_op jit(solution)/shard_map/ppermute | solution.py:479
  57.0 3.3 %collective-permute-done.16.refs_4_ = bf16[256,256]{1,0:T(8,128)(2,1)S(1)} collective-permute-done((bf16[256,256]{1,0:T(8,128)(2,1)S(1)}, bf16[256,256]{1,0:T(8,128)(2,1)S(1)}, u32[]{:S(2)}, u32[]{:S(2)}) %collective-permute-start.16) | collective-permute-done | bytes 131104 | tf_op jit(solution)/shard_map/ppermute | solution.py:479
  60.3 0.8 %shard_map.86 = (bf16[256,256]{1,0:T(8,128)(2,1)}, bf16[256,256]{1,0:T(8,128)(2,1)}) custom-call(f32[256,256]{1,0:T(8,128)S(1)} %get-tuple-element.39.refs_0_, bf16[256,256]{1,0:T(8,128)(2,1)S(1)} %collective-permute-done.12.refs_1_, bf16[256,256]{1,0:T(8,128)(2,1)S(1)} %collective-permute-done.11.refs_3_.refs_2_, f32[256,256]{1,0:T(8,128)S(1)} %get-tuple-element.45.refs_3_, ...), custom_call_target="tpu_custom_call" | custom-call | tf_op jit(solution)/shard_map/pallas_call | solution.py:184
  (21 shorter events, 2.9 us)
Async XLA Ops:
  2.1 11.8 %collective-permute-start = (bf16[272,512]{1,0:T(8,128)(2,1)S(1)}, bf16[272,512]{1,0:T(8,128)(2,1)S(1)}, u32[]{:S(2)}, u32[]{:S(2)}) collective-permute-start(bf16[272,512]{1,0:T(8,128)(2,1)S(1)} %get-tuple-element.29.even_ref.refs_5_), channel_id=1, source_target_pairs={{0,8},{4,12},{8,16},{12,20},{16,24},{20,28},{24,0},{28,4},{1,9},{5... | collective-permute-start | bytes 835592 | tf_op jit(solution)/shard_map/ppermute | solution.py:432
  5.2 12.8 %collective-permute-start.3 = (bf16[128,1024]{1,0:T(8,128)(2,1)S(1)}, bf16[128,1024]{1,0:T(8,128)(2,1)S(1)}, u32[]{:S(2)}, u32[]{:S(2)}) collective-permute-start(bf16[128,1024]{1,0:T(8,128)(2,1)S(1)} %get-tuple-element.34), channel_id=1, source_target_pairs={{0,2},{1,3},{2,0},{3,1},{4,6},{5,7},{6,4},{7,5},{8,10},{9,11},{10,... | collective-permute-start | bytes 786440 | tf_op jit(solution)/shard_map/ppermute | solution.py:434
  6.7 11.9 %collective-permute-start.4 = (bf16[128,1024]{1,0:T(8,128)(2,1)S(1)}, bf16[128,1024]{1,0:T(8,128)(2,1)S(1)}, u32[]{:S(2)}, u32[]{:S(2)}) collective-permute-start(bf16[128,1024]{1,0:T(8,128)(2,1)S(1)} %get-tuple-element.35), channel_id=1, source_target_pairs={{0,2},{1,3},{2,0},{3,1},{4,6},{5,7},{6,4},{7,5},{8,10},{9,11},{10,... | collective-permute-start | bytes 786440 | tf_op jit(solution)/shard_map/ppermute | solution.py:434
  13.9 6.7 %collective-permute-start.1 = (bf16[272,256]{1,0:T(8,128)(2,1)S(1)}, bf16[272,256]{1,0:T(8,128)(2,1)S(1)}, u32[]{:S(2)}, u32[]{:S(2)}) collective-permute-start(bf16[272,256]{1,0:T(8,128)(2,1)S(1)} %shard_map.78), channel_id=1, source_target_pairs={{8,12},{12,16},{16,20},{20,24},{24,28},{0,4},{4,0},{28,8},{9,13},{... | collective-permute-start | bytes 417800 | tf_op jit(solution)/shard_map/ppermute | solution.py:441
  15.5 10.2 %collective-permute-start.6 = (bf16[272,512]{1,0:T(8,128)(2,1)S(1)}, bf16[272,512]{1,0:T(8,128)(2,1)S(1)}, u32[]{:S(2)}, u32[]{:S(2)}) collective-permute-start(bf16[272,512]{1,0:T(8,128)(2,1)S(1)} %shard_map.80), channel_id=1, source_target_pairs={{0,4},{4,0},{8,12},{12,8},{16,20},{20,16},{24,28},{28,24},{1,5},{5... | collective-permute-start | bytes 835592 | tf_op jit(solution)/shard_map/ppermute | solution.py:446
  16.1 9.7 %collective-permute-start.8 = (bf16[272,512]{1,0:T(8,128)(2,1)S(1)}, bf16[272,512]{1,0:T(8,128)(2,1)S(1)}, u32[]{:S(2)}, u32[]{:S(2)}) collective-permute-start(bf16[272,512]{1,0:T(8,128)(2,1)S(1)} %collective-permute-done.even_ref.odd_ref.refs_8_), channel_id=1, source_target_pairs={{0,8},{4,12},{8,16},{12,20},{16,24},{20,28},{24,0},{28,4},{1,9},{5... | collective-permute-start | bytes 835592 | tf_op jit(solution)/shard_map/ppermute | solution.py:442
  20.6 5.2 %collective-permute-start.5 = (bf16[64,2048]{1,0:T(8,128)(2,1)S(1)}, bf16[64,2048]{1,0:T(8,128)(2,1)S(1)}, u32[]{:S(2)}, u32[]{:S(2)}) collective-permute-start(bf16[64,2048]{1,0:T(8,128)(2,1)S(1)} %shard_map.79), channel_id=1, source_target_pairs={{0,1},{1,0},{2,3},{3,2},{4,5},{5,4},{6,7},{7,6},{8,9},{9,8},{10,11... | collective-permute-start | bytes 786440 | tf_op jit(solution)/shard_map/ppermute | solution.py:451
  20.6 5.2 %collective-permute-start.2 = (bf16[64,2048]{1,0:T(8,128)(2,1)S(1)}, bf16[64,2048]{1,0:T(8,128)(2,1)S(1)}, u32[]{:S(2)}, u32[]{:S(2)}) collective-permute-start(bf16[64,2048]{1,0:T(8,128)(2,1)S(1)} %get-tuple-element.33), channel_id=1, source_target_pairs={{0,1},{1,0},{2,3},{3,2},{4,5},{5,4},{6,7},{7,6},{8,9},{9,8},{10,11... | collective-permute-start | bytes 786440 | tf_op jit(solution)/shard_map/ppermute | solution.py:447
  21.1 16.5 %collective-permute-start.7 = (bf16[272,256]{1,0:T(8,128)(2,1)S(1)}, bf16[272,256]{1,0:T(8,128)(2,1)S(1)}, u32[]{:S(2)}, u32[]{:S(2)}) collective-permute-start(bf16[272,256]{1,0:T(8,128)(2,1)S(1)} %shard_map.81), channel_id=1, source_target_pairs={{8,12},{12,16},{16,20},{20,24},{24,28},{0,4},{4,0},{28,8},{9,13},{... | collective-permute-start | bytes 417800 | tf_op jit(solution)/shard_map/ppermute | solution.py:445
  34.2 11.9 %collective-permute-start.9 = (bf16[256,256]{1,0:T(8,128)(2,1)S(1)}, bf16[256,256]{1,0:T(8,128)(2,1)S(1)}, u32[]{:S(2)}, u32[]{:S(2)}) collective-permute-start(bf16[256,256]{1,0:T(8,128)(2,1)S(1)} %get-tuple-element.40), channel_id=1, source_target_pairs={{8,0},{12,4},{16,8},{20,12},{24,16},{28,20},{0,24},{4,28},{9,1},{1... | collective-permute-start | bytes 393224 | tf_op jit(solution)/shard_map/ppermute | solution.py:467
  35.6 10.5 %collective-permute-start.10 = (bf16[256,256]{1,0:T(8,128)(2,1)S(1)}, bf16[256,256]{1,0:T(8,128)(2,1)S(1)}, u32[]{:S(2)}, u32[]{:S(2)}) collective-permute-start(bf16[256,256]{1,0:T(8,128)(2,1)S(1)} %get-tuple-element.43), channel_id=1, source_target_pairs={{4,0},{8,4},{12,8},{16,12},{20,16},{24,20},{28,24},{0,28},{5,1},{9... | collective-permute-start | bytes 393224 | tf_op jit(solution)/shard_map/ppermute | solution.py:469
  36.7 9.4 %collective-permute-start.11 = (bf16[256,256]{1,0:T(8,128)(2,1)S(1)}, bf16[256,256]{1,0:T(8,128)(2,1)S(1)}, u32[]{:S(2)}, u32[]{:S(2)}) collective-permute-start(bf16[256,256]{1,0:T(8,128)(2,1)S(1)} %get-tuple-element.44), channel_id=1, source_target_pairs={{0,4},{4,0},{8,12},{12,8},{16,20},{20,16},{24,28},{28,24},{1,5},{5... | collective-permute-start | bytes 393224 | tf_op jit(solution)/shard_map/ppermute | solution.py:469
  46.1 6.5 %collective-permute-start.13 = (bf16[256,256]{1,0:T(8,128)(2,1)S(1)}, bf16[256,256]{1,0:T(8,128)(2,1)S(1)}, u32[]{:S(2)}, u32[]{:S(2)}) collective-permute-start(bf16[256,256]{1,0:T(8,128)(2,1)S(1)} %get-tuple-element.47), channel_id=1, source_target_pairs={{8,0},{12,4},{16,8},{20,12},{24,16},{28,20},{0,24},{4,28},{9,1},{1... | collective-permute-start | bytes 393224 | tf_op jit(solution)/shard_map/ppermute | solution.py:467
  46.6 7.2 %collective-permute-start.14 = (bf16[256,256]{1,0:T(8,128)(2,1)S(1)}, bf16[256,256]{1,0:T(8,128)(2,1)S(1)}, u32[]{:S(2)}, u32[]{:S(2)}) collective-permute-start(bf16[256,256]{1,0:T(8,128)(2,1)S(1)} %get-tuple-element.50), channel_id=1, source_target_pairs={{4,0},{8,4},{12,8},{16,12},{20,16},{24,20},{28,24},{0,28},{5,1},{9... | collective-permute-start | bytes 393224 | tf_op jit(solution)/shard_map/ppermute | solution.py:469
  50.2 5.0 %collective-permute-start.15 = (bf16[256,256]{1,0:T(8,128)(2,1)S(1)}, bf16[256,256]{1,0:T(8,128)(2,1)S(1)}, u32[]{:S(2)}, u32[]{:S(2)}) collective-permute-start(bf16[256,256]{1,0:T(8,128)(2,1)S(1)} %get-tuple-element.52), channel_id=1, source_target_pairs={{0,4},{4,0},{8,12},{12,8},{16,20},{20,16},{24,28},{28,24},{1,5},{5... | collective-permute-start | bytes 393224 | tf_op jit(solution)/shard_map/ppermute | solution.py:469
  50.3 6.7 %collective-permute-start.12 = (bf16[256,256]{1,0:T(8,128)(2,1)S(1)}, bf16[256,256]{1,0:T(8,128)(2,1)S(1)}, u32[]{:S(2)}, u32[]{:S(2)}) collective-permute-start(bf16[256,256]{1,0:T(8,128)(2,1)S(1)} %shard_map.84), channel_id=1, source_target_pairs={{8,0},{12,4},{16,8},{20,12},{24,16},{28,20},{0,24},{4,28},{9,1},{1... | collective-permute-start | bytes 393224 | tf_op jit(solution)/shard_map/ppermute | solution.py:479
  55.3 5.0 %collective-permute-start.16 = (bf16[256,256]{1,0:T(8,128)(2,1)S(1)}, bf16[256,256]{1,0:T(8,128)(2,1)S(1)}, u32[]{:S(2)}, u32[]{:S(2)}) collective-permute-start(bf16[256,256]{1,0:T(8,128)(2,1)S(1)} %shard_map.85), channel_id=1, source_target_pairs={{8,0},{12,4},{16,8},{20,12},{24,16},{28,20},{0,24},{4,28},{9,1},{1... | collective-permute-start | bytes 393224 | tf_op jit(solution)/shard_map/ppermute | solution.py:479

commit v5 on v4

--- a/solution.py
+++ b/solution.py
@@ -19,7 +19,7 @@
 
 def prepare_kernel(n_tp, heads, key_ref, value_ref, doc_ref, grad_ref, *rest):
     outs, (doc_scr, sems) = rest[:-2], rest[-2:]
-    block_out, own_out, beside_out, across_outs = *outs[:3], outs[3:]
+    block_out, across_outs = outs[0], outs[1:]
     tokens = key_ref.shape[0]
     rows = grad_ref.shape[0]
     me = lax.axis_index("tp")
@@ -48,8 +48,6 @@
             out = across_outs[(m // 2 - 1) * heads + h]
             src = columns(m, h * part, part)
             add(src, out.at[pl.ds(m % 2 * rows, rows), :])
-    add(columns(1, 0, width), beside_out)
-    add(columns(0, 0, width), own_out)
     copies[0].wait()
     row = doc_scr[...].astype(jnp.float32).astype(jnp.bfloat16)
     row = jnp.concatenate([row] * heads, axis=1)
@@ -63,15 +61,12 @@
     heads = kv_width // HEAD_WIDTH
     rows, width = output_gradient.shape
     chips = n_tp // 2 - 1
-    one = pltpu.VMEM((rows, width // n_tp), jnp.bfloat16)
     two = pltpu.VMEM((2 * rows, width // n_tp // heads), jnp.bfloat16)
     shapes = (
         pltpu.VMEM((tokens + PAD, 2 * kv_width), jnp.bfloat16),
-        one,
-        one,
     ) + (two,) * (chips * heads)
     args = (key_matrix, value_matrix, document.reshape(1, tokens), output_gradient)
-    block, own, beside, *across = pl.pallas_call(
+    block, *across = pl.pallas_call(
         functools.partial(prepare_kernel, n_tp, heads),
         out_shape=shapes,
         in_specs=[ANY] * len(args),
@@ -82,24 +77,35 @@
         ],
         compiler_params=SMALL,
     )(*[pltpu.with_memory_space_constraint(x, pltpu.HBM) for x in args])
-    return block, own, beside, across
-
-
-def fetch_kernel(from_ref, out_ref, sem):
-    copy = pltpu.make_async_copy(from_ref, out_ref, sem)
-    copy.start()
-    copy.wait()
-
-
-def fetch(array):
+    return block, across
+
+
+def fetch_kernel(n_tp, query_ref, grad_ref, query_out, own_out, beside_out, sems):
+    me = lax.axis_index("tp")
+    width = grad_ref.shape[1] // n_tp
+    copies = [pltpu.make_async_copy(query_ref, query_out, sems.at[0])]
+    for m, out in enumerate((own_out, beside_out)):
+        start = pl.multiple_of((me ^ m) * width, width)
+        src = grad_ref.at[:, pl.ds(start, width)]
+        copies.append(pltpu.make_async_copy(src, out, sems.at[m + 1]))
+    for copy in copies:
+        copy.start()
+    for copy in copies:
+        copy.wait()
+
+
+def fetch(queries, output_gradient, n_tp):
+    rows, width = output_gradient.shape
+    one = pltpu.VMEM((rows, width // n_tp), jnp.bfloat16)
+    args = [pltpu.with_memory_space_constraint(x, pltpu.HBM) for x in (queries, output_gradient)]
     return pl.pallas_call(
-        fetch_kernel,
-        out_shape=pltpu.VMEM(array.shape, array.dtype),
-        in_specs=[ANY],
-        out_specs=VMEM,
-        scratch_shapes=[pltpu.SemaphoreType.DMA],
-        compiler_params=SMALL,
-    )(pltpu.with_memory_space_constraint(array, pltpu.HBM))
+        functools.partial(fetch_kernel, n_tp),
+        out_shape=(pltpu.VMEM(queries.shape, queries.dtype), one, one),
+        in_specs=[ANY, ANY],
+        out_specs=(VMEM,) * 3,
+        scratch_shapes=[pltpu.SemaphoreType.DMA((3,))],
+        compiler_params=SMALL,
+    )(*args)
 
 
 def choose_kernel(at, even_ref, odd_ref, out_ref):
@@ -410,10 +416,10 @@
     reach = n // 2
     half = reach // 2
 
-    block, mine, beside, across = prepare(
+    block, across = prepare(
         key_matrix, value_matrix, document, output_gradient, n_tp
     )
-    queries = fetch(after(queries, block))
+    queries, mine, beside = fetch(after(queries, block), output_gradient, n_tp)
 
     swap = [(a, a ^ 1) for a in range(n)]
 

time: 61.3 us -> 61.1 us (level)
  no operation moved by 1% of the time
where the time goes in v5:
time: 61.1 us; the launch traced here: 60.9 us
  Pallas kernels  20.5 us (34%)
  waiting for transfers between devices  19.9 us (33%)
  starting transfers between devices  19.8 us (32%)
  between operations  0.73 us (1%)
    pallas_call x2, Pallas kernels, head_call(): pl.pallas_call(functools.partial(main_kernel, h, reach, group, n_tp, firs...  16.8 us
    ppermute x1, waiting for transfers between devices, local(): evens = [lax.ppermute(block, 'seq', up(2, 0))]  6.65 us
    ppermute x4, starting transfers between devices, local(): lax.ppermute(x, 'seq', down(1, 2 * k) if k else swap)  5.65 us
    ppermute x2, waiting for transfers between devices, local(): moving = lax.ppermute(relay(k == 1, *parts), 'seq', down(2, 2 * k - 2))  3.95 us
    ppermute x1, waiting for transfers between devices, local(): near = lax.ppermute(choose(block, evens[0]), 'seq', swap)  3.08 us
    ppermute x1, starting transfers between devices, local(): evens = [lax.ppermute(block, 'seq', up(2, 0))]  3.08 us
    ppermute x4, waiting for transfers between devices, local(): lax.ppermute(x, 'seq', down(1, 2 * k) if k else swap)  2.62 us
    ppermute x2, starting transfers between devices, local(): moving = lax.ppermute(relay(k == 1, *parts), 'seq', down(2, 2 * k - 2))  2.15 us
  transfers between devices with their start and end apart: 17, of which 9 were waited for; matrix products, arithmetic and copies ran while one was open for 0% of the time, Pallas kernels for 30%

profile of v5, /device:TPU:0, one launch (start us, length us, event | category | flops | bytes accessed | tf_op | source)
XLA Modules:
  0.0 60.9 jit_solution(1739570625754558888)
XLA Ops:
  0.6 1.3 %shard_map.76 = (bf16[272,512]{1,0:T(8,128)(2,1)S(1)}, bf16[128,1024]{1,0:T(8,128)(2,1)S(1)}, bf16[128,1024]{1,0:T(8,128)(2,1)S(1)}) custom-call(bf16[256,256]{1,0:T(8,128)(2,1)} %key_ref.1, bf16[256,256]{1,0:T(8,128)(2,1)} %value_ref.1, s32[1,256]{1,0:T(1,128)} %bitcast.1, bf16[64,8192]{1,0:T(8,128)(2,1)} %grad_ref.3), custom_call_target="tpu_custom_call" | custom-call | tf_op jit(solution)/shard_map/pallas_call | solution.py:69
  2.0 3.1 %collective-permute-start = (bf16[272,512]{1,0:T(8,128)(2,1)S(1)}, bf16[272,512]{1,0:T(8,128)(2,1)S(1)}, u32[]{:S(2)}, u32[]{:S(2)}) collective-permute-start(bf16[272,512]{1,0:T(8,128)(2,1)S(1)} %get-tuple-element.30.even_ref.refs_5_), channel_id=1, source_target_pairs={{0,8},{4,12},{8,16},{12,20},{16,24},{20,28},{24,0},{28,4},{1,9},{5... | collective-permute-start | bytes 835592 | tf_op jit(solution)/shard_map/ppermute | solution.py:438
  5.0 1.5 %collective-permute-start.3 = (bf16[128,1024]{1,0:T(8,128)(2,1)S(1)}, bf16[128,1024]{1,0:T(8,128)(2,1)S(1)}, u32[]{:S(2)}, u32[]{:S(2)}) collective-permute-start(bf16[128,1024]{1,0:T(8,128)(2,1)S(1)} %get-tuple-element.36), channel_id=1, source_target_pairs={{0,2},{1,3},{2,0},{3,1},{4,6},{5,7},{6,4},{7,5},{8,10},{9,11},{10,... | collective-permute-start | bytes 786440 | tf_op jit(solution)/shard_map/ppermute | solution.py:440
  7.1 6.7 %collective-permute-done.even_ref.odd_ref.refs_8_ = bf16[272,512]{1,0:T(8,128)(2,1)S(1)} collective-permute-done((bf16[272,512]{1,0:T(8,128)(2,1)S(1)}, bf16[272,512]{1,0:T(8,128)(2,1)S(1)}, u32[]{:S(2)}, u32[]{:S(2)}) %collective-permute-start) | collective-permute-done | bytes 278560 | tf_op jit(solution)/shard_map/ppermute | solution.py:438
  13.7 1.6 %collective-permute-start.1 = (bf16[272,256]{1,0:T(8,128)(2,1)S(1)}, bf16[272,256]{1,0:T(8,128)(2,1)S(1)}, u32[]{:S(2)}, u32[]{:S(2)}) collective-permute-start(bf16[272,256]{1,0:T(8,128)(2,1)S(1)} %shard_map.78), channel_id=1, source_target_pairs={{8,12},{12,16},{16,20},{20,24},{24,28},{0,4},{4,0},{28,8},{9,13},{... | collective-permute-start | bytes 417800 | tf_op jit(solution)/shard_map/ppermute | solution.py:447
  15.9 0.7 %collective-permute-start.8 = (bf16[272,512]{1,0:T(8,128)(2,1)S(1)}, bf16[272,512]{1,0:T(8,128)(2,1)S(1)}, u32[]{:S(2)}, u32[]{:S(2)}) collective-permute-start(bf16[272,512]{1,0:T(8,128)(2,1)S(1)} %collective-permute-done.even_ref.odd_ref.refs_8_), channel_id=1, source_target_pairs={{0,8},{4,12},{8,16},{12,20},{16,24},{20,28},{24,0},{28,4},{1,9},{5... | collective-permute-start | bytes 835592 | tf_op jit(solution)/shard_map/ppermute | solution.py:448
  16.6 1.4 %shard_map.77 = (bf16[256,2048]{1,0:T(8,128)(2,1)S(1)}, bf16[64,2048]{1,0:T(8,128)(2,1)S(1)}, bf16[64,2048]{1,0:T(8,128)(2,1)S(1)}) custom-call(bf16[256,2048]{1,0:T(8,128)(2,1)} %query_ref, bf16[64,8192]{1,0:T(8,128)(2,1)} %grad_ref.3), custom_call_target="tpu_custom_call" | custom-call | tf_op jit(solution)/shard_map/pallas_call | solution.py:101
  18.5 2.0 %collective-permute-done.1.refs_7_ = bf16[272,256]{1,0:T(8,128)(2,1)S(1)} collective-permute-done((bf16[272,256]{1,0:T(8,128)(2,1)S(1)}, bf16[272,256]{1,0:T(8,128)(2,1)S(1)}, u32[]{:S(2)}, u32[]{:S(2)}) %collective-permute-start.1) | collective-permute-done | bytes 139296 | tf_op jit(solution)/shard_map/ppermute | solution.py:447
  20.9 1.6 %collective-permute-start.7 = (bf16[272,256]{1,0:T(8,128)(2,1)S(1)}, bf16[272,256]{1,0:T(8,128)(2,1)S(1)}, u32[]{:S(2)}, u32[]{:S(2)}) collective-permute-start(bf16[272,256]{1,0:T(8,128)(2,1)S(1)} %shard_map.81), channel_id=1, source_target_pairs={{8,12},{12,16},{16,20},{20,24},{24,28},{0,4},{4,0},{28,8},{9,13},{... | collective-permute-start | bytes 417800 | tf_op jit(solution)/shard_map/ppermute | solution.py:451
  22.5 3.1 %collective-permute-done.6.refs_6_ = bf16[272,512]{1,0:T(8,128)(2,1)S(1)} collective-permute-done((bf16[272,512]{1,0:T(8,128)(2,1)S(1)}, bf16[272,512]{1,0:T(8,128)(2,1)S(1)}, u32[]{:S(2)}, u32[]{:S(2)}) %collective-permute-start.6) | collective-permute-done | bytes 278560 | tf_op jit(solution)/shard_map/ppermute | solution.py:452
  25.6 8.4 %shard_map.82 = (bf16[256,2048]{1,0:T(8,128)(2,1)}, bf16[256,256]{1,0:T(8,128)(2,1)S(1)}, bf16[256,256]{1,0:T(8,128)(2,1)S(1)}, bf16[256,256]{1,0:T(8,128)(2,1)S...) custom-call(bf16[256,2048]{1,0:T(8,128)(2,1)S(1)} %get-tuple-element.32.refs_0_, ...), custom_call_target="tpu_custom_call" | custom-call | flops 13421772800 | bytes 4194304 | tf_op jit(solution)/shard_map/pallas_call | solution.py:388
  34.0 1.4 %collective-permute-start.9 = (bf16[256,256]{1,0:T(8,128)(2,1)S(1)}, bf16[256,256]{1,0:T(8,128)(2,1)S(1)}, u32[]{:S(2)}, u32[]{:S(2)}) collective-permute-start(bf16[256,256]{1,0:T(8,128)(2,1)S(1)} %get-tuple-element.42), channel_id=1, source_target_pairs={{8,0},{12,4},{16,8},{20,12},{24,16},{28,20},{0,24},{4,28},{9,1},{1... | collective-permute-start | bytes 393224 | tf_op jit(solution)/shard_map/ppermute | solution.py:473
  35.4 1.1 %collective-permute-start.10 = (bf16[256,256]{1,0:T(8,128)(2,1)S(1)}, bf16[256,256]{1,0:T(8,128)(2,1)S(1)}, u32[]{:S(2)}, u32[]{:S(2)}) collective-permute-start(bf16[256,256]{1,0:T(8,128)(2,1)S(1)} %get-tuple-element.45), channel_id=1, source_target_pairs={{4,0},{8,4},{12,8},{16,12},{20,16},{24,20},{28,24},{0,28},{5,1},{9... | collective-permute-start | bytes 393224 | tf_op jit(solution)/shard_map/ppermute | solution.py:475
  36.5 0.9 %collective-permute-start.11 = (bf16[256,256]{1,0:T(8,128)(2,1)S(1)}, bf16[256,256]{1,0:T(8,128)(2,1)S(1)}, u32[]{:S(2)}, u32[]{:S(2)}) collective-permute-start(bf16[256,256]{1,0:T(8,128)(2,1)S(1)} %get-tuple-element.46), channel_id=1, source_target_pairs={{0,4},{4,0},{8,12},{12,8},{16,20},{20,16},{24,28},{28,24},{1,5},{5... | collective-permute-start | bytes 393224 | tf_op jit(solution)/shard_map/ppermute | solution.py:475
  37.5 8.4 %shard_map.83 = (bf16[256,2048]{1,0:T(8,128)(2,1)}, bf16[256,256]{1,0:T(8,128)(2,1)S(1)}, bf16[256,256]{1,0:T(8,128)(2,1)S(1)}, bf16[256,256]{1,0:T(8,128)(2,1)S...) custom-call(bf16[256,2048]{1,0:T(8,128)(2,1)S(1)} %get-tuple-element.32.refs_0_, ...), custom_call_target="tpu_custom_call", output_to_operand_aliasing={{0}: (10, {})} | custom-call | flops 13421772800 | bytes 4194304 | tf_op jit(solution)/shard_map/pallas_call | solution.py:388
  46.4 3.6 %collective-permute-start.14 = (bf16[256,256]{1,0:T(8,128)(2,1)S(1)}, bf16[256,256]{1,0:T(8,128)(2,1)S(1)}, u32[]{:S(2)}, u32[]{:S(2)}) collective-permute-start(bf16[256,256]{1,0:T(8,128)(2,1)S(1)} %get-tuple-element.52), channel_id=1, source_target_pairs={{4,0},{8,4},{12,8},{16,12},{20,16},{24,20},{28,24},{0,28},{5,1},{9... | collective-permute-start | bytes 393224 | tf_op jit(solution)/shard_map/ppermute | solution.py:475
  50.1 1.1 %collective-permute-start.12 = (bf16[256,256]{1,0:T(8,128)(2,1)S(1)}, bf16[256,256]{1,0:T(8,128)(2,1)S(1)}, u32[]{:S(2)}, u32[]{:S(2)}) collective-permute-start(bf16[256,256]{1,0:T(8,128)(2,1)S(1)} %shard_map.84), channel_id=1, source_target_pairs={{8,0},{12,4},{16,8},{20,12},{24,16},{28,20},{0,24},{4,28},{9,1},{1... | collective-permute-start | bytes 393224 | tf_op jit(solution)/shard_map/ppermute | solution.py:485
  51.2 1.2 %collective-permute-done.13.refs_0_ = bf16[256,256]{1,0:T(8,128)(2,1)S(1)} collective-permute-done((bf16[256,256]{1,0:T(8,128)(2,1)S(1)}, bf16[256,256]{1,0:T(8,128)(2,1)S(1)}, u32[]{:S(2)}, u32[]{:S(2)}) %collective-permute-start.13) | collective-permute-done | bytes 131104 | tf_op jit(solution)/shard_map/ppermute | solution.py:473
  52.4 1.2 %collective-permute-done.14.refs_2_ = bf16[256,256]{1,0:T(8,128)(2,1)S(1)} collective-permute-done((bf16[256,256]{1,0:T(8,128)(2,1)S(1)}, bf16[256,256]{1,0:T(8,128)(2,1)S(1)}, u32[]{:S(2)}, u32[]{:S(2)}) %collective-permute-start.14) | collective-permute-done | bytes 131104 | tf_op jit(solution)/shard_map/ppermute | solution.py:475
  53.6 1.4 %collective-permute-done.15.refs_3_.refs_5_ = bf16[256,256]{1,0:T(8,128)(2,1)S(1)} collective-permute-done((bf16[256,256]{1,0:T(8,128)(2,1)S(1)}, bf16[256,256]{1,0:T(8,128)(2,1)S(1)}, u32[]{:S(2)}, u32[]{:S(2)}) %collective-permute-start.15) | collective-permute-done | bytes 131104 | tf_op jit(solution)/shard_map/ppermute | solution.py:475
  55.1 1.1 %collective-permute-start.16 = (bf16[256,256]{1,0:T(8,128)(2,1)S(1)}, bf16[256,256]{1,0:T(8,128)(2,1)S(1)}, u32[]{:S(2)}, u32[]{:S(2)}) collective-permute-start(bf16[256,256]{1,0:T(8,128)(2,1)S(1)} %shard_map.85), channel_id=1, source_target_pairs={{8,0},{12,4},{16,8},{20,12},{24,16},{28,20},{0,24},{4,28},{9,1},{1... | collective-permute-start | bytes 393224 | tf_op jit(solution)/shard_map/ppermute | solution.py:485
  56.2 0.7 %collective-permute-done.12.refs_1_ = bf16[256,256]{1,0:T(8,128)(2,1)S(1)} collective-permute-done((bf16[256,256]{1,0:T(8,128)(2,1)S(1)}, bf16[256,256]{1,0:T(8,128)(2,1)S(1)}, u32[]{:S(2)}, u32[]{:S(2)}) %collective-permute-start.12) | collective-permute-done | bytes 131104 | tf_op jit(solution)/shard_map/ppermute | solution.py:485
  56.8 3.3 %collective-permute-done.16.refs_4_ = bf16[256,256]{1,0:T(8,128)(2,1)S(1)} collective-permute-done((bf16[256,256]{1,0:T(8,128)(2,1)S(1)}, bf16[256,256]{1,0:T(8,128)(2,1)S(1)}, u32[]{:S(2)}, u32[]{:S(2)}) %collective-permute-start.16) | collective-permute-done | bytes 131104 | tf_op jit(solution)/shard_map/ppermute | solution.py:485
  60.1 0.8 %shard_map.86 = (bf16[256,256]{1,0:T(8,128)(2,1)}, bf16[256,256]{1,0:T(8,128)(2,1)}) custom-call(f32[256,256]{1,0:T(8,128)S(1)} %get-tuple-element.41.refs_0_, bf16[256,256]{1,0:T(8,128)(2,1)S(1)} %collective-permute-done.12.refs_1_, bf16[256,256]{1,0:T(8,128)(2,1)S(1)} %collective-permute-done.11.refs_3_.refs_2_, f32[256,256]{1,0:T(8,128)S(1)} %get-tuple-element.47.refs_3_, ...), custom_call_target="tpu_custom_call" | custom-call | tf_op jit(solution)/shard_map/pallas_call | solution.py:190
  (21 shorter events, 2.8 us)
Async XLA Ops:
  2.0 11.8 %collective-permute-start = (bf16[272,512]{1,0:T(8,128)(2,1)S(1)}, bf16[272,512]{1,0:T(8,128)(2,1)S(1)}, u32[]{:S(2)}, u32[]{:S(2)}) collective-permute-start(bf16[272,512]{1,0:T(8,128)(2,1)S(1)} %get-tuple-element.30.even_ref.refs_5_), channel_id=1, source_target_pairs={{0,8},{4,12},{8,16},{12,20},{16,24},{20,28},{24,0},{28,4},{1,9},{5... | collective-permute-start | bytes 835592 | tf_op jit(solution)/shard_map/ppermute | solution.py:438
  5.0 13.0 %collective-permute-start.3 = (bf16[128,1024]{1,0:T(8,128)(2,1)S(1)}, bf16[128,1024]{1,0:T(8,128)(2,1)S(1)}, u32[]{:S(2)}, u32[]{:S(2)}) collective-permute-start(bf16[128,1024]{1,0:T(8,128)(2,1)S(1)} %get-tuple-element.36), channel_id=1, source_target_pairs={{0,2},{1,3},{2,0},{3,1},{4,6},{5,7},{6,4},{7,5},{8,10},{9,11},{10,... | collective-permute-start | bytes 786440 | tf_op jit(solution)/shard_map/ppermute | solution.py:440
  6.5 11.9 %collective-permute-start.4 = (bf16[128,1024]{1,0:T(8,128)(2,1)S(1)}, bf16[128,1024]{1,0:T(8,128)(2,1)S(1)}, u32[]{:S(2)}, u32[]{:S(2)}) collective-permute-start(bf16[128,1024]{1,0:T(8,128)(2,1)S(1)} %get-tuple-element.37), channel_id=1, source_target_pairs={{0,2},{1,3},{2,0},{3,1},{4,6},{5,7},{6,4},{7,5},{8,10},{9,11},{10,... | collective-permute-start | bytes 786440 | tf_op jit(solution)/shard_map/ppermute | solution.py:440
  13.7 6.7 %collective-permute-start.1 = (bf16[272,256]{1,0:T(8,128)(2,1)S(1)}, bf16[272,256]{1,0:T(8,128)(2,1)S(1)}, u32[]{:S(2)}, u32[]{:S(2)}) collective-permute-start(bf16[272,256]{1,0:T(8,128)(2,1)S(1)} %shard_map.78), channel_id=1, source_target_pairs={{8,12},{12,16},{16,20},{20,24},{24,28},{0,4},{4,0},{28,8},{9,13},{... | collective-permute-start | bytes 417800 | tf_op jit(solution)/shard_map/ppermute | solution.py:447
  15.3 10.2 %collective-permute-start.6 = (bf16[272,512]{1,0:T(8,128)(2,1)S(1)}, bf16[272,512]{1,0:T(8,128)(2,1)S(1)}, u32[]{:S(2)}, u32[]{:S(2)}) collective-permute-start(bf16[272,512]{1,0:T(8,128)(2,1)S(1)} %shard_map.80), channel_id=1, source_target_pairs={{0,4},{4,0},{8,12},{12,8},{16,20},{20,16},{24,28},{28,24},{1,5},{5... | collective-permute-start | bytes 835592 | tf_op jit(solution)/shard_map/ppermute | solution.py:452
  15.9 9.7 %collective-permute-start.8 = (bf16[272,512]{1,0:T(8,128)(2,1)S(1)}, bf16[272,512]{1,0:T(8,128)(2,1)S(1)}, u32[]{:S(2)}, u32[]{:S(2)}) collective-permute-start(bf16[272,512]{1,0:T(8,128)(2,1)S(1)} %collective-permute-done.even_ref.odd_ref.refs_8_), channel_id=1, source_target_pairs={{0,8},{4,12},{8,16},{12,20},{16,24},{20,28},{24,0},{28,4},{1,9},{5... | collective-permute-start | bytes 835592 | tf_op jit(solution)/shard_map/ppermute | solution.py:448
  20.4 5.2 %collective-permute-start.5 = (bf16[64,2048]{1,0:T(8,128)(2,1)S(1)}, bf16[64,2048]{1,0:T(8,128)(2,1)S(1)}, u32[]{:S(2)}, u32[]{:S(2)}) collective-permute-start(bf16[64,2048]{1,0:T(8,128)(2,1)S(1)} %shard_map.79), channel_id=1, source_target_pairs={{0,1},{1,0},{2,3},{3,2},{4,5},{5,4},{6,7},{7,6},{8,9},{9,8},{10,11... | collective-permute-start | bytes 786440 | tf_op jit(solution)/shard_map/ppermute | solution.py:457
  20.4 5.2 %collective-permute-start.2 = (bf16[64,2048]{1,0:T(8,128)(2,1)S(1)}, bf16[64,2048]{1,0:T(8,128)(2,1)S(1)}, u32[]{:S(2)}, u32[]{:S(2)}) collective-permute-start(bf16[64,2048]{1,0:T(8,128)(2,1)S(1)} %get-tuple-element.35), channel_id=1, source_target_pairs={{0,1},{1,0},{2,3},{3,2},{4,5},{5,4},{6,7},{7,6},{8,9},{9,8},{10,11... | collective-permute-start | bytes 786440 | tf_op jit(solution)/shard_map/ppermute | solution.py:453
  20.9 16.5 %collective-permute-start.7 = (bf16[272,256]{1,0:T(8,128)(2,1)S(1)}, bf16[272,256]{1,0:T(8,128)(2,1)S(1)}, u32[]{:S(2)}, u32[]{:S(2)}) collective-permute-start(bf16[272,256]{1,0:T(8,128)(2,1)S(1)} %shard_map.81), channel_id=1, source_target_pairs={{8,12},{12,16},{16,20},{20,24},{24,28},{0,4},{4,0},{28,8},{9,13},{... | collective-permute-start | bytes 417800 | tf_op jit(solution)/shard_map/ppermute | solution.py:451
  34.0 11.9 %collective-permute-start.9 = (bf16[256,256]{1,0:T(8,128)(2,1)S(1)}, bf16[256,256]{1,0:T(8,128)(2,1)S(1)}, u32[]{:S(2)}, u32[]{:S(2)}) collective-permute-start(bf16[256,256]{1,0:T(8,128)(2,1)S(1)} %get-tuple-element.42), channel_id=1, source_target_pairs={{8,0},{12,4},{16,8},{20,12},{24,16},{28,20},{0,24},{4,28},{9,1},{1... | collective-permute-start | bytes 393224 | tf_op jit(solution)/shard_map/ppermute | solution.py:473
  35.4 10.4 %collective-permute-start.10 = (bf16[256,256]{1,0:T(8,128)(2,1)S(1)}, bf16[256,256]{1,0:T(8,128)(2,1)S(1)}, u32[]{:S(2)}, u32[]{:S(2)}) collective-permute-start(bf16[256,256]{1,0:T(8,128)(2,1)S(1)} %get-tuple-element.45), channel_id=1, source_target_pairs={{4,0},{8,4},{12,8},{16,12},{20,16},{24,20},{28,24},{0,28},{5,1},{9... | collective-permute-start | bytes 393224 | tf_op jit(solution)/shard_map/ppermute | solution.py:475
  36.5 9.4 %collective-permute-start.11 = (bf16[256,256]{1,0:T(8,128)(2,1)S(1)}, bf16[256,256]{1,0:T(8,128)(2,1)S(1)}, u32[]{:S(2)}, u32[]{:S(2)}) collective-permute-start(bf16[256,256]{1,0:T(8,128)(2,1)S(1)} %get-tuple-element.46), channel_id=1, source_target_pairs={{0,4},{4,0},{8,12},{12,8},{16,20},{20,16},{24,28},{28,24},{1,5},{5... | collective-permute-start | bytes 393224 | tf_op jit(solution)/shard_map/ppermute | solution.py:475
  45.9 6.5 %collective-permute-start.13 = (bf16[256,256]{1,0:T(8,128)(2,1)S(1)}, bf16[256,256]{1,0:T(8,128)(2,1)S(1)}, u32[]{:S(2)}, u32[]{:S(2)}) collective-permute-start(bf16[256,256]{1,0:T(8,128)(2,1)S(1)} %get-tuple-element.49), channel_id=1, source_target_pairs={{8,0},{12,4},{16,8},{20,12},{24,16},{28,20},{0,24},{4,28},{9,1},{1... | collective-permute-start | bytes 393224 | tf_op jit(solution)/shard_map/ppermute | solution.py:473
  46.4 7.2 %collective-permute-start.14 = (bf16[256,256]{1,0:T(8,128)(2,1)S(1)}, bf16[256,256]{1,0:T(8,128)(2,1)S(1)}, u32[]{:S(2)}, u32[]{:S(2)}) collective-permute-start(bf16[256,256]{1,0:T(8,128)(2,1)S(1)} %get-tuple-element.52), channel_id=1, source_target_pairs={{4,0},{8,4},{12,8},{16,12},{20,16},{24,20},{28,24},{0,28},{5,1},{9... | collective-permute-start | bytes 393224 | tf_op jit(solution)/shard_map/ppermute | solution.py:475
  50.0 5.0 %collective-permute-start.15 = (bf16[256,256]{1,0:T(8,128)(2,1)S(1)}, bf16[256,256]{1,0:T(8,128)(2,1)S(1)}, u32[]{:S(2)}, u32[]{:S(2)}) collective-permute-start(bf16[256,256]{1,0:T(8,128)(2,1)S(1)} %get-tuple-element.54), channel_id=1, source_target_pairs={{0,4},{4,0},{8,12},{12,8},{16,20},{20,16},{24,28},{28,24},{1,5},{5... | collective-permute-start | bytes 393224 | tf_op jit(solution)/shard_map/ppermute | solution.py:475
  50.1 6.7 %collective-permute-start.12 = (bf16[256,256]{1,0:T(8,128)(2,1)S(1)}, bf16[256,256]{1,0:T(8,128)(2,1)S(1)}, u32[]{:S(2)}, u32[]{:S(2)}) collective-permute-start(bf16[256,256]{1,0:T(8,128)(2,1)S(1)} %shard_map.84), channel_id=1, source_target_pairs={{8,0},{12,4},{16,8},{20,12},{24,16},{28,20},{0,24},{4,28},{9,1},{1... | collective-permute-start | bytes 393224 | tf_op jit(solution)/shard_map/ppermute | solution.py:485
  55.1 5.0 %collective-permute-start.16 = (bf16[256,256]{1,0:T(8,128)(2,1)S(1)}, bf16[256,256]{1,0:T(8,128)(2,1)S(1)}, u32[]{:S(2)}, u32[]{:S(2)}) collective-permute-start(bf16[256,256]{1,0:T(8,128)(2,1)S(1)} %shard_map.85), channel_id=1, source_target_pairs={{8,0},{12,4},{16,8},{20,12},{24,16},{28,20},{0,24},{4,28},{9,1},{1... | collective-permute-start | bytes 393224 | tf_op jit(solution)/shard_map/ppermute | solution.py:485
